TPU v7x, 256 devices: a whole 4x4x8 slice. The times are simulated.
256 devices in a mesh: batch: 32 (over y, x, core), leaf: 8 (over z).
Axes of the slice: x: 4, y: 4, z: 8, core: 2. Of those that a mesh axis runs over, the one named last changes fastest.
Arguments:
- queries: bfloat16 [32, 1024, 4096], P('batch', 'leaf'), may hold values from -6 to 6
- keys: bfloat16 [32, 1024, 512], P('batch', 'leaf'), may hold values from -6 to 6
- values: bfloat16 [32, 1024, 512], P('batch', 'leaf'), may hold values from -6 to 6
- out_grad: bfloat16 [32, 1024, 4096], P('batch', 'leaf'), may hold values from -6 to 6
- inputs: bfloat16 [32, 1024, 5120], P('batch', 'leaf'), may hold values from -6 to 6
- parents: int32 [32, 8], P('batch'), may hold values from 0 to 6, as said below
- lengths: int32 [32, 8], P('batch'), may hold values from 16 to 128, as said below
Outputs:
- query_grad: bfloat16 [32, 1024, 4096], P('batch', 'leaf')
- key_grad: bfloat16 [32, 1024, 512], P('batch', 'leaf')
- value_grad: bfloat16 [32, 1024, 512], P('batch', 'leaf')
- weight_grad: float32 [5120, 512], P(('batch', 'leaf'))
Inputs may be any that keep to these rules, and one draw needn't show every extreme that they name: parents[t, 0] = 0 and parents[t, s] < s for s >= 1. `lengths`: segment 0 of every tree holds 128 live tokens; the others at least 16.
All inputs are finite; a program needn't handle non-finite values.
Results may differ from a plain program's by a relative error of at most 0.015.
Values may be sent and summed in bfloat16 or wider, within the bound.
No kernel may reach another device: no remote copies, remote signals or barrier semaphores. Data moves between devices by JAX's collectives and lax.ppermute only.
A program may use at most 128 MiB of HBM per device.

v0:
```python
import math

import jax
import jax.numpy as jnp
from jax import lax
from jax.sharding import PartitionSpec as P

HD = 128


def spread_rows(table, segment):
    node_count = table.shape[0]
    return jnp.broadcast_to(table[:, None], (node_count, segment)).reshape(node_count * segment)


def on_device(queries, keys, values, out_grad, inputs, parents, lengths):
    segment = queries.shape[1]
    kv_width = keys.shape[2]
    heads_kv = kv_width // HD
    group_size = queries.shape[2] // kv_width
    node_count = lax.axis_size("leaf")
    total_rows = node_count * segment
    own_node = lax.axis_index("leaf")
    key_all, value_all = (
        lax.all_gather(keys[0], "leaf", axis=0, tiled=True),
        lax.all_gather(values[0], "leaf", axis=0, tiled=True),
    )
    parent_row = parents[0]
    length_row = lengths[0]
    node_ids = jnp.arange(node_count, dtype=jnp.int32)

    def climb(step, state):
        cursor, member = state
        cursor = jnp.sum(jnp.where(node_ids == cursor, parent_row, 0))
        return (cursor, member | (node_ids == cursor))

    start_state = (own_node, node_ids == own_node)
    cursor, member = lax.fori_loop(0, node_count, climb, start_state)
    key_member = spread_rows(member, segment)
    key_length = spread_rows(length_row, segment)
    key_own = spread_rows(node_ids == own_node, segment)
    key_place = jnp.arange(total_rows, dtype=jnp.int32) % segment
    query_place = jnp.arange(segment, dtype=jnp.int32)
    above = (key_member & ~key_own & (key_place < key_length))[None, :]
    allowed = above | key_own[None, :] & (key_place[None, :] <= query_place[:, None])
    own_length = jnp.sum(jnp.where(node_ids == own_node, length_row, 0))
    live = query_place < own_length
    masked_grad = jnp.where(live[:, None], out_grad[0], jnp.zeros_like(out_grad[0]))
    query_four = queries[0].reshape(segment, heads_kv, group_size, HD)
    grad_four = masked_grad.reshape(segment, heads_kv, group_size, HD)
    key_heads = key_all.reshape(total_rows, heads_kv, HD)
    value_heads = value_all.reshape(total_rows, heads_kv, HD)
    score_scale = 1.0 / math.sqrt(HD)
    prob_list = []
    dscore_list = []
    query_list = []
    for head in range(heads_kv):
        key_one = key_heads[:, head]
        scores = (
            jnp.einsum(
                "igd,jd->gij", query_four[:, head], key_one, preferred_element_type=jnp.float32
            )
            * score_scale
        )
        scores = jnp.where(allowed[None], scores, -jnp.inf)
        row_max = jnp.max(scores, axis=-1, keepdims=True)
        raised = jnp.exp(scores - row_max)
        probs = raised / jnp.sum(raised, axis=-1, keepdims=True)
        dprobs = jnp.einsum(
            "igd,jd->gij",
            grad_four[:, head],
            value_heads[:, head],
            preferred_element_type=jnp.float32,
        )
        delta = jnp.sum(probs * dprobs, axis=-1, keepdims=True)
        dscores_low = (probs * (dprobs - delta)).astype(jnp.bfloat16)
        prob_list.append(probs.astype(jnp.bfloat16))
        dscore_list.append(dscores_low)
        query_list.append(
            jnp.einsum("gij,jd->igd", dscores_low, key_one, preferred_element_type=jnp.float32)
            * score_scale
        )
    probs_all = jnp.stack(prob_list, axis=0)
    dscores_all = jnp.stack(dscore_list, axis=0)
    query_grad = (
        jnp.stack(query_list, axis=1)
        .reshape(segment, heads_kv * group_size * HD)
        .astype(jnp.bfloat16)
    )
    key_term = (
        jnp.einsum("kgij,ikgd->jkd", dscores_all, query_four, preferred_element_type=jnp.float32)
        * score_scale
    )
    value_term = jnp.einsum(
        "kgij,ikgd->jkd", probs_all, grad_four, preferred_element_type=jnp.float32
    )
    owned_sums = lax.psum_scatter(
        jnp.concatenate(
            (
                key_term.reshape(lax.axis_size("leaf") * segment, kv_width),
                value_term.reshape(lax.axis_size("leaf") * segment, kv_width),
            ),
            axis=1,
        ),
        "leaf",
        scatter_dimension=0,
        tiled=True,
    )
    key_grad = owned_sums[:, :kv_width].astype(jnp.bfloat16)
    value_grad = owned_sums[:, kv_width:].astype(jnp.bfloat16)
    features = inputs[0]
    weight_grad = lax.psum_scatter(
        lax.dot_general(
            features, value_grad, (((0,), (0,)), ((), ())), preferred_element_type=jnp.float32
        ),
        ("batch", "leaf"),
        scatter_dimension=0,
        tiled=True,
    )
    return (query_grad[None], key_grad[None], value_grad[None], weight_grad)


def solution(mesh):
    return jax.shard_map(
        on_device,
        mesh=mesh,
        in_specs=(
            P("batch", "leaf", None),
            P("batch", "leaf", None),
            P("batch", "leaf", None),
            P("batch", "leaf", None),
            P("batch", "leaf", None),
            P("batch", None),
            P("batch", None),
        ),
        out_specs=(
            P("batch", "leaf", None),
            P("batch", "leaf", None),
            P("batch", "leaf", None),
            P(("batch", "leaf"), None),
        ),
        check_vma=False,
    )
```

profile of v0, /device:TPU:8, one launch (start us, length us, event | category | flops | bytes accessed | tf_op | source)
XLA Modules:
  0.0 492.8 jit_solution(13515654388312424642)
XLA Ops:
  7.2 1.8 copy.67
  9.0 0.0 all-gather.7.cloned.1.call-start
  9.1 1.7 copy.73
  10.8 0.1 broadcast_bitcast_fusion
  10.9 20.9 %while.14 = (s32[]{:T(128)}, s32[]{:T(128)}, pred[8]{0:T(512)(128)(4,1)S(1)}, s32[8]{0:T(128)}, s32[]{:T(128)}) while((s32[]{:T(128)}, s32[]{:T(128)}, pred[8]{0:T(512)(128)(4,1)S(1)}, s32[8]{0:T(128)}, s32[]{:T(128)}) %tuple.59), condition=%wide.region_2.3_spmd.clone.clone, body=%wide.region_0.2_spmd.clone.clone.sunk | while | flops 41 | bytes 129 | solution.py:38
  10.9 1.3 fusion.106
  12.2 0.7 compare_or_fusion.2
  13.5 1.3 fusion.106
  14.8 0.7 compare_or_fusion.2
  16.1 1.3 fusion.106
  17.4 0.7 compare_or_fusion.2
  18.8 1.3 fusion.106
  20.1 0.7 compare_or_fusion.2
  21.4 1.3 fusion.106
  22.7 0.7 compare_or_fusion.2
  24.0 1.3 fusion.106
  25.3 0.7 compare_or_fusion.2
  26.6 1.3 fusion.106
  27.9 0.7 compare_or_fusion.2
  29.2 1.3 fusion.106
  30.5 0.7 compare_or_fusion.2
  31.8 2.3 copy.69
  34.1 1.3 select_reduce_fusion
  35.4 0.6 iota_compare_fusion.1
  36.0 1.6 copy.71
  37.7 0.7 copy.72
  38.4 0.1 fusion.84
  38.4 0.9 fusion.63
  39.3 0.1 broadcast_select_fusion
  39.5 13.4 %all-gather.5.cloned.1.call-done = bf16[1,1024,512]{1,2,0:T(8,128)(2,1)} async-done(((bf16[1,128,512]{1,2,0:T(8,128)(2,1)}), bf16[1,1024,512]{1,2,0:T(8,128)(2,1)}) %all-gather.5.cloned.1.call-update) | async-done | bytes 1048592 | tf_op jit(solution)/shard_map/all_gather | solution.py:25
  52.9 4.4 fusion.97
  57.3 4.3 fusion.98
  61.5 4.2 fusion.96
  65.8 4.3 fusion.95
  70.1 23.8 %all-gather.7.cloned.1.call-done = bf16[1,1024,512]{1,2,0:T(8,128)(2,1)} async-done(((bf16[1,128,512]{1,2,0:T(8,128)(2,1)}), bf16[1,1024,512]{1,2,0:T(8,128)(2,1)}) %all-gather.7.cloned.1.call-update) | async-done | bytes 1048592 | tf_op jit(solution)/shard_map/all_gather | solution.py:26
  93.9 5.1 %fusion.29 = (f32[8,128]{1,0:T(8,128)S(1)}, f32[128,8,1024]{0,2,1:T(8,128)}) fusion(f32[8,128,1024]{1,2,0:T(8,128)} %get-tuple-element.98, f32[8,128]{1,0:T(8,128)S(1)} %get-tuple-element.97, bf16[1024,4,128]{0,2,1:T(8,128)(2,1)} %bitcast.342, bf16[128,4,8,128]{3,0,2,1:T(8,128)(2,1)S(1)} %broadcast_select_fusion), kind=kOutput, calls=%fused_computation.40 | convolution fusion | flops 271580160 | bytes 8921088 | tf_op jit(solution)/shard_map/igd,jd->gij/dot_general | solution.py:69
  99.1 2.7 fusion.32
  101.8 0.6 copy-done.8
  102.5 0.8 fusion.26
  103.2 1.4 copy-done.9
  104.6 2.7 fusion.23
  107.4 0.6 copy-done.10
  108.0 5.6 %convert_bitcast_fusion.2 = (bf16[1,8,128,1024]{2,3,1,0:T(8,128)(2,1)}, bf16[8,128,1024]{1,2,0:T(8,128)(2,1)S(1)}, bf16[8,128,1024]{1,2,0:T(8,128)(2,1)S(1)}, bf16[1,8,128,1024]{2,3,1,0:T(8,128)(2,1)}) fusion(f32[8,128,1024]{1,2,0:T(8,128)S(1)} %copy-done.10, f32[8,128]{1,0:T(8,128)S(1)} %get-tuple-element.97, f32[8,128]{1,0:T(8,128)S(1)} %get-tuple-element.99, ...), kind=kLoop, calls=%fused_computation.61 | loop fusion | flops 10485760 | bytes 25182208 | tf_op jit(solution)/shard_map/stack | solution.py:83
  113.7 6.2 %convert_bitcast_fusion = (bf16[1,8,128,1024]{2,3,1,0:T(8,128)(2,1)}, bf16[8,128,1024]{1,2,0:T(8,128)(2,1)S(1)}, bf16[8,128,1024]{1,2,0:T(8,128)(2,1)S(1)}, bf16[1,8,128,1024]{2,3,1,0:T(8,128)(2,1)}) fusion(f32[8,128,1024]{1,2,0:T(8,128)S(1)} %copy-done.9, f32[8,128]{1,0:T(8,128)S(1)} %get-tuple-element.89, f32[8,128]{1,0:T(8,128)S(1)} %get-tuple-element.91, ...), kind=kLoop, calls=%fused_computation.59 | loop fusion | flops 10485760 | bytes 25182208 | tf_op jit(solution)/shard_map/stack | solution.py:83
  119.8 4.6 bitcast_multiply_fusion.4
  124.4 1.9 copy.99
  126.3 6.5 %fusion.15 = f32[4,128,1024,1]{2,1,3,0:T(8,128)} fusion(bf16[128,4,8,128]{3,0,2,1:T(8,128)(2,1)} %copy-done.16, bf16[1,8,128,1024]{2,3,1,0:T(8,128)(2,1)} %get-tuple-element.85, bf16[1,8,128,1024]{2,3,1,0:T(8,128)(2,1)} %get-tuple-element.106, bf16[1,8,128,1024]{2,3,1,0:T(8,128)(2,1)} %get-tuple-element.81, bf16[1,8,128,1024]{2,3,1,0:T(8,128)(2,1)} %get-tuple-element.108), kind=kOutput, calls=%fused_computation.16 | convolution fusion | flops 1086324736 | bytes 11534336 | tf_op jit(solution)/shard_map/kgij,ikgd->jkd/dot_general | solution.py:94
  132.9 2.9 copy.100
  135.8 4.0 pad_maximum_fusion
  139.9 0.0 all-reduce.3.cloned.1.call-start
  139.9 54.6 %reduce-scatter.3.cloned.1.call-done = f32[128,1024]{1,0:T(8,128)} async-done(((f32[1024,1024]{1,0:T(8,128)}), f32[128,1024]{1,0:T(8,128)}) %reduce-scatter.3.cloned.1.call-update) | async-done | bytes 524304 | tf_op jit(solution)/shard_map/reduce_scatter | solution.py:97
  194.5 1.1 convert.28
  195.6 0.7 copy-done.12
  196.3 5.4 %convolution_bitcast_fusion = f32[5120,512]{0,1:T(8,128)} fusion(bf16[1,128,5120]{2,1,0:T(8,128)(2,1)S(1)} %copy-done, bf16[128,1024]{1,0:T(8,128)(2,1)S(1)} %convert.28), kind=kOutput, calls=%fused_computation.24 | convolution fusion | flops 671088640 | bytes 11927552 | tf_op jit(solution)/shard_map/dot_general | solution.py:113
  201.7 2.3 fusion.61
  204.0 1.9 fusion.60
  206.0 0.4 fusion.59
  206.5 0.4 fusion.58
  206.9 0.1 pad_maximum_fusion.1
  207.1 1.3 copy.101
  208.4 0.7 slice_bitcast_fusion.69
  209.1 275.3 %all-reduce.3.cloned.1.call-done = f32[5120,512]{0,1:T(8,128)} async-done(((f32[5120,512]{0,1:T(8,128)}), f32[5120,512]{0,1:T(8,128)}) %all-reduce.3.cloned.1.call-update) | async-done | bytes 10485776
  484.4 1.2 constant_dynamic-slice_fusion
  485.5 0.7 copy.102
  (45 shorter events, 0.2 us)
Async XLA Ops:
  7.2 189.1 %copy-start = (bf16[1,128,5120]{2,1,0:T(8,128)(2,1)S(1)}, bf16[1,128,5120]{2,1,0:T(8,128)(2,1)}, u32[]{:S(2)}) copy-start(bf16[1,128,5120]{2,1,0:T(8,128)(2,1)} %param.13) | copy-start | bytes 3932164
  7.2 31.2 %copy-start.18 = (s32[1,8]{1,0:T(1,128)S(1)}, s32[1,8]{1,0:T(1,128)}, u32[]{:S(2)}) copy-start(s32[1,8]{1,0:T(1,128)} %param.15) | copy-start | bytes 100
  7.2 45.7 %all-gather.5.cloned.1.call-start = ((), (), s32[]{:S(2)}) async-start(), calls=%async_computation.2 | async-start | bytes 1179648 | tf_op jit(solution)/shard_map/all_gather | solution.py:25
  9.0 84.9 %all-gather.7.cloned.1.call-start = ((), (), s32[]{:S(2)}) async-start(), calls=%async_computation.3 | async-start | bytes 1179648 | tf_op jit(solution)/shard_map/all_gather | solution.py:26
  10.8 183.8 %reduce-scatter.3.cloned.1.call-start = ((), (), s32[]{:S(2)}) async-start(), calls=%async_computation.1 | async-start | bytes 4718592 | tf_op jit(solution)/shard_map/reduce_scatter | solution.py:97
  39.4 63.8 %copy-start.16 = (bf16[128,4,8,128]{3,0,2,1:T(8,128)(2,1)}, bf16[128,4,8,128]{3,0,2,1:T(8,128)(2,1)S(1)}, u32[]{:S(2)}) copy-start(bf16[128,4,8,128]{3,0,2,1:T(8,128)(2,1)S(1)} %broadcast_select_fusion) | copy-start | bytes 3145732
  52.8 4.4 copy-start.14
  93.9 5.2 %copy-start.11 = (f32[8,128,1024]{1,2,0:T(8,128)S(1)}, f32[8,128,1024]{1,2,0:T(8,128)}, u32[]{:S(2)}) copy-start(f32[8,128,1024]{1,2,0:T(8,128)} %get-tuple-element.102) | copy-start | bytes 12582916
  93.9 5.2 %copy-start.19 = (bf16[1,1024,512]{1,2,0:T(8,128)(2,1)S(1)}, bf16[1,1024,512]{1,2,0:T(8,128)(2,1)}, u32[]{:S(2)}) copy-start(bf16[1,1024,512]{1,2,0:T(8,128)(2,1)} %all-gather.7.cloned.1.call-done) | copy-start | bytes 3145732
  99.1 3.3 copy-start.8
  102.5 2.2 copy-start.9
  104.6 3.4 copy-start.10
  113.6 6.2 %copy-start.1 = (bf16[8,128,1024]{1,2,0:T(8,128)(2,1)}, bf16[8,128,1024]{1,2,0:T(8,128)(2,1)S(1)}, u32[]{:S(2)}) copy-start(bf16[8,128,1024]{1,2,0:T(8,128)(2,1)S(1)} %get-tuple-element.82) | copy-start | bytes 6291460
  113.6 6.2 %copy-start.3 = (bf16[8,128,1024]{1,2,0:T(8,128)(2,1)}, bf16[8,128,1024]{1,2,0:T(8,128)(2,1)S(1)}, u32[]{:S(2)}) copy-start(bf16[8,128,1024]{1,2,0:T(8,128)(2,1)S(1)} %get-tuple-element.107) | copy-start | bytes 6291460
  113.6 6.2 %copy-start.17 = (bf16[1,128,4096]{1,2,0:T(8,128)(2,1)S(1)}, bf16[1,128,4096]{1,2,0:T(8,128)(2,1)}, u32[]{:S(2)}) copy-start(bf16[1,128,4096]{1,2,0:T(8,128)(2,1)} %copy.69) | copy-start | bytes 3145732
  119.8 4.6 copy-start.4
  119.8 4.6 copy-start.6
  139.9 344.5 %all-reduce.3.cloned.1.call-start = ((), (), s32[]{:S(2)}) async-start(), calls=%async_computation.4 | async-start | bytes 20971520
  195.6 0.7 copy-start.12
  201.7 2.3 copy-start.2
  201.7 4.2 copy-start.7
  201.7 4.2 copy-start.15
  201.7 4.7 copy-start.5
  206.0 2.4 copy-start.13
Sparse Core Ops, SparseCore 0:
  10.3 42.4 all-gather.4
  55.1 38.7 all-gather.6
  140.0 54.4 reduce-scatter.2
  201.8 282.4 all-reduce.2
where the time goes:
time: 494 us; the launch traced here: 493 us
  waiting for transfers between devices  367 us (74%)
  matrix products  50.3 us (10%)
  other arithmetic  35.7 us (7%)
  local copies, waits for them, and re-layouts  20.2 us (4%)
  between operations  14.1 us (3%)
  loops' own time  5.3 us (1%)
    unnamed x5, waiting for transfers between devices  275 us
    reduce_scatter x1, waiting for transfers between devices, on_device(): lax.psum_scatter(jnp.concatenate((key_term.reshape(lax.axis_size('leaf')...  54.6 us
    all_gather x1, waiting for transfers between devices, on_device(): lax.all_gather(values[0], 'leaf', axis=0, tiled=True)  23.8 us
    sub x4, matrix products, on_device(): raised = jnp.exp(scores - row_max)  17.2 us
    unnamed x48, local copies, waits for them, and re-layouts  13.9 us
    all_gather x1, waiting for transfers between devices, on_device(): lax.all_gather(keys[0], 'leaf', axis=0, tiled=True)  13.4 us
    another operation x2, other arithmetic, on_device(): probs_all = jnp.stack(prob_list, axis=0)  11.8 us
    dot_general x4, matrix products, on_device(): jnp.einsum('igd,jd->gij', grad_four[:, head], value_heads[:, head], prefe...  11.4 us
  transfers between devices with their start and end apart: 4, of which 4 were waited for; matrix products, arithmetic and copies ran while one was open for 10% of the time, Pallas kernels for 0%

commit v1 on v0

v1 whole, which is shorter than its diff:
```python
import math

import jax
import jax.numpy as jnp
from jax import lax
from jax.experimental import pallas as pl
from jax.experimental.pallas import tpu as pltpu
from jax.sharding import Mesh
from jax.sharding import PartitionSpec as P

HD = 128
NEG = -1e30
F32 = jnp.float32
BF16 = jnp.bfloat16
NT = (((1,), (1,)), ((), ()))
TN = (((0,), (0,)), ((), ()))


def attention_kernel(
    own_ref, par_ref, len_ref, q_ref, g_ref, k_ref, v_ref, dq_ref, dk_ref, dv_ref,
    qs, gs, s_scr, dp_scr, p_low, ds_low, m_scr, l_scr, t_scr, dqt, slot_ref, lim_ref,
):
    seg = q_ref.shape[0]
    group = q_ref.shape[1] // HD
    nodes = k_ref.shape[0] // seg
    width = group * seg
    chunk = 2 * seg
    chunks = width // chunk
    scale = 1.0 / math.sqrt(HD)
    own = own_ref[0]

    cursor = own
    slot_ref[0] = own
    lim_ref[0] = seg
    count = jnp.int32(1)
    for step in range(1, nodes):
        more = cursor > 0
        up = jnp.where(more, par_ref[cursor], 0)
        slot_ref[step] = up
        lim_ref[step] = jnp.where(more, len_ref[up], 0)
        count = count + more.astype(jnp.int32)
        cursor = up
    pairs = (count + 1) // 2

    live = lax.broadcasted_iota(jnp.int32, (seg, HD), 0) < len_ref[own]
    for head in range(group):
        qs[head * seg : (head + 1) * seg, :] = q_ref[:, head * HD : (head + 1) * HD]
        gs[head * seg : (head + 1) * seg, :] = jnp.where(
            live, g_ref[:, head * HD : (head + 1) * HD], jnp.zeros((), BF16)
        )

    dk_ref[...] = jnp.zeros_like(dk_ref)
    dv_ref[...] = jnp.zeros_like(dv_ref)
    m_scr[...] = jnp.full_like(m_scr, NEG)
    l_scr[...] = jnp.zeros_like(l_scr)
    t_scr[...] = jnp.zeros_like(t_scr)
    dqt[...] = jnp.zeros_like(dqt)

    def rows_of(ref, p):
        first = pl.multiple_of(slot_ref[2 * p] * seg, seg)
        second = pl.multiple_of(slot_ref[2 * p + 1] * seg, seg)
        return jnp.concatenate([ref[pl.ds(first, seg), :], ref[pl.ds(second, seg), :]], axis=0)

    key_place = lax.broadcasted_iota(jnp.int32, (seg, chunk), 0)
    query_place = lax.broadcasted_iota(jnp.int32, (1, chunk), 1) % seg

    def score_step(p, carry):
        k2 = rows_of(k_ref, p)
        last0 = jnp.where(p == 0, query_place, lim_ref[2 * p] - 1)
        last1 = jnp.broadcast_to(lim_ref[2 * p + 1] - 1, query_place.shape)
        for c in range(chunks):
            cols = slice(c * chunk, (c + 1) * chunk)
            s = lax.dot_general(k2, qs[cols, :], NT, preferred_element_type=F32)
            s0 = jnp.where(key_place <= last0, s[:seg], NEG)
            s1 = jnp.where(key_place <= last1, s[seg:], NEG)
            s_scr[p, :seg, cols] = s0
            s_scr[p, seg:, cols] = s1
            top = jnp.max(jnp.maximum(s0, s1), axis=0, keepdims=True)
            m_scr[:, cols] = jnp.maximum(m_scr[:, cols], top)
        return carry

    lax.fori_loop(0, pairs, score_step, 0)
    rate = scale * math.log2(math.e)

    def prob_step(p, carry):
        v2 = rows_of(v_ref, p)
        for c in range(chunks):
            cols = slice(c * chunk, (c + 1) * chunk)
            e = jnp.exp2((s_scr[p, :, cols] - m_scr[:, cols]) * rate)
            dp = lax.dot_general(v2, gs[cols, :], NT, preferred_element_type=F32)
            s_scr[p, :, cols] = e
            dp_scr[p, :, cols] = dp
            l_scr[:, cols] = l_scr[:, cols] + jnp.sum(e, axis=0, keepdims=True)
            t_scr[:, cols] = t_scr[:, cols] + jnp.sum(e * dp, axis=0, keepdims=True)
        return carry

    lax.fori_loop(0, pairs, prob_step, 0)
    l_scr[...] = 1.0 / l_scr[...]
    t_scr[...] = t_scr[...] * l_scr[...]

    def grad_step(p, carry):
        k2 = rows_of(k_ref, p)
        for c in range(chunks):
            cols = slice(c * chunk, (c + 1) * chunk)
            prob = s_scr[p, :, cols] * l_scr[:, cols]
            p_low[:, cols] = prob.astype(BF16)
            ds = (prob * (dp_scr[p, :, cols] - t_scr[:, cols])).astype(BF16)
            ds_low[:, cols] = ds
            dqt[:, cols] = dqt[:, cols] + lax.dot_general(k2, ds, TN, preferred_element_type=F32)
        dv = jnp.dot(p_low[...], gs[...], preferred_element_type=F32).astype(BF16)
        dk = (jnp.dot(ds_low[...], qs[...], preferred_element_type=F32) * scale).astype(BF16)
        first = pl.multiple_of(slot_ref[2 * p] * seg, seg)
        dv_ref[pl.ds(first, seg), :] = dv[:seg]
        dk_ref[pl.ds(first, seg), :] = dk[:seg]

        @pl.when(2 * p + 1 < count)
        def _():
            second = pl.multiple_of(slot_ref[2 * p + 1] * seg, seg)
            dv_ref[pl.ds(second, seg), :] = dv[seg:]
            dk_ref[pl.ds(second, seg), :] = dk[seg:]

        return carry

    lax.fori_loop(0, pairs, grad_step, 0)
    for head in range(group):
        block = dqt[:, head * seg : (head + 1) * seg] * scale
        dq_ref[:, head * HD : (head + 1) * HD] = block.T.astype(BF16)


def attention(own, parents, lengths, queries, out_grad, kv_all):
    seg, q_width = queries.shape
    rows, kv_width = kv_all.shape[0], kv_all.shape[1] // 2
    heads_kv = kv_width // HD
    per_head = q_width // heads_kv
    nodes = rows // seg
    width = (per_head // HD) * seg
    spec_q = pl.BlockSpec((seg, per_head), lambda k, *_: (0, k))
    spec_k = pl.BlockSpec((rows, HD), lambda k, *_: (0, k))
    spec_v = pl.BlockSpec((rows, HD), lambda k, *_: (0, k + heads_kv))
    pairs = nodes // 2
    return pl.pallas_call(
        attention_kernel,
        out_shape=(
            jax.ShapeDtypeStruct((seg, q_width), BF16),
            jax.ShapeDtypeStruct((rows, kv_width), BF16),
            jax.ShapeDtypeStruct((rows, kv_width), BF16),
        ),
        grid_spec=pltpu.PrefetchScalarGridSpec(
            num_scalar_prefetch=3,
            grid=(heads_kv,),
            in_specs=[spec_q, spec_q, spec_k, spec_v],
            out_specs=[spec_q, spec_k, spec_k],
            scratch_shapes=[
                pltpu.VMEM((width, HD), BF16),
                pltpu.VMEM((width, HD), BF16),
                pltpu.VMEM((pairs, 2 * seg, width), F32),
                pltpu.VMEM((pairs, 2 * seg, width), F32),
                pltpu.VMEM((2 * seg, width), BF16),
                pltpu.VMEM((2 * seg, width), BF16),
                pltpu.VMEM((1, width), F32),
                pltpu.VMEM((1, width), F32),
                pltpu.VMEM((1, width), F32),
                pltpu.VMEM((HD, width), F32),
                pltpu.SMEM((nodes,), jnp.int32),
                pltpu.SMEM((nodes,), jnp.int32),
            ],
        ),
        compiler_params=pltpu.CompilerParams(vmem_limit_bytes=40 * 1024 * 1024),
        cost_estimate=pl.CostEstimate(
            flops=10 * seg * rows * q_width, bytes_accessed=8 * seg * q_width, transcendentals=0
        ),
    )(own, parents, lengths, queries, out_grad, kv_all, kv_all)


def weight_kernel(x_ref, v_ref, out_ref):
    trees = x_ref.shape[0]
    parts = out_ref.shape[0]
    rows = out_ref.shape[1]
    for part in range(parts):
        total = None
        for tree in range(0, trees, 2):
            x2 = jnp.concatenate(
                [
                    x_ref[tree, part * rows : (part + 1) * rows, :],
                    x_ref[tree + 1, part * rows : (part + 1) * rows, :],
                ],
                axis=1,
            )
            v2 = jnp.concatenate([v_ref[tree], v_ref[tree + 1]], axis=0)
            term = jnp.dot(x2, v2, preferred_element_type=F32)
            total = term if total is None else total + term
        out_ref[part] = total.astype(BF16)


def on_device(queries, keys, values, out_grad, inputs, parents, lengths):
    ny, nx, nc = lax.axis_size("y"), lax.axis_size("x"), lax.axis_size("core")
    nz = lax.axis_size("leaf")
    seg, features = inputs.shape[1:]
    kv_width = keys.shape[2]
    own = lax.axis_index("leaf").astype(jnp.int32).reshape(1)

    kv_all = lax.all_gather(
        jnp.concatenate([keys[0], values[0]], axis=1), "leaf", axis=0, tiled=True
    )

    group = nx * nc
    owned = features // (ny * group)
    turned = inputs[0].T.reshape(ny, group, owned, seg).transpose(1, 0, 2, 3)
    turned = turned.reshape(group, ny * owned, seg)
    turned = lax.all_to_all(turned, ("x", "core"), 0, 0, tiled=True)
    kv_all, turned = lax.optimization_barrier((kv_all, turned))

    query_grad, key_part, value_part = attention(
        own, parents[0], lengths[0], queries[0], out_grad[0], kv_all
    )
    value_grad = lax.psum_scatter(value_part, "leaf", scatter_dimension=0, tiled=True)
    key_part, value_grad = lax.optimization_barrier((key_part, value_grad))
    key_grad = lax.psum_scatter(key_part, "leaf", scatter_dimension=0, tiled=True)

    line = lax.all_gather(value_grad, "x", axis=0)
    both = lax.all_gather(line, "core", axis=1).reshape(group, seg, kv_width)
    term = pl.pallas_call(
        weight_kernel,
        out_shape=jax.ShapeDtypeStruct((ny, owned, kv_width), BF16),
        compiler_params=pltpu.CompilerParams(vmem_limit_bytes=40 * 1024 * 1024),
        cost_estimate=pl.CostEstimate(
            flops=2 * features * seg * kv_width, bytes_accessed=4 * features * seg, transcendentals=0
        ),
    )(turned, both)
    term = lax.all_to_all(term, "y", 0, 0, tiled=True)
    term = jnp.sum(term.astype(F32), axis=0).astype(BF16)
    term = lax.all_to_all(term.reshape(nz, owned // nz, kv_width), "leaf", 0, 0, tiled=True)
    weight_grad = jnp.sum(term.astype(F32), axis=0)
    return (query_grad[None], key_grad[None], value_grad[None], weight_grad)


def solution(mesh):
    trees, nodes = mesh.devices.shape
    side = math.isqrt(trees // 2)
    fine = Mesh(mesh.devices.reshape(side, side, 2, nodes), ("y", "x", "core", "leaf"))
    batch = ("y", "x", "core")
    rows = P(batch, "leaf", None)
    return jax.shard_map(
        on_device,
        mesh=fine,
        in_specs=(rows, rows, rows, rows, rows, P(batch, None), P(batch, None)),
        out_specs=(rows, rows, rows, P((*batch, "leaf"), None)),
        check_vma=False,
    )
```

time: 494 us -> 189 us (0.38)
  waiting for transfers between devices: 367 us -> 103 us
  matrix products: 50.3 us -> 0 us
  blocking collectives: 0 us -> 48.9 us
  other arithmetic: 35.7 us -> 2.45 us
  local copies, waits for them, and re-layouts: 20.2 us -> 5.8 us
  Pallas kernels: 0 us -> 9.7 us
  loops' own time: 5.3 us -> 0 us
    unnamed x5 -> x4, waiting for transfers between devices: 275 us -> 0.57 us
    all_to_all x0 -> x2, blocking collectives: none -> 33.8 us  [the longest x1 19.3 us: on_device(): lax.all_to_all(term.reshape(nz, owned // nz, kv_width), 'leaf', 0, 0, til...]
    dot_general x11 -> x0, matrix products: 33 us -> none  [the longest x4 11.4 us: on_device(): jnp.einsum('igd,jd->gij', grad_four[:, head], value_heads[:, head], prefe...]
    all_to_all x0 -> x1, waiting for transfers between devices: none -> 18.7 us  [on_device(): turned = lax.all_to_all(turned, ('x', 'core'), 0, 0, tiled=True)]
    sub x4 -> x0, matrix products: 17.2 us -> none  [on_device(): raised = jnp.exp(scores - row_max)]
    all_gather x0 -> x1, blocking collectives: none -> 15.1 us  [on_device(): line = lax.all_gather(value_grad, 'x', axis=0)]
    another operation x4 -> x0, other arithmetic: 13 us -> none  [the longest x2 11.8 us: on_device(): probs_all = jnp.stack(prob_list, axis=0)]
    reduce_sum x9 -> x2, other arithmetic: 11.7 us -> 0.75 us  [the longest x1 0.65 us: on_device(): weight_grad = jnp.sum(term.astype(F32), axis=0)]
  transfers between devices with their start and end apart: 4 -> 5, of which waited for: 4 -> 5; matrix products, arithmetic and copies ran while one was open for 10% -> 2% of each run, Pallas kernels for 0% -> 0%
where the time goes in v1:
time: 189 us; the launch traced here: 188 us
  waiting for transfers between devices  103 us (54%)
  blocking collectives  48.9 us (26%)
  between operations  13.8 us (7%)
  Pallas kernels  9.7 us (5%)
  local copies, waits for them, and re-layouts  5.8 us (3%)
  starting transfers between devices  4.6 us (2%)
  other arithmetic  2.45 us (1%)
    reduce_scatter x1, waiting for transfers between devices, on_device(): lax.psum_scatter(value_part, 'leaf', scatter_dimension=0, tiled=True)  44.6 us
    all_gather x1, waiting for transfers between devices, on_device(): lax.all_gather(jnp.concatenate([keys[0], values[0]], axis=1), 'leaf', axi...  19.5 us
    all_to_all x1, blocking collectives, on_device(): lax.all_to_all(term.reshape(nz, owned // nz, kv_width), 'leaf', 0, 0, til...  19.3 us
    all_to_all x1, waiting for transfers between devices, on_device(): turned = lax.all_to_all(turned, ('x', 'core'), 0, 0, tiled=True)  18.7 us
    all_gather x1, blocking collectives, on_device(): line = lax.all_gather(value_grad, 'x', axis=0)  15.1 us
    all_to_all x1, blocking collectives, on_device(): term = lax.all_to_all(term, 'y', 0, 0, tiled=True)  14.5 us
    all_gather x1, waiting for transfers between devices, on_device(): both = lax.all_gather(line, 'core', axis=1).reshape(group, seg, kv_width)  11.4 us
    pallas_call x1, Pallas kernels, attention(): pl.pallas_call(attention_kernel, out_shape=(jax.ShapeDtypeStruct((seg, q_...  8.86 us
  transfers between devices with their start and end apart: 5, of which 5 were waited for; matrix products, arithmetic and copies ran while one was open for 2% of the time, Pallas kernels for 0%

profile of v1, /device:TPU:8, one launch (start us, length us, event | category | flops | bytes accessed | tf_op | source)
XLA Modules:
  0.0 188.1 jit_solution(16856063227688267352)
XLA Ops:
  7.2 0.0 all-gather.5.cloned.1.call-start
  7.2 1.7 pad_maximum_fusion
  8.9 0.0 all-gather.5.cloned.1.call-update
  8.9 1.8 copy.12
  10.7 1.2 copy.13
  11.9 0.0 copy-start.2
  11.9 0.0 copy-start.3
  11.9 0.0 copy-start.4
  11.9 0.0 copy-start.5
  11.9 4.4 %all-to-all-start = ((bf16[8,640,128]{2,1,0:T(8,128)(2,1)}), bf16[8,640,128]{2,1,0:T(8,128)(2,1)S(1)}, u32[]{:S(2)}, u32[]{:S(2)}) async-start(bf16[8,640,128]{2,1,0:T(8,128)(2,1)} %bitcast.25), calls=%async_computation | async-start | bytes 2621440 | tf_op jit(solution)/shard_map/all_to_all | solution.py:210
  16.3 0.0 reduce-scatter.3.cloned.1.call-start
  16.4 18.7 %all-to-all-done.x_ref = bf16[8,640,128]{2,1,0:T(8,128)(2,1)S(1)} async-done(((bf16[8,640,128]{2,1,0:T(8,128)(2,1)}), bf16[8,640,128]{2,1,0:T(8,128)(2,1)S(1)}, u32[]{:S(2)}, u32[]{:S(2)}) %all-to-all-start) | async-done | bytes 1310752 | tf_op jit(solution)/shard_map/all_to_all | solution.py:210
  35.1 19.5 %all-gather.5.cloned.1.call-done.k_ref.v_ref = bf16[1024,1024]{1,0:T(8,128)(2,1)} async-done(((bf16[128,1024]{1,0:T(8,128)(2,1)}), bf16[1024,1024]{1,0:T(8,128)(2,1)}) %all-gather.5.cloned.1.call-update) | async-done | bytes 2097168 | tf_op jit(solution)/shard_map/all_gather | solution.py:202
  54.6 0.0 copy-done.2
  54.6 0.0 copy-done.3
  54.6 0.0 copy-done.4
  54.6 0.0 copy-done.5
  54.6 0.0 copy-start.1
  54.6 1.6 copy-done.1
  56.2 8.9 %shard_map.102 = (bf16[128,4096]{1,0:T(8,128)(2,1)}, bf16[1024,512]{1,0:T(8,128)(2,1)}, bf16[1024,512]{1,0:T(8,128)(2,1)}) custom-call(s32[1]{0:T(128)} %bitcast.own_ref, s32[8]{0:T(128)S(1)} %bitcast.23, s32[8]{0:T(128)S(1)} %bitcast.24, bf16[128,4096]{1,0:T(8,128)(2,1)S(1)} %bitcast.21, bf16[128,4096]{1,0:T(8,128)(2,1)S(1)} %bitcast.22, ...), custom_call_target="tpu_custom_call" | custom-call | flops 5368709120 | bytes 4194304 | tf_op jit(solution)/shard_map/pallas_call | solution.py:141
  65.1 0.0 reduce-scatter.3.cloned.1.call-update
  65.1 0.0 all-gather.7.cloned.1.call-start
  65.1 44.6 %reduce-scatter.3.cloned.1.call-done = bf16[128,512]{1,0:T(8,128)(2,1)} async-done(((bf16[1024,512]{1,0:T(8,128)(2,1)}), bf16[128,512]{1,0:T(8,128)(2,1)}) %reduce-scatter.3.cloned.1.call-update) | async-done | bytes 131088 | tf_op jit(solution)/shard_map/reduce_scatter | solution.py:216
  109.8 15.1 %all-gather = bf16[512,512]{1,0:T(8,128)(2,1)} all-gather(bf16[128,512]{1,0:T(8,128)(2,1)} %reduce-scatter.3.cloned.1.call-done), channel_id=2, replica_groups=mesh['y'=4,'x'=4,'core'=2,'leaf'=8] {'x'}, dimensions={0}, use_global_device_ids=true | all-gather | bytes 655360 | tf_op jit(solution)/shard_map/all_gather | solution.py:220
  124.9 0.0 all-gather.7.cloned.1.call-update
  124.9 0.0 reduce-scatter.5.cloned.1.call-start
  124.9 0.5 reduce-scatter.5.cloned.1.call-update
  125.5 11.4 %all-gather.7.cloned.1.call-done = bf16[4,256,512]{2,1,0:T(8,128)(2,1)} async-done(((bf16[4,128,512]{2,1,0:T(8,128)(2,1)}), bf16[4,256,512]{2,1,0:T(8,128)(2,1)}) %all-gather.7.cloned.1.call-update) | async-done | bytes 1048592 | tf_op jit(solution)/shard_map/all_gather | solution.py:221
  136.9 0.0 copy-start
  136.9 1.2 copy-done
  138.1 0.8 shard_map.103
  139.0 14.5 %all_to_all.15 = bf16[4,160,512]{2,1,0:T(8,128)(2,1)S(1)} all-to-all(bf16[4,160,512]{2,1,0:T(8,128)(2,1)S(1)} %shard_map.103), channel_id=1, replica_groups=mesh['y'=4,'x'=4,'core'=2,'leaf'=8] {'y'}, dimensions={0} | all-to-all | bytes 1310720 | tf_op jit(solution)/shard_map/all_to_all | solution.py:230
  153.5 0.1 reduce_sum.21
  153.7 19.3 %all_to_all.16 = bf16[8,20,512]{2,1,0:T(8,128)(2,1)S(1)} all-to-all(bf16[8,20,512]{2,1,0:T(8,128)(2,1)S(1)} %reshape.27), channel_id=1, replica_groups=mesh['y'=4,'x'=4,'core'=2,'leaf'=8] {'leaf'}, dimensions={0} | all-to-all | bytes 327680 | tf_op jit(solution)/shard_map/all_to_all | solution.py:232
  173.0 0.7 convert_reduce_fusion
  173.6 8.0 %reduce-scatter.5.cloned.1.call-done = bf16[128,512]{1,0:T(8,128)(2,1)} async-done(((bf16[1024,512]{1,0:T(8,128)(2,1)}), bf16[128,512]{1,0:T(8,128)(2,1)}) %reduce-scatter.5.cloned.1.call-update) | async-done | bytes 131088 | tf_op jit(solution)/shard_map/reduce_scatter | solution.py:218
  (1 shorter events, 0.0 us)
Async XLA Ops:
  7.2 47.4 %all-gather.5.cloned.1.call-start = ((), (), s32[]{:S(2)}) async-start(), calls=%async_computation.5 | async-start | bytes 2359296 | tf_op jit(solution)/shard_map/all_gather | solution.py:202
  11.9 42.7 %copy-start.2 = (bf16[1,128,4096]{2,1,0:T(8,128)(2,1)S(1)}, bf16[1,128,4096]{2,1,0:T(8,128)(2,1)}, u32[]{:S(2)}) copy-start(bf16[1,128,4096]{2,1,0:T(8,128)(2,1)} %param.7) | copy-start | bytes 3145732
  11.9 42.7 %copy-start.3 = (bf16[1,128,4096]{2,1,0:T(8,128)(2,1)S(1)}, bf16[1,128,4096]{2,1,0:T(8,128)(2,1)}, u32[]{:S(2)}) copy-start(bf16[1,128,4096]{2,1,0:T(8,128)(2,1)} %param.10) | copy-start | bytes 3145732
  11.9 42.7 %copy-start.4 = (s32[1,8]{1,0:T(1,128)S(1)}, s32[1,8]{1,0:T(1,128)}, u32[]{:S(2)}) copy-start(s32[1,8]{1,0:T(1,128)} %param.12) | copy-start | bytes 100
  11.9 42.7 %copy-start.5 = (s32[1,8]{1,0:T(1,128)S(1)}, s32[1,8]{1,0:T(1,128)}, u32[]{:S(2)}) copy-start(s32[1,8]{1,0:T(1,128)} %param.13) | copy-start | bytes 100
  11.9 23.2 %all-to-all-start = ((bf16[8,640,128]{2,1,0:T(8,128)(2,1)}), bf16[8,640,128]{2,1,0:T(8,128)(2,1)S(1)}, u32[]{:S(2)}, u32[]{:S(2)}) async-start(bf16[8,640,128]{2,1,0:T(8,128)(2,1)} %bitcast.25), calls=%async_computation | async-start | bytes 2621440 | tf_op jit(solution)/shard_map/all_to_all | solution.py:210
  16.3 93.4 %reduce-scatter.3.cloned.1.call-start = ((), (), s32[]{:S(2)}) async-start(), calls=%async_computation.6 | async-start | bytes 1179648 | tf_op jit(solution)/shard_map/reduce_scatter | solution.py:216
  54.6 1.6 copy-start.1
  65.1 71.8 %all-gather.7.cloned.1.call-start = ((), (), s32[]{:S(2)}) async-start(), calls=%async_computation.8 | async-start | bytes 1572864 | tf_op jit(solution)/shard_map/all_gather | solution.py:221
  124.9 56.7 %reduce-scatter.5.cloned.1.call-start = ((), (), s32[]{:S(2)}) async-start(), calls=%async_computation.7 | async-start | bytes 1179648 | tf_op jit(solution)/shard_map/reduce_scatter | solution.py:218
  136.9 1.2 copy-start
Sparse Core Ops, SparseCore 0:
  10.4 44.2 all-gather.4
  65.2 44.5 reduce-scatter.2
  125.0 11.8 all-gather.6
  139.9 41.6 reduce-scatter.4

commit v2 on v1

v2 whole, which is shorter than its diff:
```python
import functools
import math

import jax
import jax.numpy as jnp
from jax import lax
from jax.experimental import pallas as pl
from jax.experimental.pallas import tpu as pltpu
from jax.sharding import Mesh
from jax.sharding import PartitionSpec as P

HD = 128
NEG = -1e30
F32 = jnp.float32
BF16 = jnp.bfloat16
NT = (((1,), (1,)), ((), ()))
TN = (((0,), (0,)), ((), ()))
SCALE = 1.0 / math.sqrt(HD)
RATE = SCALE * math.log2(math.e)
LIMIT = pltpu.CompilerParams(vmem_limit_bytes=60 * 1024 * 1024)


def climb(own_ref, par_ref, len_ref, slot_ref, lim_ref, seg, nodes):
    cursor = own_ref[0]
    slot_ref[0] = cursor
    lim_ref[0] = seg
    count = jnp.int32(1)
    for step in range(1, nodes):
        more = cursor > 0
        up = jnp.where(more, par_ref[cursor], 0)
        slot_ref[step] = up
        lim_ref[step] = jnp.where(more, len_ref[up], 0)
        count = count + more.astype(jnp.int32)
        cursor = up
    return count


def stack_heads(q_ref, g_ref, qs, gs, length):
    seg = q_ref.shape[0]
    live = lax.broadcasted_iota(jnp.int32, (seg, HD), 0) < length
    for head in range(q_ref.shape[1] // HD):
        rows, cols = slice(head * seg, (head + 1) * seg), slice(head * HD, (head + 1) * HD)
        qs[rows, :] = q_ref[:, cols]
        gs[rows, :] = jnp.where(live, g_ref[:, cols], jnp.zeros((), BF16))


def last_places(lim_ref, p, seg, chunk):
    query_place = lax.broadcasted_iota(jnp.int32, (1, chunk), 1) % seg
    last0 = jnp.where(p == 0, query_place, lim_ref[2 * p] - 1)
    last1 = jnp.broadcast_to(lim_ref[2 * p + 1] - 1, query_place.shape)
    return last0, last1


def masked_scores(k2, q, last0, last1):
    seg = k2.shape[0] // 2
    place = lax.broadcasted_iota(jnp.int32, (seg, q.shape[0]), 0)
    s = lax.dot_general(k2, q, NT, preferred_element_type=F32)
    return jnp.where(place <= last0, s[:seg], NEG), jnp.where(place <= last1, s[seg:], NEG)


def value_kernel(own_ref, par_ref, len_ref, q_ref, g_ref, *refs):
    nodes = (len(refs) - 10) // 2
    keys, values = refs[:nodes], refs[nodes : 2 * nodes]
    m_ref, l_ref, qs, gs, kc, dvc, s_scr, p_low, slot_ref, lim_ref = refs[2 * nodes :]
    seg = q_ref.shape[0]
    width = qs.shape[0]
    chunk = 2 * seg
    own = own_ref[0]
    count = climb(own_ref, par_ref, len_ref, slot_ref, lim_ref, seg, nodes)
    pairs = (count + 1) // 2
    stack_heads(q_ref, g_ref, qs, gs, len_ref[own])
    for back in range(nodes):
        kc[back] = keys[back][...]
    dvc[...] = jnp.zeros_like(dvc)
    m_ref[...] = jnp.full_like(m_ref, NEG)
    l_ref[...] = jnp.zeros_like(l_ref)

    def score_step(p, carry):
        k2 = jnp.concatenate([kc[own - slot_ref[2 * p]], kc[own - slot_ref[2 * p + 1]]], axis=0)
        last0, last1 = last_places(lim_ref, p, seg, chunk)
        for c in range(width // chunk):
            cols = slice(c * chunk, (c + 1) * chunk)
            s0, s1 = masked_scores(k2, qs[cols, :], last0, last1)
            s_scr[p, :seg, cols] = s0
            s_scr[p, seg:, cols] = s1
            top = jnp.max(jnp.maximum(s0, s1), axis=0, keepdims=True)
            m_ref[0, :, cols] = jnp.maximum(m_ref[0, :, cols], top)
        return carry

    lax.fori_loop(0, pairs, score_step, 0)

    def sum_step(p, carry):
        for c in range(width // chunk):
            cols = slice(c * chunk, (c + 1) * chunk)
            e = jnp.exp2((s_scr[p, :, cols] - m_ref[0, :, cols]) * RATE)
            s_scr[p, :, cols] = e
            l_ref[0, :, cols] = l_ref[0, :, cols] + jnp.sum(e, axis=0, keepdims=True)
        return carry

    lax.fori_loop(0, pairs, sum_step, 0)
    l_ref[...] = 1.0 / l_ref[...]

    def value_step(p, carry):
        for c in range(width // chunk):
            cols = slice(c * chunk, (c + 1) * chunk)
            p_low[:, cols] = (s_scr[p, :, cols] * l_ref[0, :, cols]).astype(BF16)
        dv = jnp.dot(p_low[...], gs[...], preferred_element_type=F32).astype(BF16)
        dvc[own - slot_ref[2 * p]] = dv[:seg]

        @pl.when(2 * p + 1 < count)
        def _():
            dvc[own - slot_ref[2 * p + 1]] = dv[seg:]

        return carry

    lax.fori_loop(0, pairs, value_step, 0)
    for back in range(nodes):
        values[back][...] = dvc[back]


def score_kernel(kept, own_ref, par_ref, len_ref, q_ref, g_ref, m_ref, l_ref, *refs):
    nodes = len(refs) - 13 - kept
    keys = refs[:nodes]
    v_ref = refs[nodes]
    dq_ref, dk_ref, qs, gs, kc, s_scr, dp_scr, ds_low, t_scr, dqt, slot_ref, lim_ref = refs[nodes + 1 + kept :]
    seg = q_ref.shape[0]
    width = qs.shape[0]
    chunk = 2 * seg
    own = own_ref[0]
    count = climb(own_ref, par_ref, len_ref, slot_ref, lim_ref, seg, nodes)
    pairs = (count + 1) // 2
    stack_heads(q_ref, g_ref, qs, gs, len_ref[own])
    for back in range(nodes):
        kc[back] = keys[back][...]
    dk_ref[...] = jnp.zeros_like(dk_ref)
    t_scr[...] = jnp.zeros_like(t_scr)
    dqt[...] = jnp.zeros_like(dqt)

    def rows(slot):
        return pl.ds(pl.multiple_of(slot_ref[slot] * seg, seg), seg)

    def prob_step(p, carry):
        k2 = jnp.concatenate([kc[own - slot_ref[2 * p]], kc[own - slot_ref[2 * p + 1]]], axis=0)
        v2 = jnp.concatenate([v_ref[rows(2 * p), :], v_ref[rows(2 * p + 1), :]], axis=0)
        last0, last1 = last_places(lim_ref, p, seg, chunk)
        for c in range(width // chunk):
            cols = slice(c * chunk, (c + 1) * chunk)
            s0, s1 = masked_scores(k2, qs[cols, :], last0, last1)
            s = jnp.concatenate([s0, s1], axis=0)
            prob = jnp.exp2((s - m_ref[0, :, cols]) * RATE) * l_ref[0, :, cols]
            dp = lax.dot_general(v2, gs[cols, :], NT, preferred_element_type=F32)
            s_scr[p, :, cols] = prob
            dp_scr[p, :, cols] = dp
            t_scr[:, cols] = t_scr[:, cols] + jnp.sum(prob * dp, axis=0, keepdims=True)
        return carry

    lax.fori_loop(0, pairs, prob_step, 0)

    def grad_step(p, carry):
        k2 = jnp.concatenate([kc[own - slot_ref[2 * p]], kc[own - slot_ref[2 * p + 1]]], axis=0)
        for c in range(width // chunk):
            cols = slice(c * chunk, (c + 1) * chunk)
            ds = (s_scr[p, :, cols] * (dp_scr[p, :, cols] - t_scr[:, cols])).astype(BF16)
            ds_low[:, cols] = ds
            dqt[:, cols] = dqt[:, cols] + lax.dot_general(k2, ds, TN, preferred_element_type=F32)
        dk = (jnp.dot(ds_low[...], qs[...], preferred_element_type=F32) * SCALE).astype(BF16)
        dk_ref[rows(2 * p), :] = dk[:seg]

        @pl.when(2 * p + 1 < count)
        def _():
            dk_ref[rows(2 * p + 1), :] = dk[seg:]

        return carry

    lax.fori_loop(0, pairs, grad_step, 0)
    for head in range(width // seg):
        block = dqt[:, head * seg : (head + 1) * seg] * SCALE
        dq_ref[:, head * HD : (head + 1) * HD] = block.T.astype(BF16)


def weight_kernel(place_ref, x_ref, *refs):
    trees = x_ref.shape[0]
    values, outs = refs[:trees], refs[trees:]
    rows = outs[0].shape[0]
    nx, ny = trees // 2, len(outs)
    px, pc, py = place_ref[0], place_ref[1], place_ref[2]
    for ahead in range(ny):
        part = lax.rem(py + ahead, ny)
        span = pl.ds(pl.multiple_of(part * rows, rows), rows)
        total = None
        for back in range(nx):
            line = 2 * lax.rem(px + nx - back, nx)
            x2 = jnp.concatenate([x_ref[line + pc, span, :], x_ref[line + 1 - pc, span, :]], axis=1)
            v2 = jnp.concatenate([values[2 * back][...], values[2 * back + 1][...]], axis=0)
            term = jnp.dot(x2, v2, preferred_element_type=F32)
            total = term if total is None else total + term
        outs[ahead][...] = total.astype(BF16)


def shift(block, axis, step):
    n = lax.axis_size(axis)
    return lax.ppermute(block, axis, [(i, (i + step) % n) for i in range(n)])


def after(block, *others):
    return lax.optimization_barrier((block, *others))[0]


def plus(a, b):
    return (a.astype(F32) + b.astype(F32)).astype(BF16)


def on_device(queries, keys, values, out_grad, inputs, parents, lengths):
    ny, nx, nc, nz = (lax.axis_size(axis) for axis in ("y", "x", "core", "leaf"))
    seg, features = inputs.shape[1:]
    kv_width, q_width = keys.shape[2], queries.shape[2]
    heads_kv = kv_width // HD
    per_head = q_width // heads_kv
    width = per_head // HD * seg
    rows = nz * seg
    own = lax.axis_index("leaf").astype(jnp.int32).reshape(1)
    scalars = (own, parents[0], lengths[0])

    value_all = lax.all_gather(values[0], "leaf", axis=0, tiled=True)

    group = nx * nc
    owned = features // (ny * group)
    turned = inputs[0].T.reshape(ny, group, owned, seg).transpose(1, 0, 2, 3)
    turned = turned.reshape(group, ny * owned, seg)
    turned = lax.all_to_all(turned, ("x", "core"), 0, 0, tiled=True)

    half = nz // 2
    key_back = [keys[0]] + [None] * (nz - 1)
    for hop in range(1, half + 1):
        held = key_back[hop - 1]
        key_back[hop] = shift(held, "leaf", 1)
        if hop < half:
            key_back[nz - hop] = shift(key_back[(nz - hop + 1) % nz], "leaf", -1)

    turned, *key_back = lax.optimization_barrier((turned, *key_back))

    spec_q = pl.BlockSpec((seg, per_head), lambda k, *_: (0, k))
    spec_b = pl.BlockSpec((seg, HD), lambda k, *_: (0, k))
    spec_k = pl.BlockSpec((rows, HD), lambda k, *_: (0, k))
    spec_s = pl.BlockSpec((1, 1, width), lambda k, *_: (k, 0, 0))
    stats = jax.ShapeDtypeStruct((heads_kv, 1, width), F32)
    stacked = [pltpu.VMEM((width, HD), BF16), pltpu.VMEM((width, HD), BF16)]
    tall = pltpu.VMEM((nz // 2, 2 * seg, width), F32)
    tree = [pltpu.SMEM((nz,), jnp.int32), pltpu.SMEM((nz,), jnp.int32)]
    *value_back, row_max, row_rate = pl.pallas_call(
        value_kernel,
        out_shape=[jax.ShapeDtypeStruct((seg, kv_width), BF16)] * nz + [stats, stats],
        grid_spec=pltpu.PrefetchScalarGridSpec(
            num_scalar_prefetch=3,
            grid=(heads_kv,),
            in_specs=[spec_q, spec_q] + [spec_b] * nz,
            out_specs=[spec_b] * nz + [spec_s, spec_s],
            scratch_shapes=[
                *stacked,
                pltpu.VMEM((nz, seg, HD), BF16),
                pltpu.VMEM((nz, seg, HD), BF16),
                tall,
                pltpu.VMEM((2 * seg, width), BF16),
                *tree,
            ],
        ),
        compiler_params=LIMIT,
        cost_estimate=pl.CostEstimate(
            flops=4 * seg * rows * q_width, bytes_accessed=4 * seg * q_width, transcendentals=0
        ),
    )(*scalars, queries[0], out_grad[0], *key_back)

    def score_grads(first, heads, row_max, kept):
        def moved(spec):
            return pl.BlockSpec(spec.block_shape, lambda k, *_: spec.index_map(k + first))

        given = [moved(spec_q)] * 2 + [moved(spec_s)] * 2 + [moved(spec_b)] * nz + [moved(spec_k)]
        count = len(scalars) + len(given)
        return pl.pallas_call(
            functools.partial(score_kernel, len(kept)),
            out_shape=(
                jax.ShapeDtypeStruct((seg, q_width), BF16),
                jax.ShapeDtypeStruct((rows, kv_width), BF16),
            ),
            grid_spec=pltpu.PrefetchScalarGridSpec(
                num_scalar_prefetch=3,
                grid=(heads,),
                in_specs=given + [pl.BlockSpec(memory_space=pl.ANY)] * len(kept),
                out_specs=[moved(spec_q), moved(spec_k)],
                scratch_shapes=[
                    *stacked,
                    pltpu.VMEM((nz, seg, HD), BF16),
                    tall,
                    tall,
                    pltpu.VMEM((2 * seg, width), BF16),
                    pltpu.VMEM((1, width), F32),
                    pltpu.VMEM((HD, width), F32),
                    *tree,
                ],
            ),
            input_output_aliases={count + i: i for i in range(len(kept))},
            compiler_params=LIMIT,
            cost_estimate=pl.CostEstimate(
                flops=8 * seg * rows * q_width * heads // heads_kv,
                bytes_accessed=6 * seg * q_width * heads // heads_kv,
                transcendentals=0,
            ),
        )(*scalars, queries[0], out_grad[0], row_max, row_rate, *key_back, value_all, *kept)

    up, down = value_back[half], value_back[half - 1]
    grads = ()
    done = 0
    for hop in range(1, half + 1):
        ready = up
        up = shift(up, "leaf", 1)
        if hop < half:
            down = shift(down, "leaf", -1)
        if hop in (2, 3):
            part = heads_kv // 2
            grads = score_grads(done, part, after(row_max, ready), grads)
            done += part
            up, *grads = lax.optimization_barrier((up, *grads))
        if hop < half:
            up = plus(up, value_back[half + hop])
            if hop < half - 1:
                down = plus(down, value_back[half - 1 - hop])
    query_grad, key_part = grads
    value_grad = (
        up.astype(F32) + down.astype(F32) + value_back[0].astype(F32)
    ).astype(BF16)
    key_grad = lax.psum_scatter(key_part, "leaf", scatter_dimension=0, tiled=True)

    line = [value_grad] + [shift(value_grad, "x", back) for back in range(1, nx)]
    both = [block for mine in line for block in (mine, shift(mine, "core", 1))]
    place = jnp.stack([lax.axis_index(axis).astype(jnp.int32) for axis in ("x", "core", "y")])
    whole = pl.BlockSpec(memory_space=pltpu.VMEM)
    terms = pl.pallas_call(
        weight_kernel,
        out_shape=[jax.ShapeDtypeStruct((owned, kv_width), BF16)] * ny,
        in_specs=[pl.BlockSpec(memory_space=pltpu.SMEM)] + [whole] * (1 + group),
        out_specs=[whole] * ny,
        compiler_params=pltpu.CompilerParams(vmem_limit_bytes=24 * 1024 * 1024),
        cost_estimate=pl.CostEstimate(
            flops=2 * features * seg * kv_width, bytes_accessed=4 * features * seg, transcendentals=0
        ),
    )(place, turned, *both)
    term = terms[0].astype(F32)
    for ahead in range(1, ny):
        term = term + shift(terms[ahead], "y", ahead).astype(F32)
    term = term.astype(BF16).reshape(nz, owned // nz, kv_width)
    term = lax.all_to_all(term, "leaf", 0, 0, tiled=True)
    weight_grad = jnp.sum(term.astype(F32), axis=0)
    return (query_grad[None], key_grad[None], value_grad[None], weight_grad)


def solution(mesh):
    trees, nodes = mesh.devices.shape
    side = math.isqrt(trees // 2)
    fine = Mesh(mesh.devices.reshape(side, side, 2, nodes), ("y", "x", "core", "leaf"))
    batch = ("y", "x", "core")
    rows = P(batch, "leaf", None)
    return jax.shard_map(
        on_device,
        mesh=fine,
        in_specs=(rows, rows, rows, rows, rows, P(batch, None), P(batch, None)),
        out_specs=(rows, rows, rows, P((*batch, "leaf"), None)),
        check_vma=False,
    )
```

time: 189 us -> 142 us (0.75)
  waiting for transfers between devices: 103 us -> 45 us
  starting transfers between devices: 4.6 us -> 40.7 us
  blocking collectives: 48.9 us -> 16.6 us
  Pallas kernels: 9.7 us -> 18.4 us
  local copies, waits for them, and re-layouts: 5.8 us -> 3.65 us
    reduce_scatter x1 -> x0, waiting for transfers between devices: 44.6 us -> none  [on_device(): lax.psum_scatter(value_part, 'leaf', scatter_dimension=0, tiled=True)]
    ppermute x0 -> x24, waiting for transfers between devices: none -> 44.3 us  [shift(): return lax.ppermute(block, axis, [(i, (i + step) % n) for i in range(n)])]
    ppermute x0 -> x24, starting transfers between devices: none -> 36.2 us  [shift(): return lax.ppermute(block, axis, [(i, (i + step) % n) for i in range(n)])]
    all_gather x2 -> x1, waiting for transfers between devices: 30.9 us -> 0.01 us  [on_device(): value_all = lax.all_gather(values[0], 'leaf', axis=0, tiled=True)]
    all_to_all x1, waiting for transfers between devices: 18.7 us -> 0.01 us  [on_device(): turned = lax.all_to_all(turned, ('x', 'core'), 0, 0, tiled=True)]
    all_to_all x2 -> x1, blocking collectives: 33.8 us -> 16.6 us  [on_device(): term = lax.all_to_all(term, 'leaf', 0, 0, tiled=True)]
    all_gather x1 -> x0, blocking collectives: 15.1 us -> none  [on_device(): line = lax.all_gather(value_grad, 'x', axis=0)]
    pallas_call x2 -> x4, Pallas kernels: 9.7 us -> 18.4 us  [the longest x2 10.4 us: score_grads(): pl.pallas_call(functools.partial(score_kernel, len(kept)), out_shape=(jax...]
  transfers between devices with their start and end apart: 5 -> 27, of which waited for: 5 -> 16; matrix products, arithmetic and copies ran while one was open for 2% -> 2% of each run, Pallas kernels for 0% -> 13%
where the time goes in v2:
time: 142 us
  waiting for transfers between devices  45 us (32%)
  starting transfers between devices  40.7 us (29%)
  Pallas kernels  18.4 us (13%)
  blocking collectives  16.6 us (12%)
  between operations  14.3 us (10%)
  local copies, waits for them, and re-layouts  3.65 us (3%)
  other arithmetic  2.85 us (2%)
    ppermute x24, waiting for transfers between devices, shift(): return lax.ppermute(block, axis, [(i, (i + step) % n) for i in range(n)])  44.3 us
    ppermute x24, starting transfers between devices, shift(): return lax.ppermute(block, axis, [(i, (i + step) % n) for i in range(n)])  36.2 us
    all_to_all x1, blocking collectives, on_device(): term = lax.all_to_all(term, 'leaf', 0, 0, tiled=True)  16.6 us
    pallas_call x2, Pallas kernels, score_grads(): pl.pallas_call(functools.partial(score_kernel, len(kept)), out_shape=(jax...  10.4 us
    pallas_call x1, Pallas kernels, on_device(): pl.pallas_call(value_kernel, out_shape=[jax.ShapeDtypeStruct((seg, kv_wid...  6.6 us
    all_to_all x1, starting transfers between devices, on_device(): turned = lax.all_to_all(turned, ('x', 'core'), 0, 0, tiled=True)  4.43 us
  transfers between devices with their start and end apart: 27, of which 16 were waited for; matrix products, arithmetic and copies ran while one was open for 2% of the time, Pallas kernels for 13%

profile of v2, /device:TPU:8, one launch (start us, length us, event | category | flops | bytes accessed | tf_op | source)
XLA Modules:
  0.0 141.6 jit_solution(1229345356272543112)
XLA Ops:
  7.2 1.8 %copy.14 = bf16[1,128,5120]{1,2,0:T(8,128)(2,1)S(1)} copy(bf16[1,128,5120]{2,1,0:T(8,128)(2,1)} %param.11) | data formatting | bytes 2621440 | tf_op args[4]
  8.9 1.2 copy.15
  10.2 4.4 %all-to-all-start = ((bf16[8,640,128]{2,1,0:T(8,128)(2,1)}), bf16[8,640,128]{2,1,0:T(8,128)(2,1)S(1)}, u32[]{:S(2)}, u32[]{:S(2)}) async-start(bf16[8,640,128]{2,1,0:T(8,128)(2,1)} %bitcast.9), calls=%async_computation | async-start | bytes 2621440 | tf_op jit(solution)/shard_map/all_to_all | solution.py:230
  14.6 0.0 all-gather.3.cloned.1.call-start
  14.6 0.7 all-gather.3.cloned.1.call-update
  15.3 0.0 reduce-scatter.2.cloned.1.call-start
  15.4 2.0 %collective-permute-start = (bf16[128,512]{1,0:T(8,128)(2,1)S(1)}, bf16[128,512]{1,0:T(8,128)(2,1)S(1)}, u32[]{:S(2)}, u32[]{:S(2)}) collective-permute-start(bf16[128,512]{1,0:T(8,128)(2,1)S(1)} %bitcast.34), channel_id=1, source_target_pairs={{0,1},{1,2},{2,3},{3,4},{4,5},{5,6},{6,7},{7,0},{8,9},{9,10},{10,1... | collective-permute-start | bytes 393224 | tf_op jit(solution)/shard_map/ppermute | solution.py:202
  17.4 4.0 %collective-permute-start.4 = (bf16[128,512]{1,0:T(8,128)(2,1)S(1)}, bf16[128,512]{1,0:T(8,128)(2,1)S(1)}, u32[]{:S(2)}, u32[]{:S(2)}) collective-permute-start(bf16[128,512]{1,0:T(8,128)(2,1)S(1)} %bitcast.35), channel_id=1, source_target_pairs={{0,7},{1,0},{2,1},{3,2},{4,3},{5,4},{6,5},{7,6},{8,15},{9,8},{10,9... | collective-permute-start | bytes 393224 | tf_op jit(solution)/shard_map/ppermute | solution.py:202
  21.4 4.1 %collective-permute-done.refs_1_ = bf16[128,512]{1,0:T(8,128)(2,1)S(1)} collective-permute-done((bf16[128,512]{1,0:T(8,128)(2,1)S(1)}, bf16[128,512]{1,0:T(8,128)(2,1)S(1)}, u32[]{:S(2)}, u32[]{:S(2)}) %collective-permute-start) | collective-permute-done | bytes 131104 | tf_op jit(solution)/shard_map/ppermute | solution.py:202
  25.5 0.0 collective-permute-start.1
  25.5 0.0 collective-permute-done.4.refs_7_
  25.5 3.2 %collective-permute-start.5 = (bf16[128,512]{1,0:T(8,128)(2,1)S(1)}, bf16[128,512]{1,0:T(8,128)(2,1)S(1)}, u32[]{:S(2)}, u32[]{:S(2)}) collective-permute-start(bf16[128,512]{1,0:T(8,128)(2,1)S(1)} %collective-permute-done.4.refs_7_), channel_id=1, source_target_pairs={{0,7},{1,0},{2,1},{3,2},{4,3},{5,4},{6,5},{7,6},{8,15},{9,8},{10,9... | collective-permute-start | bytes 393224 | tf_op jit(solution)/shard_map/ppermute | solution.py:202
  28.7 3.3 %collective-permute-done.1.refs_2_ = bf16[128,512]{1,0:T(8,128)(2,1)S(1)} collective-permute-done((bf16[128,512]{1,0:T(8,128)(2,1)S(1)}, bf16[128,512]{1,0:T(8,128)(2,1)S(1)}, u32[]{:S(2)}, u32[]{:S(2)}) %collective-permute-start.1) | collective-permute-done | bytes 131104 | tf_op jit(solution)/shard_map/ppermute | solution.py:202
  32.0 0.0 collective-permute-start.2
  32.0 0.0 collective-permute-done.5.refs_6_
  32.0 3.2 %collective-permute-start.6 = (bf16[128,512]{1,0:T(8,128)(2,1)S(1)}, bf16[128,512]{1,0:T(8,128)(2,1)S(1)}, u32[]{:S(2)}, u32[]{:S(2)}) collective-permute-start(bf16[128,512]{1,0:T(8,128)(2,1)S(1)} %collective-permute-done.5.refs_6_), channel_id=1, source_target_pairs={{0,7},{1,0},{2,1},{3,2},{4,3},{5,4},{6,5},{7,6},{8,15},{9,8},{10,9... | collective-permute-start | bytes 393224 | tf_op jit(solution)/shard_map/ppermute | solution.py:202
  35.2 4.0 %collective-permute-done.2.refs_3_ = bf16[128,512]{1,0:T(8,128)(2,1)S(1)} collective-permute-done((bf16[128,512]{1,0:T(8,128)(2,1)S(1)}, bf16[128,512]{1,0:T(8,128)(2,1)S(1)}, u32[]{:S(2)}, u32[]{:S(2)}) %collective-permute-start.2) | collective-permute-done | bytes 131104 | tf_op jit(solution)/shard_map/ppermute | solution.py:202
  39.3 7.2 %collective-permute-done.3.refs_4_ = bf16[128,512]{1,0:T(8,128)(2,1)S(1)} collective-permute-done((bf16[128,512]{1,0:T(8,128)(2,1)S(1)}, bf16[128,512]{1,0:T(8,128)(2,1)S(1)}, u32[]{:S(2)}, u32[]{:S(2)}) %collective-permute-start.3) | collective-permute-done | bytes 131104 | tf_op jit(solution)/shard_map/ppermute | solution.py:202
  46.5 0.0 all-to-all-done.x_ref
  46.5 0.6 copy-done.12
  47.1 6.6 %shard_map.102 = (bf16[128,512]{1,0:T(8,128)(2,1)}, bf16[128,512]{1,0:T(8,128)(2,1)}, bf16[128,512]{1,0:T(8,128)(2,1)}, bf16[128,512]{1,0:T(8,128)(2,1)}, bf16[1...) custom-call(s32[1]{0:T(128)} %bitcast.own_ref, ...), custom_call_target="tpu_custom_call" | custom-call | flops 2147483648 | bytes 2097152 | tf_op jit(solution)/shard_map/pallas_call | solution.py:250
  53.7 0.1 collective-permute-start.7
  53.8 3.2 %collective-permute-start.11 = (bf16[128,512]{1,0:T(8,128)(2,1)}, bf16[128,512]{1,0:T(8,128)(2,1)S(1)}, u32[]{:S(2)}, u32[]{:S(2)}) collective-permute-start(bf16[128,512]{1,0:T(8,128)(2,1)} %get-tuple-element.65), channel_id=1, source_target_pairs={{0,7},{1,0},{2,1},{3,2},{4,3},{5,4},{6,5},{7,6},{8,15},{9,8},{10,9... | collective-permute-start | bytes 393224 | tf_op jit(solution)/shard_map/ppermute | solution.py:202
  57.0 3.3 %collective-permute-done.7 = bf16[128,512]{1,0:T(8,128)(2,1)S(1)} collective-permute-done((bf16[128,512]{1,0:T(8,128)(2,1)}, bf16[128,512]{1,0:T(8,128)(2,1)S(1)}, u32[]{:S(2)}, u32[]{:S(2)}) %collective-permute-start.7) | collective-permute-done | bytes 131104 | tf_op jit(solution)/shard_map/ppermute | solution.py:202
  60.4 0.9 add_convert_fusion.6
  61.3 0.1 collective-permute-start.8
  61.4 0.9 add_convert_fusion.3
  62.4 3.3 %collective-permute-start.12 = (bf16[128,512]{1,0:T(8,128)(2,1)S(1)}, bf16[128,512]{1,0:T(8,128)(2,1)S(1)}, u32[]{:S(2)}, u32[]{:S(2)}) collective-permute-start(bf16[128,512]{1,0:T(8,128)(2,1)S(1)} %add_convert_fusion.3), channel_id=1, source_target_pairs={{0,7},{1,0},{2,1},{3,2},{4,3},{5,4},{6,5},{7,6},{8,15},{9,8},{10,9... | collective-permute-start | bytes 393224 | tf_op jit(solution)/shard_map/ppermute | solution.py:202
  65.7 5.3 %shard_map.103 = (bf16[128,4096]{1,0:T(8,128)(2,1)}, bf16[1024,512]{1,0:T(8,128)(2,1)}) custom-call(s32[1]{0:T(128)} %bitcast.own_ref, s32[8]{0:T(128)} %bitcast.38, s32[8]{0:T(128)} %bitcast.41, bf16[128,4096]{1,0:T(8,128)(2,1)} %bitcast.24, bf16[128,4096]{1,0:T(8,128)(2,1)} %bitcast.27, f32[4,1,1024]{2,1,0:T(1,128)} %get-tuple-element.56.m_ref, ...), custom_call_target="tpu_custom_call" | custom-call | flops 2147483648 | bytes 1572864 | tf_op jit(solution)/shard_map/pallas_call | solution.py:279
  70.9 0.0 collective-permute-done.8
  71.0 0.3 collective-permute-start.9
  71.3 5.2 %shard_map.104 = (bf16[128,4096]{1,0:T(8,128)(2,1)}, bf16[1024,512]{1,0:T(8,128)(2,1)}) custom-call(s32[1]{0:T(128)} %bitcast.own_ref, s32[8]{0:T(128)} %bitcast.39, s32[8]{0:T(128)} %bitcast.42, bf16[128,4096]{1,0:T(8,128)(2,1)} %bitcast.25, bf16[128,4096]{1,0:T(8,128)(2,1)} %bitcast.28, ...), custom_call_target="tpu_custom_call", output_to_operand_aliasing={{0}: (16, {}), {1}: (17, {})} | custom-call | flops 2147483648 | bytes 1572864 | tf_op jit(solution)/shard_map/pallas_call | solution.py:279
  76.5 1.0 collective-permute-done.9
  77.4 0.0 reduce-scatter.2.cloned.1.call-update
  77.5 0.0 collective-permute-done.12
  77.5 4.1 %collective-permute-start.13 = (bf16[128,512]{1,0:T(8,128)(2,1)S(1)}, bf16[128,512]{1,0:T(8,128)(2,1)S(1)}, u32[]{:S(2)}, u32[]{:S(2)}) collective-permute-start(bf16[128,512]{1,0:T(8,128)(2,1)S(1)} %add_convert_fusion.2), channel_id=1, source_target_pairs={{0,7},{1,0},{2,1},{3,2},{4,3},{5,4},{6,5},{7,6},{8,15},{9,8},{10,9... | collective-permute-start | bytes 393224 | tf_op jit(solution)/shard_map/ppermute | solution.py:202
  81.7 0.1 collective-permute-start.10
  81.8 2.4 %collective-permute-done.13 = bf16[128,512]{1,0:T(8,128)(2,1)S(1)} collective-permute-done((bf16[128,512]{1,0:T(8,128)(2,1)S(1)}, bf16[128,512]{1,0:T(8,128)(2,1)S(1)}, u32[]{:S(2)}, u32[]{:S(2)}) %collective-permute-start.13) | collective-permute-done | bytes 131104 | tf_op jit(solution)/shard_map/ppermute | solution.py:202
  84.2 3.8 %collective-permute-done.10 = bf16[128,512]{1,0:T(8,128)(2,1)S(1)} collective-permute-done((bf16[128,512]{1,0:T(8,128)(2,1)S(1)}, bf16[128,512]{1,0:T(8,128)(2,1)S(1)}, u32[]{:S(2)}, u32[]{:S(2)}) %collective-permute-start.10) | collective-permute-done | bytes 131104 | tf_op jit(solution)/shard_map/ppermute | solution.py:202
  87.9 0.1 add_convert_fusion.1.refs_0_
  88.0 0.0 copy-start
  88.0 8.0 %collective-permute-start.19 = (bf16[128,512]{1,0:T(8,128)(2,1)S(1)}, bf16[128,512]{1,0:T(8,128)(2,1)S(1)}, u32[]{:S(2)}, u32[]{:S(2)}) collective-permute-start(bf16[128,512]{1,0:T(8,128)(2,1)S(1)} %add_convert_fusion.1.refs_0_), channel_id=1, source_target_pairs={{0,48},{16,0},{32,16},{48,32},{1,49},{17,1},{33,17},{49,33},{2,50}... | collective-permute-start | bytes 393224 | tf_op jit(solution)/shard_map/ppermute | solution.py:202
  96.0 1.0 collective-permute-start.15
  97.0 0.0 collective-permute-start.14
  97.0 3.0 %collective-permute-done.19.refs_6_ = bf16[128,512]{1,0:T(8,128)(2,1)S(1)} collective-permute-done((bf16[128,512]{1,0:T(8,128)(2,1)S(1)}, bf16[128,512]{1,0:T(8,128)(2,1)S(1)}, u32[]{:S(2)}, u32[]{:S(2)}) %collective-permute-start.19) | collective-permute-done | bytes 131104 | tf_op jit(solution)/shard_map/ppermute | solution.py:202
  99.9 0.0 collective-permute-start.20
  99.9 2.6 %collective-permute-done.17.refs_4_ = bf16[128,512]{1,0:T(8,128)(2,1)S(1)} collective-permute-done((bf16[128,512]{1,0:T(8,128)(2,1)S(1)}, bf16[128,512]{1,0:T(8,128)(2,1)S(1)}, u32[]{:S(2)}, u32[]{:S(2)}) %collective-permute-start.17) | collective-permute-done | bytes 131104 | tf_op jit(solution)/shard_map/ppermute | solution.py:202
  102.6 0.0 collective-permute-start.18
  102.6 1.0 collective-permute-done.15.refs_2_
  103.6 0.1 pad_add_fusion.place_ref
  103.7 0.0 collective-permute-done.14.refs_1_
  103.7 0.0 collective-permute-done.20.refs_7_
  103.7 0.3 collective-permute-done.18.refs_5_
  103.9 1.0 collective-permute-done.16.refs_3_
  104.9 1.4 shard_map.105
  106.3 0.1 collective-permute-start.21
  106.4 1.0 collective-permute-start.22
  107.4 2.5 %collective-permute-start.23 = (bf16[160,512]{1,0:T(8,128)(2,1)S(1)}, bf16[160,512]{1,0:T(8,128)(2,1)S(1)}, u32[]{:S(2)}, u32[]{:S(2)}) collective-permute-start(bf16[160,512]{1,0:T(8,128)(2,1)S(1)} %get-tuple-element.73), channel_id=1, source_target_pairs={{0,192},{64,0},{128,64},{192,128},{1,193},{65,1},{129,65},{193,129... | collective-permute-start | bytes 491528 | tf_op jit(solution)/shard_map/ppermute | solution.py:202
  110.0 3.5 %collective-permute-done.21 = bf16[160,512]{1,0:T(8,128)(2,1)S(1)} collective-permute-done((bf16[160,512]{1,0:T(8,128)(2,1)S(1)}, bf16[160,512]{1,0:T(8,128)(2,1)S(1)}, u32[]{:S(2)}, u32[]{:S(2)}) %collective-permute-start.21) | collective-permute-done | bytes 163872 | tf_op jit(solution)/shard_map/ppermute | solution.py:202
  113.4 1.7 %collective-permute-done.22 = bf16[160,512]{1,0:T(8,128)(2,1)S(1)} collective-permute-done((bf16[160,512]{1,0:T(8,128)(2,1)S(1)}, bf16[160,512]{1,0:T(8,128)(2,1)S(1)}, u32[]{:S(2)}, u32[]{:S(2)}) %collective-permute-start.22) | collective-permute-done | bytes 163872 | tf_op jit(solution)/shard_map/ppermute | solution.py:202
  115.1 2.3 %collective-permute-done.23 = bf16[160,512]{1,0:T(8,128)(2,1)S(1)} collective-permute-done((bf16[160,512]{1,0:T(8,128)(2,1)S(1)}, bf16[160,512]{1,0:T(8,128)(2,1)S(1)}, u32[]{:S(2)}, u32[]{:S(2)}) %collective-permute-start.23) | collective-permute-done | bytes 163872 | tf_op jit(solution)/shard_map/ppermute | solution.py:202
  117.4 0.1 add_convert_fusion
  117.5 16.6 %all_to_all.10 = bf16[8,20,512]{2,1,0:T(8,128)(2,1)S(1)} all-to-all(bf16[8,20,512]{2,1,0:T(8,128)(2,1)S(1)} %reshape.23), channel_id=1, replica_groups=mesh['y'=4,'x'=4,'core'=2,'leaf'=8] {'leaf'}, dimensions={0} | all-to-all | bytes 327680 | tf_op jit(solution)/shard_map/all_to_all | solution.py:351
  134.1 0.7 convert_reduce_fusion
  (35 shorter events, 0.2 us)
Async XLA Ops:
  10.2 5.2 %copy-start.5 = (bf16[1,128,512]{2,1,0:T(8,128)(2,1)S(1)}, bf16[1,128,512]{2,1,0:T(8,128)(2,1)}, u32[]{:S(2)}) copy-start(bf16[1,128,512]{2,1,0:T(8,128)(2,1)} %param.8) | copy-start | bytes 393220
  10.2 36.3 %all-to-all-start = ((bf16[8,640,128]{2,1,0:T(8,128)(2,1)}), bf16[8,640,128]{2,1,0:T(8,128)(2,1)S(1)}, u32[]{:S(2)}, u32[]{:S(2)}) async-start(bf16[8,640,128]{2,1,0:T(8,128)(2,1)} %bitcast.9), calls=%async_computation | async-start | bytes 2621440 | tf_op jit(solution)/shard_map/all_to_all | solution.py:230
  14.6 51.1 %all-gather.3.cloned.1.call-start = ((), (), s32[]{:S(2)}) async-start(), calls=%async_computation.4 | async-start | bytes 1179648 | tf_op jit(solution)/shard_map/all_gather | solution.py:224
  15.3 119.4 %reduce-scatter.2.cloned.1.call-start = ((), (), s32[]{:S(2)}) async-start(), calls=%async_computation.3 | async-start | bytes 1179648 | tf_op jit(solution)/shard_map/reduce_scatter | solution.py:331
  15.4 10.1 %collective-permute-start = (bf16[128,512]{1,0:T(8,128)(2,1)S(1)}, bf16[128,512]{1,0:T(8,128)(2,1)S(1)}, u32[]{:S(2)}, u32[]{:S(2)}) collective-permute-start(bf16[128,512]{1,0:T(8,128)(2,1)S(1)} %bitcast.34), channel_id=1, source_target_pairs={{0,1},{1,2},{2,3},{3,4},{4,5},{5,6},{6,7},{7,0},{8,9},{9,10},{10,1... | collective-permute-start | bytes 393224 | tf_op jit(solution)/shard_map/ppermute | solution.py:202
  17.4 8.1 %collective-permute-start.4 = (bf16[128,512]{1,0:T(8,128)(2,1)S(1)}, bf16[128,512]{1,0:T(8,128)(2,1)S(1)}, u32[]{:S(2)}, u32[]{:S(2)}) collective-permute-start(bf16[128,512]{1,0:T(8,128)(2,1)S(1)} %bitcast.35), channel_id=1, source_target_pairs={{0,7},{1,0},{2,1},{3,2},{4,3},{5,4},{6,5},{7,6},{8,15},{9,8},{10,9... | collective-permute-start | bytes 393224 | tf_op jit(solution)/shard_map/ppermute | solution.py:202
  25.5 21.0 %copy-start.6 = (bf16[128,512]{1,0:T(8,128)(2,1)}, bf16[128,512]{1,0:T(8,128)(2,1)S(1)}, u32[]{:S(2)}) copy-start(bf16[128,512]{1,0:T(8,128)(2,1)S(1)} %collective-permute-done.refs_1_) | copy-start | bytes 393220
  25.5 6.5 %collective-permute-start.1 = (bf16[128,512]{1,0:T(8,128)(2,1)S(1)}, bf16[128,512]{1,0:T(8,128)(2,1)S(1)}, u32[]{:S(2)}, u32[]{:S(2)}) collective-permute-start(bf16[128,512]{1,0:T(8,128)(2,1)S(1)} %collective-permute-done.refs_1_), channel_id=1, source_target_pairs={{0,1},{1,2},{2,3},{3,4},{4,5},{5,6},{6,7},{7,0},{8,9},{9,10},{10,1... | collective-permute-start | bytes 393224 | tf_op jit(solution)/shard_map/ppermute | solution.py:202
  25.5 21.0 %copy-start.7 = (bf16[128,512]{1,0:T(8,128)(2,1)}, bf16[128,512]{1,0:T(8,128)(2,1)S(1)}, u32[]{:S(2)}) copy-start(bf16[128,512]{1,0:T(8,128)(2,1)S(1)} %collective-permute-done.4.refs_7_) | copy-start | bytes 393220
  25.5 6.5 %collective-permute-start.5 = (bf16[128,512]{1,0:T(8,128)(2,1)S(1)}, bf16[128,512]{1,0:T(8,128)(2,1)S(1)}, u32[]{:S(2)}, u32[]{:S(2)}) collective-permute-start(bf16[128,512]{1,0:T(8,128)(2,1)S(1)} %collective-permute-done.4.refs_7_), channel_id=1, source_target_pairs={{0,7},{1,0},{2,1},{3,2},{4,3},{5,4},{6,5},{7,6},{8,15},{9,8},{10,9... | collective-permute-start | bytes 393224 | tf_op jit(solution)/shard_map/ppermute | solution.py:202
  32.0 14.5 %copy-start.8 = (bf16[128,512]{1,0:T(8,128)(2,1)}, bf16[128,512]{1,0:T(8,128)(2,1)S(1)}, u32[]{:S(2)}) copy-start(bf16[128,512]{1,0:T(8,128)(2,1)S(1)} %collective-permute-done.1.refs_2_) | copy-start | bytes 393220
  32.0 7.3 %collective-permute-start.2 = (bf16[128,512]{1,0:T(8,128)(2,1)S(1)}, bf16[128,512]{1,0:T(8,128)(2,1)S(1)}, u32[]{:S(2)}, u32[]{:S(2)}) collective-permute-start(bf16[128,512]{1,0:T(8,128)(2,1)S(1)} %collective-permute-done.1.refs_2_), channel_id=1, source_target_pairs={{0,1},{1,2},{2,3},{3,4},{4,5},{5,6},{6,7},{7,0},{8,9},{9,10},{10,1... | collective-permute-start | bytes 393224 | tf_op jit(solution)/shard_map/ppermute | solution.py:202
  32.0 14.5 %copy-start.9 = (bf16[128,512]{1,0:T(8,128)(2,1)}, bf16[128,512]{1,0:T(8,128)(2,1)S(1)}, u32[]{:S(2)}) copy-start(bf16[128,512]{1,0:T(8,128)(2,1)S(1)} %collective-permute-done.5.refs_6_) | copy-start | bytes 393220
  32.0 7.2 %collective-permute-start.6 = (bf16[128,512]{1,0:T(8,128)(2,1)S(1)}, bf16[128,512]{1,0:T(8,128)(2,1)S(1)}, u32[]{:S(2)}, u32[]{:S(2)}) collective-permute-start(bf16[128,512]{1,0:T(8,128)(2,1)S(1)} %collective-permute-done.5.refs_6_), channel_id=1, source_target_pairs={{0,7},{1,0},{2,1},{3,2},{4,3},{5,4},{6,5},{7,6},{8,15},{9,8},{10,9... | collective-permute-start | bytes 393224 | tf_op jit(solution)/shard_map/ppermute | solution.py:202
  39.3 7.3 %copy-start.10 = (bf16[128,512]{1,0:T(8,128)(2,1)}, bf16[128,512]{1,0:T(8,128)(2,1)S(1)}, u32[]{:S(2)}) copy-start(bf16[128,512]{1,0:T(8,128)(2,1)S(1)} %collective-permute-done.2.refs_3_) | copy-start | bytes 393220
  39.3 7.2 %collective-permute-start.3 = (bf16[128,512]{1,0:T(8,128)(2,1)S(1)}, bf16[128,512]{1,0:T(8,128)(2,1)S(1)}, u32[]{:S(2)}, u32[]{:S(2)}) collective-permute-start(bf16[128,512]{1,0:T(8,128)(2,1)S(1)} %collective-permute-done.2.refs_3_), channel_id=1, source_target_pairs={{0,1},{1,2},{2,3},{3,4},{4,5},{5,6},{6,7},{7,0},{8,9},{9,10},{10,1... | collective-permute-start | bytes 393224 | tf_op jit(solution)/shard_map/ppermute | solution.py:202
  39.3 7.3 %copy-start.11 = (bf16[128,512]{1,0:T(8,128)(2,1)}, bf16[128,512]{1,0:T(8,128)(2,1)S(1)}, u32[]{:S(2)}) copy-start(bf16[128,512]{1,0:T(8,128)(2,1)S(1)} %collective-permute-done.6.refs_5_) | copy-start | bytes 393220
  46.5 0.6 copy-start.12
  53.7 6.6 %collective-permute-start.7 = (bf16[128,512]{1,0:T(8,128)(2,1)}, bf16[128,512]{1,0:T(8,128)(2,1)S(1)}, u32[]{:S(2)}, u32[]{:S(2)}) collective-permute-start(bf16[128,512]{1,0:T(8,128)(2,1)} %get-tuple-element.47), channel_id=1, source_target_pairs={{0,1},{1,2},{2,3},{3,4},{4,5},{5,6},{6,7},{7,0},{8,9},{9,10},{10,1... | collective-permute-start | bytes 393224 | tf_op jit(solution)/shard_map/ppermute | solution.py:202
  53.8 7.6 %collective-permute-start.11 = (bf16[128,512]{1,0:T(8,128)(2,1)}, bf16[128,512]{1,0:T(8,128)(2,1)S(1)}, u32[]{:S(2)}, u32[]{:S(2)}) collective-permute-start(bf16[128,512]{1,0:T(8,128)(2,1)} %get-tuple-element.65), channel_id=1, source_target_pairs={{0,7},{1,0},{2,1},{3,2},{4,3},{5,4},{6,5},{7,6},{8,15},{9,8},{10,9... | collective-permute-start | bytes 393224 | tf_op jit(solution)/shard_map/ppermute | solution.py:202
  61.3 9.6 %collective-permute-start.8 = (bf16[128,512]{1,0:T(8,128)(2,1)S(1)}, bf16[128,512]{1,0:T(8,128)(2,1)S(1)}, u32[]{:S(2)}, u32[]{:S(2)}) collective-permute-start(bf16[128,512]{1,0:T(8,128)(2,1)S(1)} %add_convert_fusion.6), channel_id=1, source_target_pairs={{0,1},{1,2},{2,3},{3,4},{4,5},{5,6},{6,7},{7,0},{8,9},{9,10},{10,1... | collective-permute-start | bytes 393224 | tf_op jit(solution)/shard_map/ppermute | solution.py:202
  62.4 15.1 %collective-permute-start.12 = (bf16[128,512]{1,0:T(8,128)(2,1)S(1)}, bf16[128,512]{1,0:T(8,128)(2,1)S(1)}, u32[]{:S(2)}, u32[]{:S(2)}) collective-permute-start(bf16[128,512]{1,0:T(8,128)(2,1)S(1)} %add_convert_fusion.3), channel_id=1, source_target_pairs={{0,7},{1,0},{2,1},{3,2},{4,3},{5,4},{6,5},{7,6},{8,15},{9,8},{10,9... | collective-permute-start | bytes 393224 | tf_op jit(solution)/shard_map/ppermute | solution.py:202
  65.6 5.3 %copy-start.3 = (bf16[128,512]{1,0:T(8,128)(2,1)S(1)}, bf16[128,512]{1,0:T(8,128)(2,1)}, u32[]{:S(2)}) copy-start(bf16[128,512]{1,0:T(8,128)(2,1)} %get-tuple-element.55) | copy-start | bytes 393220
  71.0 6.5 %copy-start.2 = (bf16[128,512]{1,0:T(8,128)(2,1)S(1)}, bf16[128,512]{1,0:T(8,128)(2,1)}, u32[]{:S(2)}) copy-start(bf16[128,512]{1,0:T(8,128)(2,1)} %get-tuple-element.67) | copy-start | bytes 393220
  71.0 6.4 %collective-permute-start.9 = (bf16[128,512]{1,0:T(8,128)(2,1)S(1)}, bf16[128,512]{1,0:T(8,128)(2,1)S(1)}, u32[]{:S(2)}, u32[]{:S(2)}) collective-permute-start(bf16[128,512]{1,0:T(8,128)(2,1)S(1)} %add_convert_fusion.5), channel_id=1, source_target_pairs={{0,1},{1,2},{2,3},{3,4},{4,5},{5,6},{6,7},{7,0},{8,9},{9,10},{10,1... | collective-permute-start | bytes 393224 | tf_op jit(solution)/shard_map/ppermute | solution.py:202
  76.4 5.2 %copy-start.1 = (bf16[128,512]{1,0:T(8,128)(2,1)S(1)}, bf16[128,512]{1,0:T(8,128)(2,1)}, u32[]{:S(2)}) copy-start(bf16[128,512]{1,0:T(8,128)(2,1)} %get-tuple-element.64) | copy-start | bytes 393220
  76.4 11.5 %copy-start.4 = (bf16[128,512]{1,0:T(8,128)(2,1)S(1)}, bf16[128,512]{1,0:T(8,128)(2,1)}, u32[]{:S(2)}) copy-start(bf16[128,512]{1,0:T(8,128)(2,1)} %get-tuple-element.68) | copy-start | bytes 393220
  77.5 6.6 %collective-permute-start.13 = (bf16[128,512]{1,0:T(8,128)(2,1)S(1)}, bf16[128,512]{1,0:T(8,128)(2,1)S(1)}, u32[]{:S(2)}, u32[]{:S(2)}) collective-permute-start(bf16[128,512]{1,0:T(8,128)(2,1)S(1)} %add_convert_fusion.2), channel_id=1, source_target_pairs={{0,7},{1,0},{2,1},{3,2},{4,3},{5,4},{6,5},{7,6},{8,15},{9,8},{10,9... | collective-permute-start | bytes 393224 | tf_op jit(solution)/shard_map/ppermute | solution.py:202
  81.7 6.3 %collective-permute-start.10 = (bf16[128,512]{1,0:T(8,128)(2,1)S(1)}, bf16[128,512]{1,0:T(8,128)(2,1)S(1)}, u32[]{:S(2)}, u32[]{:S(2)}) collective-permute-start(bf16[128,512]{1,0:T(8,128)(2,1)S(1)} %add_convert_fusion.4), channel_id=1, source_target_pairs={{0,1},{1,2},{2,3},{3,4},{4,5},{5,6},{6,7},{7,0},{8,9},{9,10},{10,1... | collective-permute-start | bytes 393224 | tf_op jit(solution)/shard_map/ppermute | solution.py:202
  88.0 29.4 %copy-start = (bf16[128,512]{1,0:T(8,128)(2,1)}, bf16[128,512]{1,0:T(8,128)(2,1)S(1)}, u32[]{:S(2)}) copy-start(bf16[128,512]{1,0:T(8,128)(2,1)S(1)} %add_convert_fusion.1.refs_0_) | copy-start | bytes 393220
  88.0 11.9 %collective-permute-start.19 = (bf16[128,512]{1,0:T(8,128)(2,1)S(1)}, bf16[128,512]{1,0:T(8,128)(2,1)S(1)}, u32[]{:S(2)}, u32[]{:S(2)}) collective-permute-start(bf16[128,512]{1,0:T(8,128)(2,1)S(1)} %add_convert_fusion.1.refs_0_), channel_id=1, source_target_pairs={{0,48},{16,0},{32,16},{48,32},{1,49},{17,1},{33,17},{49,33},{2,50}... | collective-permute-start | bytes 393224 | tf_op jit(solution)/shard_map/ppermute | solution.py:202
  96.0 6.6 %collective-permute-start.17 = (bf16[128,512]{1,0:T(8,128)(2,1)S(1)}, bf16[128,512]{1,0:T(8,128)(2,1)S(1)}, u32[]{:S(2)}, u32[]{:S(2)}) collective-permute-start(bf16[128,512]{1,0:T(8,128)(2,1)S(1)} %add_convert_fusion.1.refs_0_), channel_id=1, source_target_pairs={{0,32},{16,48},{32,0},{48,16},{1,33},{17,49},{33,1},{49,17},{2,34}... | collective-permute-start | bytes 393224 | tf_op jit(solution)/shard_map/ppermute | solution.py:202
  96.0 7.6 %collective-permute-start.15 = (bf16[128,512]{1,0:T(8,128)(2,1)S(1)}, bf16[128,512]{1,0:T(8,128)(2,1)S(1)}, u32[]{:S(2)}, u32[]{:S(2)}) collective-permute-start(bf16[128,512]{1,0:T(8,128)(2,1)S(1)} %add_convert_fusion.1.refs_0_), channel_id=1, source_target_pairs={{0,16},{16,32},{32,48},{48,0},{1,17},{17,33},{33,49},{49,1},{2,18}... | collective-permute-start | bytes 393224 | tf_op jit(solution)/shard_map/ppermute | solution.py:202
  97.0 6.7 %collective-permute-start.14 = (bf16[128,512]{1,0:T(8,128)(2,1)S(1)}, bf16[128,512]{1,0:T(8,128)(2,1)S(1)}, u32[]{:S(2)}, u32[]{:S(2)}) collective-permute-start(bf16[128,512]{1,0:T(8,128)(2,1)S(1)} %add_convert_fusion.1.refs_0_), channel_id=1, source_target_pairs={{0,8},{8,0},{1,9},{9,1},{2,10},{10,2},{3,11},{11,3},{4,12},{12,4},... | collective-permute-start | bytes 393224 | tf_op jit(solution)/shard_map/ppermute | solution.py:202
  99.9 3.7 %collective-permute-start.20 = (bf16[128,512]{1,0:T(8,128)(2,1)S(1)}, bf16[128,512]{1,0:T(8,128)(2,1)S(1)}, u32[]{:S(2)}, u32[]{:S(2)}) collective-permute-start(bf16[128,512]{1,0:T(8,128)(2,1)S(1)} %collective-permute-done.19.refs_6_), channel_id=1, source_target_pairs={{0,8},{8,0},{1,9},{9,1},{2,10},{10,2},{3,11},{11,3},{4,12},{12,4},... | collective-permute-start | bytes 393224 | tf_op jit(solution)/shard_map/ppermute | solution.py:202
  102.6 1.3 collective-permute-start.18
  103.6 1.3 collective-permute-start.16
  106.3 7.1 %collective-permute-start.21 = (bf16[160,512]{1,0:T(8,128)(2,1)S(1)}, bf16[160,512]{1,0:T(8,128)(2,1)S(1)}, u32[]{:S(2)}, u32[]{:S(2)}) collective-permute-start(bf16[160,512]{1,0:T(8,128)(2,1)S(1)} %get-tuple-element.71), channel_id=1, source_target_pairs={{0,64},{64,128},{128,192},{192,0},{1,65},{65,129},{129,193},{193,1... | collective-permute-start | bytes 491528 | tf_op jit(solution)/shard_map/ppermute | solution.py:202
  106.4 8.7 %collective-permute-start.22 = (bf16[160,512]{1,0:T(8,128)(2,1)S(1)}, bf16[160,512]{1,0:T(8,128)(2,1)S(1)}, u32[]{:S(2)}, u32[]{:S(2)}) collective-permute-start(bf16[160,512]{1,0:T(8,128)(2,1)S(1)} %get-tuple-element.72), channel_id=1, source_target_pairs={{0,128},{64,192},{128,0},{192,64},{1,129},{65,193},{129,1},{193,65... | collective-permute-start | bytes 491528 | tf_op jit(solution)/shard_map/ppermute | solution.py:202
  107.4 9.9 %collective-permute-start.23 = (bf16[160,512]{1,0:T(8,128)(2,1)S(1)}, bf16[160,512]{1,0:T(8,128)(2,1)S(1)}, u32[]{:S(2)}, u32[]{:S(2)}) collective-permute-start(bf16[160,512]{1,0:T(8,128)(2,1)S(1)} %get-tuple-element.73), channel_id=1, source_target_pairs={{0,192},{64,0},{128,64},{192,128},{1,193},{65,1},{129,65},{193,129... | collective-permute-start | bytes 491528 | tf_op jit(solution)/shard_map/ppermute | solution.py:202
Sparse Core Ops, SparseCore 0:
  17.2 42.6 all-gather.2
  77.6 45.7 reduce-scatter.1

commit v3 on v2

v3 whole, which is shorter than its diff:
```python
import functools
import math

import jax
import jax.numpy as jnp
from jax import lax
from jax.experimental import pallas as pl
from jax.experimental.pallas import tpu as pltpu
from jax.sharding import Mesh
from jax.sharding import PartitionSpec as P

HD = 128
NEG = -1e30
TINY = 1e-30
FAR = 1 << 20
TILE = 16
F32 = jnp.float32
BF16 = jnp.bfloat16
NT = (((1,), (1,)), ((), ()))
TN = (((0,), (0,)), ((), ()))
SCALE = 1.0 / math.sqrt(HD)
RATE = SCALE * math.log2(math.e)
LIMIT = pltpu.CompilerParams(vmem_limit_bytes=60 * 1024 * 1024)


def climb(own_ref, par_ref, len_ref, slot_ref, lim_ref, off_ref, nodes):
    own = own_ref[0]
    slot_ref[0] = own
    lim_ref[0] = len_ref[own]
    off_ref[0] = 0
    cursor = own
    count = jnp.int32(1)
    total = tiled(len_ref[own])
    for step in range(1, nodes):
        more = cursor > 0
        up = jnp.where(more, par_ref[cursor], 0)
        length = jnp.where(more, len_ref[up], 0)
        slot_ref[step] = up
        lim_ref[step] = length
        off_ref[step] = total
        total = total + tiled(length)
        count = count + more.astype(jnp.int32)
        cursor = up
    return count, total


def tiled(length):
    return (length + (TILE - 1)) // TILE * TILE


def at(start, size):
    return pl.ds(pl.multiple_of(start, TILE), size)


def each_slot(count, nodes, act):
    for slot in range(nodes):
        pl.when(slot < count)(functools.partial(act, slot))


def stack_heads(q_ref, g_ref, qs, gs, length):
    seg = q_ref.shape[0]
    step = tiled(length)
    live = lax.broadcasted_iota(jnp.int32, (seg, HD), 0) < length
    for head in range(q_ref.shape[1] // HD):
        rows, cols = at(head * step, seg), slice(head * HD, (head + 1) * HD)
        qs[rows, :] = q_ref[:, cols]
        gs[rows, :] = jnp.where(live, g_ref[:, cols], jnp.zeros((), BF16))


def query_places(length, heads, width):
    lane = lax.broadcasted_iota(jnp.int32, (1, width), 1)
    step = tiled(length)
    place = lane
    for head in range(1, heads):
        place = jnp.where(lane >= head * step, lane - head * step, place)
    return place


def first_places(first_ref, lim_ref, off_ref, count, seg, nodes):
    first_ref[...] = jnp.full_like(first_ref, FAR)
    place = lax.broadcasted_iota(jnp.int32, (seg, HD), 0)

    def act(slot):
        seen = place if slot == 0 else jnp.zeros_like(place)
        first_ref[at(off_ref[slot], seg), :] = jnp.where(place < lim_ref[slot], seen, FAR)

    each_slot(count, nodes, act)


def masked_scores(keys, q, first, place):
    s = lax.dot_general(keys, q, NT, preferred_element_type=F32)
    seen = jnp.concatenate([first <= place[:, :HD], first <= place[:, HD:]], axis=1)
    return jnp.where(seen, s, NEG)


def value_kernel(own_ref, par_ref, len_ref, q_ref, g_ref, *refs):
    nodes = (len(refs) - 15) // 2
    keys, values = refs[:nodes], refs[nodes : 2 * nodes]
    t_ref, qs, gs, kc, dvc, kp, first_ref, e_scr, p_low, top_scr, m_scr, l_scr, slot_ref, lim_ref, off_ref = refs[2 * nodes :]
    seg = q_ref.shape[0]
    width = qs.shape[0]
    heads = width // seg
    chunk = 2 * seg
    own = own_ref[0]
    length = len_ref[own]
    count, total = climb(own_ref, par_ref, len_ref, slot_ref, lim_ref, off_ref, nodes)
    pairs = (total + chunk - 1) // chunk

    @pl.when(pl.program_id(0) == 0)
    def _():
        first_places(first_ref, lim_ref, off_ref, count, seg, nodes)
        qs[...] = jnp.zeros_like(qs)
        gs[...] = jnp.zeros_like(gs)
        kp[...] = jnp.zeros_like(kp)

    stack_heads(q_ref, g_ref, qs, gs, length)
    for back in range(nodes):
        kc[back] = keys[back][...]

    def pack(slot):
        kp[at(off_ref[slot], seg), :] = kc[own - slot_ref[slot]]

    each_slot(count, nodes, pack)
    dvc[...] = jnp.zeros_like(dvc)
    m_scr[...] = jnp.full_like(m_scr, NEG)
    l_scr[...] = jnp.zeros_like(l_scr)

    def work(chunks):
        span = chunks * chunk
        place = query_places(length, heads, width)

        def score_step(p, carry):
            rows = at(p * chunk, chunk)
            k2, first = kp[rows, :], first_ref[rows, :]
            for c in range(chunks):
                cols = slice(c * chunk, (c + 1) * chunk)
                s = masked_scores(k2, qs[cols, :], first, place[:, cols])
                before = m_scr[:, cols]
                top = jnp.maximum(before, jnp.max(s, axis=0, keepdims=True))
                e = jnp.exp2((s - top) * RATE)
                e_scr[p, :, cols] = e
                kept = l_scr[:, cols] * jnp.exp2((before - top) * RATE)
                l_scr[:, cols] = kept + jnp.sum(e, axis=0, keepdims=True)
                m_scr[:, cols] = top
                top_scr[p, :, cols] = top
            return carry

        lax.fori_loop(0, pairs, score_step, 0)

        def value_step(p, carry):
            for c in range(chunks):
                cols = slice(c * chunk, (c + 1) * chunk)
                rate = jnp.exp2((top_scr[p, :, cols] - m_scr[:, cols]) * RATE) / l_scr[:, cols]
                p_low[:, cols] = (e_scr[p, :, cols] * rate).astype(BF16)
            dv = jnp.dot(p_low[:, :span], gs[:span, :], preferred_element_type=F32)
            kp[at(p * chunk, chunk), :] = dv.astype(BF16)
            return carry

        lax.fori_loop(0, pairs, value_step, 0)

    for chunks in range(1, width // chunk + 1):
        pl.when((heads * tiled(length) + chunk - 1) // chunk == chunks)(
            functools.partial(work, chunks)
        )
    t_ref[0] = m_scr[...] * RATE + jnp.log2(jnp.maximum(l_scr[...], TINY))
    row = lax.broadcasted_iota(jnp.int32, (seg, HD), 0)

    def unpack(slot):
        dv = kp[at(off_ref[slot], seg), :]
        dvc[own - slot_ref[slot]] = jnp.where(row < lim_ref[slot], dv, jnp.zeros((), BF16))

    each_slot(count, nodes, unpack)
    for back in range(nodes):
        values[back][...] = dvc[back]


def score_kernel(own_ref, par_ref, len_ref, q_ref, g_ref, t_ref, *refs):
    nodes = len(refs) - 19
    keys = refs[:nodes]
    v_ref, dq_ref, dk_ref, qs, gs, kc, kp, vp, dkp, first_ref, s_scr, dp_scr, ds_low, t_scr, dqt, turned, slot_ref, lim_ref, off_ref = refs[nodes:]
    seg = q_ref.shape[0]
    width = qs.shape[0]
    heads = width // seg
    chunk = 2 * seg
    own = own_ref[0]
    length = len_ref[own]
    count, total = climb(own_ref, par_ref, len_ref, slot_ref, lim_ref, off_ref, nodes)
    pairs = (total + chunk - 1) // chunk

    @pl.when(pl.program_id(0) == 0)
    def _():
        first_places(first_ref, lim_ref, off_ref, count, seg, nodes)
        qs[...] = jnp.zeros_like(qs)
        gs[...] = jnp.zeros_like(gs)
        kp[...] = jnp.zeros_like(kp)
        vp[...] = jnp.zeros_like(vp)

    stack_heads(q_ref, g_ref, qs, gs, length)
    for back in range(nodes):
        kc[back] = keys[back][...]

    def whole(slot):
        return pl.ds(pl.multiple_of(slot_ref[slot] * seg, seg), seg)

    def pack(slot):
        kp[at(off_ref[slot], seg), :] = kc[own - slot_ref[slot]]
        vp[at(off_ref[slot], seg), :] = v_ref[whole(slot), :]

    each_slot(count, nodes, pack)
    dk_ref[...] = jnp.zeros_like(dk_ref)
    t_scr[...] = jnp.zeros_like(t_scr)
    dqt[...] = jnp.zeros_like(dqt)

    def work(chunks):
        span = chunks * chunk
        place = query_places(length, heads, width)

        def prob_step(p, carry):
            rows = at(p * chunk, chunk)
            k2, v2, first = kp[rows, :], vp[rows, :], first_ref[rows, :]
            for c in range(chunks):
                cols = slice(c * chunk, (c + 1) * chunk)
                s = masked_scores(k2, qs[cols, :], first, place[:, cols])
                prob = jnp.exp2(s * RATE - t_ref[0, :, cols])
                dp = lax.dot_general(v2, gs[cols, :], NT, preferred_element_type=F32)
                s_scr[p, :, cols] = prob
                dp_scr[p, :, cols] = dp
                t_scr[:, cols] = t_scr[:, cols] + jnp.sum(prob * dp, axis=0, keepdims=True)
            return carry

        lax.fori_loop(0, pairs, prob_step, 0)

        def grad_step(p, carry):
            rows = at(p * chunk, chunk)
            k2 = kp[rows, :]
            for c in range(chunks):
                cols = slice(c * chunk, (c + 1) * chunk)
                ds = (s_scr[p, :, cols] * (dp_scr[p, :, cols] - t_scr[:, cols])).astype(BF16)
                ds_low[:, cols] = ds
                dqt[:, cols] = dqt[:, cols] + lax.dot_general(
                    k2, ds, TN, preferred_element_type=F32
                )
            dk = jnp.dot(ds_low[:, :span], qs[:span, :], preferred_element_type=F32) * SCALE
            dkp[rows, :] = dk.astype(BF16)
            return carry

        lax.fori_loop(0, pairs, grad_step, 0)

    for chunks in range(1, width // chunk + 1):
        pl.when((heads * tiled(length) + chunk - 1) // chunk == chunks)(
            functools.partial(work, chunks)
        )
    row = lax.broadcasted_iota(jnp.int32, (seg, HD), 0)

    def unpack(slot):
        dk = dkp[at(off_ref[slot], seg), :]
        dk_ref[whole(slot), :] = jnp.where(row < lim_ref[slot], dk, jnp.zeros((), BF16))

    each_slot(count, nodes, unpack)
    for part in range(heads):
        turned[part * seg : (part + 1) * seg, :] = dqt[:, part * seg : (part + 1) * seg].T * SCALE
    for head in range(heads):
        dq = turned[at(head * tiled(length), seg), :]
        dq_ref[:, head * HD : (head + 1) * HD] = jnp.where(row < length, dq, 0.0).astype(BF16)


def weight_kernel(place_ref, x_ref, *refs):
    trees = x_ref.shape[0]
    values, outs = refs[:trees], refs[trees:]
    rows = outs[0].shape[0]
    nx, ny = trees // 2, len(outs)
    px, pc, py = place_ref[0], place_ref[1], place_ref[2]
    for ahead in range(ny):
        part = lax.rem(py + ahead, ny)
        span = pl.ds(pl.multiple_of(part * rows, rows), rows)
        total = None
        for back in range(nx):
            line = 2 * lax.rem(px + nx - back, nx)
            x2 = jnp.concatenate([x_ref[line + pc, span, :], x_ref[line + 1 - pc, span, :]], axis=1)
            v2 = jnp.concatenate([values[2 * back][...], values[2 * back + 1][...]], axis=0)
            term = jnp.dot(x2, v2, preferred_element_type=F32)
            total = term if total is None else total + term
        outs[ahead][...] = total.astype(BF16)


def shift(block, axis, step):
    n = lax.axis_size(axis)
    return lax.ppermute(block, axis, [(i, (i + step) % n) for i in range(n)])


def after(block, *others):
    return lax.optimization_barrier((block, *others))[0]


def plus(a, b):
    return (a.astype(F32) + b.astype(F32)).astype(BF16)


def on_device(queries, keys, values, out_grad, inputs, parents, lengths):
    ny, nx, nc, nz = (lax.axis_size(axis) for axis in ("y", "x", "core", "leaf"))
    seg, features = inputs.shape[1:]
    kv_width, q_width = keys.shape[2], queries.shape[2]
    heads_kv = kv_width // HD
    per_head = q_width // heads_kv
    width = per_head // HD * seg
    rows = nz * seg
    own = lax.axis_index("leaf").astype(jnp.int32).reshape(1)
    scalars = (own, parents[0], lengths[0])

    value_all = lax.all_gather(values[0], "leaf", axis=0, tiled=True)

    group = nx * nc
    owned = features // (ny * group)
    facing = inputs[0].T.reshape(ny, group, owned, seg).transpose(1, 0, 2, 3)
    facing = facing.reshape(group, ny * owned, seg)

    half = nz // 2
    key_back = [keys[0]] + [None] * (nz - 1)
    for hop in range(1, half + 1):
        held = key_back[hop - 1]
        if hop == 2:
            held = after(held, facing)
        key_back[hop] = shift(held, "leaf", 1)
        if hop == 1:
            turned = lax.all_to_all(after(facing, key_back[1]), ("x", "core"), 0, 0, tiled=True)
        if hop < half:
            key_back[nz - hop] = shift(key_back[(nz - hop + 1) % nz], "leaf", -1)

    spec_q = pl.BlockSpec((seg, per_head), lambda k, *_: (0, k))
    spec_b = pl.BlockSpec((seg, HD), lambda k, *_: (0, k))
    spec_k = pl.BlockSpec((rows, HD), lambda k, *_: (0, k))
    spec_s = pl.BlockSpec((1, 1, width), lambda k, *_: (k, 0, 0))
    stats = jax.ShapeDtypeStruct((heads_kv, 1, width), F32)
    stacked = [pltpu.VMEM((width, HD), BF16), pltpu.VMEM((width, HD), BF16)]
    tall = pltpu.VMEM((nz // 2, 2 * seg, width), F32)
    tree = [pltpu.SMEM((nz,), jnp.int32)] * 3
    packed = pltpu.VMEM((rows, HD), BF16)
    places = pltpu.VMEM((rows, HD), jnp.int32)
    *value_back, row_log = pl.pallas_call(
        value_kernel,
        out_shape=[jax.ShapeDtypeStruct((seg, kv_width), BF16)] * nz + [stats],
        grid_spec=pltpu.PrefetchScalarGridSpec(
            num_scalar_prefetch=3,
            grid=(heads_kv,),
            in_specs=[spec_q, spec_q] + [spec_b] * nz,
            out_specs=[spec_b] * nz + [spec_s],
            scratch_shapes=[
                *stacked,
                pltpu.VMEM((nz, seg, HD), BF16),
                pltpu.VMEM((nz, seg, HD), BF16),
                packed,
                places,
                tall,
                pltpu.VMEM((2 * seg, width), BF16),
                pltpu.VMEM((nz // 2, 1, width), F32),
                pltpu.VMEM((1, width), F32),
                pltpu.VMEM((1, width), F32),
                *tree,
            ],
        ),
        compiler_params=LIMIT,
        cost_estimate=pl.CostEstimate(
            flops=4 * seg * rows * q_width, bytes_accessed=4 * seg * q_width, transcendentals=0
        ),
    )(*scalars, queries[0], out_grad[0], *key_back)

    def score_grads(row_log):
        return pl.pallas_call(
            score_kernel,
            out_shape=(
                jax.ShapeDtypeStruct((seg, q_width), BF16),
                jax.ShapeDtypeStruct((rows, kv_width), BF16),
            ),
            grid_spec=pltpu.PrefetchScalarGridSpec(
                num_scalar_prefetch=3,
                grid=(heads_kv,),
                in_specs=[spec_q, spec_q, spec_s] + [spec_b] * nz + [spec_k],
                out_specs=[spec_q, spec_k],
                scratch_shapes=[
                    *stacked,
                    pltpu.VMEM((nz, seg, HD), BF16),
                    packed,
                    packed,
                    packed,
                    places,
                    tall,
                    tall,
                    pltpu.VMEM((2 * seg, width), BF16),
                    pltpu.VMEM((1, width), F32),
                    pltpu.VMEM((HD, width), F32),
                    pltpu.VMEM((width, HD), F32),
                    *tree,
                ],
            ),
            compiler_params=LIMIT,
            cost_estimate=pl.CostEstimate(
                flops=8 * seg * rows * q_width, bytes_accessed=6 * seg * q_width, transcendentals=0
            ),
        )(*scalars, queries[0], out_grad[0], row_log, *key_back, value_all)

    up, down = value_back[half], value_back[half - 1]
    for hop in range(1, half + 1):
        ready = up
        up = shift(up, "leaf", 1)
        if hop < half:
            down = shift(down, "leaf", -1)
        if hop == 2:
            query_grad, key_part = score_grads(after(row_log, ready))
            up, query_grad, key_part, turned = lax.optimization_barrier(
                (up, query_grad, key_part, turned)
            )
        if hop < half:
            up = plus(up, value_back[half + hop])
            if hop < half - 1:
                down = plus(down, value_back[half - 1 - hop])
    value_grad = (
        up.astype(F32) + down.astype(F32) + value_back[0].astype(F32)
    ).astype(BF16)
    key_grad = lax.psum_scatter(key_part, "leaf", scatter_dimension=0, tiled=True)

    line = [value_grad] + [shift(value_grad, "x", back) for back in range(1, nx)]
    both = [block for mine in line for block in (mine, shift(mine, "core", 1))]
    place = jnp.stack([lax.axis_index(axis).astype(jnp.int32) for axis in ("x", "core", "y")])
    whole = pl.BlockSpec(memory_space=pltpu.VMEM)
    terms = pl.pallas_call(
        weight_kernel,
        out_shape=[jax.ShapeDtypeStruct((owned, kv_width), BF16)] * ny,
        in_specs=[pl.BlockSpec(memory_space=pltpu.SMEM)] + [whole] * (1 + group),
        out_specs=[whole] * ny,
        compiler_params=pltpu.CompilerParams(vmem_limit_bytes=24 * 1024 * 1024),
        cost_estimate=pl.CostEstimate(
            flops=2 * features * seg * kv_width, bytes_accessed=4 * features * seg, transcendentals=0
        ),
    )(place, turned, *both)
    term = terms[0].astype(F32)
    for ahead in range(1, ny):
        term = term + shift(terms[ahead], "y", ahead).astype(F32)
    term = term.astype(BF16).reshape(nz, owned // nz, kv_width)
    term = lax.all_to_all(term, "leaf", 0, 0, tiled=True)
    weight_grad = jnp.sum(term.astype(F32), axis=0)
    return (query_grad[None], key_grad[None], value_grad[None], weight_grad)


def solution(mesh):
    trees, nodes = mesh.devices.shape
    side = math.isqrt(trees // 2)
    fine = Mesh(mesh.devices.reshape(side, side, 2, nodes), ("y", "x", "core", "leaf"))
    batch = ("y", "x", "core")
    rows = P(batch, "leaf", None)
    return jax.shard_map(
        on_device,
        mesh=fine,
        in_specs=(rows, rows, rows, rows, rows, P(batch, None), P(batch, None)),
        out_specs=(rows, rows, rows, P((*batch, "leaf"), None)),
        check_vma=False,
    )
```

time: 142 us -> 136 us (0.958)
  waiting for transfers between devices: 45 us -> 35.1 us
  starting transfers between devices: 40.7 us -> 42.4 us
    ppermute x24, waiting for transfers between devices: 44.3 us -> 34.4 us  [shift(): return lax.ppermute(block, axis, [(i, (i + step) % n) for i in range(n)])]
    ppermute x24, starting transfers between devices: 36.2 us -> 38.1 us  [shift(): return lax.ppermute(block, axis, [(i, (i + step) % n) for i in range(n)])]
    unnamed x27 -> x25, local copies, waits for them, and re-layouts: 2.4 us -> 3.71 us
    pallas_call x2 -> x1, Pallas kernels: 10.4 us -> 9.32 us  [score_grads(): pl.pallas_call(score_kernel, out_shape=(jax.ShapeDtypeStruct((seg, q_widt...]
  transfers between devices with their start and end apart: 27 -> 27, of which waited for: 16 -> 14; matrix products, arithmetic and copies ran while one was open for 2% -> 4% of each run, Pallas kernels for 13% -> 14%
where the time goes in v3:
time: 136 us; the launch traced here: 134 us
  starting transfers between devices  42.4 us (31%)
  waiting for transfers between devices  35.1 us (26%)
  Pallas kernels  18.2 us (13%)
  blocking collectives  16.3 us (12%)
  between operations  14.3 us (11%)
  local copies, waits for them, and re-layouts  4.96 us (4%)
  other arithmetic  2.84 us (2%)
    ppermute x24, starting transfers between devices, shift(): return lax.ppermute(block, axis, [(i, (i + step) % n) for i in range(n)])  38.1 us
    ppermute x24, waiting for transfers between devices, shift(): return lax.ppermute(block, axis, [(i, (i + step) % n) for i in range(n)])  34.4 us
    all_to_all x1, blocking collectives, on_device(): term = lax.all_to_all(term, 'leaf', 0, 0, tiled=True)  16.3 us
    pallas_call x1, Pallas kernels, score_grads(): pl.pallas_call(score_kernel, out_shape=(jax.ShapeDtypeStruct((seg, q_widt...  9.32 us
    pallas_call x1, Pallas kernels, on_device(): pl.pallas_call(value_kernel, out_shape=[jax.ShapeDtypeStruct((seg, kv_wid...  7.52 us
    all_to_all x1, starting transfers between devices, on_device(): lax.all_to_all(after(facing, key_back[1]), ('x', 'core'), 0, 0, tiled=True)  4.25 us
    unnamed x25, local copies, waits for them, and re-layouts  3.71 us
  transfers between devices with their start and end apart: 27, of which 14 were waited for; matrix products, arithmetic and copies ran while one was open for 4% of the time, Pallas kernels for 14%

profile of v3, /device:TPU:8, one launch (start us, length us, event | category | flops | bytes accessed | tf_op | source)
XLA Modules:
  0.0 134.2 jit_solution(18257289248386257807)
XLA Ops:
  7.2 0.0 all-gather.3.cloned.1.call-start
  7.2 0.7 all-gather.3.cloned.1.call-update
  7.9 2.0 %collective-permute-start = (bf16[128,512]{1,0:T(8,128)(2,1)}, bf16[128,512]{1,0:T(8,128)(2,1)S(1)}, u32[]{:S(2)}, u32[]{:S(2)}) collective-permute-start(bf16[128,512]{1,0:T(8,128)(2,1)} %bitcast.28), channel_id=1, source_target_pairs={{0,1},{1,2},{2,3},{3,4},{4,5},{5,6},{6,7},{7,0},{8,9},{9,10},{10,1... | collective-permute-start | bytes 393224 | tf_op jit(solution)/shard_map/ppermute | solution.py:288
  9.9 4.0 %collective-permute-start.4 = (bf16[128,512]{1,0:T(8,128)(2,1)}, bf16[128,512]{1,0:T(8,128)(2,1)S(1)}, u32[]{:S(2)}, u32[]{:S(2)}) collective-permute-start(bf16[128,512]{1,0:T(8,128)(2,1)} %bitcast.29), channel_id=1, source_target_pairs={{0,7},{1,0},{2,1},{3,2},{4,3},{5,4},{6,5},{7,6},{8,15},{9,8},{10,9... | collective-permute-start | bytes 393224 | tf_op jit(solution)/shard_map/ppermute | solution.py:288
  13.9 1.8 %copy.12 = bf16[1,128,5120]{1,2,0:T(8,128)(2,1)S(1)} copy(bf16[1,128,5120]{2,1,0:T(8,128)(2,1)} %param.11) | data formatting | bytes 2621440 | tf_op args[4]
  15.7 1.2 copy.13
  16.9 0.6 collective-permute-done.refs_1_
  17.5 0.0 collective-permute-start.1
  17.5 0.0 collective-permute-done.4.refs_7_
  17.6 3.2 %collective-permute-start.5 = (bf16[128,512]{1,0:T(8,128)(2,1)S(1)}, bf16[128,512]{1,0:T(8,128)(2,1)S(1)}, u32[]{:S(2)}, u32[]{:S(2)}) collective-permute-start(bf16[128,512]{1,0:T(8,128)(2,1)S(1)} %collective-permute-done.4.refs_7_), channel_id=1, source_target_pairs={{0,7},{1,0},{2,1},{3,2},{4,3},{5,4},{6,5},{7,6},{8,15},{9,8},{10,9... | collective-permute-start | bytes 393224 | tf_op jit(solution)/shard_map/ppermute | solution.py:288
  20.8 2.9 %collective-permute-done.1.refs_2_ = bf16[128,512]{1,0:T(8,128)(2,1)S(1)} collective-permute-done((bf16[128,512]{1,0:T(8,128)(2,1)S(1)}, bf16[128,512]{1,0:T(8,128)(2,1)S(1)}, u32[]{:S(2)}, u32[]{:S(2)}) %collective-permute-start.1) | collective-permute-done | bytes 131104 | tf_op jit(solution)/shard_map/ppermute | solution.py:288
  23.7 0.0 collective-permute-start.2
  23.7 0.0 collective-permute-done.5.refs_6_
  23.7 3.2 %collective-permute-start.6 = (bf16[128,512]{1,0:T(8,128)(2,1)S(1)}, bf16[128,512]{1,0:T(8,128)(2,1)S(1)}, u32[]{:S(2)}, u32[]{:S(2)}) collective-permute-start(bf16[128,512]{1,0:T(8,128)(2,1)S(1)} %collective-permute-done.5.refs_6_), channel_id=1, source_target_pairs={{0,7},{1,0},{2,1},{3,2},{4,3},{5,4},{6,5},{7,6},{8,15},{9,8},{10,9... | collective-permute-start | bytes 393224 | tf_op jit(solution)/shard_map/ppermute | solution.py:288
  27.0 3.4 %collective-permute-done.2.refs_3_ = bf16[128,512]{1,0:T(8,128)(2,1)S(1)} collective-permute-done((bf16[128,512]{1,0:T(8,128)(2,1)S(1)}, bf16[128,512]{1,0:T(8,128)(2,1)S(1)}, u32[]{:S(2)}, u32[]{:S(2)}) %collective-permute-start.2) | collective-permute-done | bytes 131104 | tf_op jit(solution)/shard_map/ppermute | solution.py:288
  30.4 0.6 copy-done.9
  31.0 4.3 %all-to-all-start = ((bf16[8,640,128]{2,1,0:T(8,128)(2,1)}), bf16[8,640,128]{2,1,0:T(8,128)(2,1)S(1)}, u32[]{:S(2)}, u32[]{:S(2)}) async-start(bf16[8,640,128]{2,1,0:T(8,128)(2,1)} %bitcast.10), calls=%async_computation | async-start | bytes 2621440 | tf_op jit(solution)/shard_map/all_to_all | solution.py:325
  35.3 0.0 reduce-scatter.2.cloned.1.call-start
  35.3 0.0 collective-permute-done.6.refs_5_
  35.3 2.3 %collective-permute-done.3.refs_4_ = bf16[128,512]{1,0:T(8,128)(2,1)S(1)} collective-permute-done((bf16[128,512]{1,0:T(8,128)(2,1)S(1)}, bf16[128,512]{1,0:T(8,128)(2,1)S(1)}, u32[]{:S(2)}, u32[]{:S(2)}) %collective-permute-start.3) | collective-permute-done | bytes 131104 | tf_op jit(solution)/shard_map/ppermute | solution.py:288
  37.6 0.6 copy-done.11
  38.3 7.5 %shard_map.102 = (bf16[128,512]{1,0:T(8,128)(2,1)}, bf16[128,512]{1,0:T(8,128)(2,1)}, bf16[128,512]{1,0:T(8,128)(2,1)}, bf16[128,512]{1,0:T(8,128)(2,1)}, bf16[1...) custom-call(s32[1]{0:T(128)} %bitcast.own_ref, ...), custom_call_target="tpu_custom_call" | custom-call | flops 2147483648 | bytes 2097152 | tf_op jit(solution)/shard_map/pallas_call | solution.py:339
  45.8 0.1 collective-permute-start.7
  45.9 3.2 %collective-permute-start.11 = (bf16[128,512]{1,0:T(8,128)(2,1)}, bf16[128,512]{1,0:T(8,128)(2,1)S(1)}, u32[]{:S(2)}, u32[]{:S(2)}) collective-permute-start(bf16[128,512]{1,0:T(8,128)(2,1)} %get-tuple-element.39), channel_id=1, source_target_pairs={{0,7},{1,0},{2,1},{3,2},{4,3},{5,4},{6,5},{7,6},{8,15},{9,8},{10,9... | collective-permute-start | bytes 393224 | tf_op jit(solution)/shard_map/ppermute | solution.py:288
  49.1 3.3 %collective-permute-done.7 = bf16[128,512]{1,0:T(8,128)(2,1)S(1)} collective-permute-done((bf16[128,512]{1,0:T(8,128)(2,1)}, bf16[128,512]{1,0:T(8,128)(2,1)S(1)}, u32[]{:S(2)}, u32[]{:S(2)}) %collective-permute-start.7) | collective-permute-done | bytes 131104 | tf_op jit(solution)/shard_map/ppermute | solution.py:288
  52.4 0.9 add_convert_fusion.6
  53.4 0.1 collective-permute-start.8
  53.5 0.9 add_convert_fusion.3
  54.4 3.5 %collective-permute-start.12 = (bf16[128,512]{1,0:T(8,128)(2,1)S(1)}, bf16[128,512]{1,0:T(8,128)(2,1)S(1)}, u32[]{:S(2)}, u32[]{:S(2)}) collective-permute-start(bf16[128,512]{1,0:T(8,128)(2,1)S(1)} %add_convert_fusion.3), channel_id=1, source_target_pairs={{0,7},{1,0},{2,1},{3,2},{4,3},{5,4},{6,5},{7,6},{8,15},{9,8},{10,9... | collective-permute-start | bytes 393224 | tf_op jit(solution)/shard_map/ppermute | solution.py:288
  57.9 9.3 %shard_map.103 = (bf16[128,4096]{1,0:T(8,128)(2,1)}, bf16[1024,512]{1,0:T(8,128)(2,1)}) custom-call(s32[1]{0:T(128)} %bitcast.own_ref, s32[8]{0:T(128)} %bitcast.34, s32[8]{0:T(128)} %bitcast.36, bf16[128,4096]{1,0:T(8,128)(2,1)} %bitcast.24, bf16[128,4096]{1,0:T(8,128)(2,1)} %bitcast.26, f32[4,1,1024]{2,1,0:T(1,128)} %get-tuple-element.30.t_ref, ...), custom_call_target="tpu_custom_call" | custom-call | flops 4294967296 | bytes 3145728 | tf_op jit(solution)/shard_map/pallas_call | solution.py:368
  67.3 0.0 all-to-all-done.x_ref
  67.3 0.0 reduce-scatter.2.cloned.1.call-update
  67.4 0.1 collective-permute-start.9
  67.5 0.7 copy-done.2
  68.2 2.8 %collective-permute-start.13 = (bf16[128,512]{1,0:T(8,128)(2,1)S(1)}, bf16[128,512]{1,0:T(8,128)(2,1)S(1)}, u32[]{:S(2)}, u32[]{:S(2)}) collective-permute-start(bf16[128,512]{1,0:T(8,128)(2,1)S(1)} %add_convert_fusion.2), channel_id=1, source_target_pairs={{0,7},{1,0},{2,1},{3,2},{4,3},{5,4},{6,5},{7,6},{8,15},{9,8},{10,9... | collective-permute-start | bytes 393224 | tf_op jit(solution)/shard_map/ppermute | solution.py:288
  71.0 3.0 %collective-permute-done.9 = bf16[128,512]{1,0:T(8,128)(2,1)S(1)} collective-permute-done((bf16[128,512]{1,0:T(8,128)(2,1)S(1)}, bf16[128,512]{1,0:T(8,128)(2,1)S(1)}, u32[]{:S(2)}, u32[]{:S(2)}) %collective-permute-start.9) | collective-permute-done | bytes 131104 | tf_op jit(solution)/shard_map/ppermute | solution.py:288
  74.0 0.7 collective-permute-start.10
  74.7 0.4 collective-permute-done.13
  75.2 5.1 %collective-permute-done.10 = bf16[128,512]{1,0:T(8,128)(2,1)S(1)} collective-permute-done((bf16[128,512]{1,0:T(8,128)(2,1)S(1)}, bf16[128,512]{1,0:T(8,128)(2,1)S(1)}, u32[]{:S(2)}, u32[]{:S(2)}) %collective-permute-start.10) | collective-permute-done | bytes 131104 | tf_op jit(solution)/shard_map/ppermute | solution.py:288
  80.3 0.1 add_convert_fusion.1.refs_0_
  80.3 0.0 copy-start
  80.3 2.5 %collective-permute-start.19 = (bf16[128,512]{1,0:T(8,128)(2,1)S(1)}, bf16[128,512]{1,0:T(8,128)(2,1)S(1)}, u32[]{:S(2)}, u32[]{:S(2)}) collective-permute-start(bf16[128,512]{1,0:T(8,128)(2,1)S(1)} %add_convert_fusion.1.refs_0_), channel_id=1, source_target_pairs={{0,48},{16,0},{32,16},{48,32},{1,49},{17,1},{33,17},{49,33},{2,50}... | collective-permute-start | bytes 393224 | tf_op jit(solution)/shard_map/ppermute | solution.py:288
  82.9 6.5 %collective-permute-start.17 = (bf16[128,512]{1,0:T(8,128)(2,1)S(1)}, bf16[128,512]{1,0:T(8,128)(2,1)S(1)}, u32[]{:S(2)}, u32[]{:S(2)}) collective-permute-start(bf16[128,512]{1,0:T(8,128)(2,1)S(1)} %add_convert_fusion.1.refs_0_), channel_id=1, source_target_pairs={{0,32},{16,48},{32,0},{48,16},{1,33},{17,49},{33,1},{49,17},{2,34}... | collective-permute-start | bytes 393224 | tf_op jit(solution)/shard_map/ppermute | solution.py:288
  89.3 1.3 collective-permute-start.15
  90.7 0.0 collective-permute-start.14
  90.7 0.0 collective-permute-done.19.refs_6_
  90.7 0.5 collective-permute-start.20
  91.2 1.1 collective-permute-done.17.refs_4_
  92.3 0.0 collective-permute-start.18
  92.3 3.2 %collective-permute-done.15.refs_2_ = bf16[128,512]{1,0:T(8,128)(2,1)S(1)} collective-permute-done((bf16[128,512]{1,0:T(8,128)(2,1)S(1)}, bf16[128,512]{1,0:T(8,128)(2,1)S(1)}, u32[]{:S(2)}, u32[]{:S(2)}) %collective-permute-start.15) | collective-permute-done | bytes 131104 | tf_op jit(solution)/shard_map/ppermute | solution.py:288
  95.5 0.1 pad_add_fusion.place_ref
  95.6 0.0 collective-permute-done.14.refs_1_
  95.6 0.0 collective-permute-done.20.refs_7_
  95.6 0.0 collective-permute-done.18.refs_5_
  95.6 1.3 collective-permute-done.16.refs_3_
  96.9 1.4 %shard_map.104 = (bf16[160,512]{1,0:T(8,128)(2,1)S(1)}, bf16[160,512]{1,0:T(8,128)(2,1)S(1)}, bf16[160,512]{1,0:T(8,128)(2,1)S(1)}, bf16[160,512]{1,0:T(8,128)(2,1)S(1)}) custom-call(s32[3]{0:T(128)S(1)} %pad_add_fusion.place_ref, bf16[8,640,128]{2,1,0:T(8,128)(2,1)S(1)} %all-to-all-done.x_ref, bf16[128,512]{1,0:T(8,128)(2,1)S(1)} %add_convert_fusion.1.refs_0_, ...), custom_call_target="tpu_custom_call" | custom-call | flops 671088640 | bytes 2621440 | tf_op jit(solution)/shard_map/pallas_call | solution.py:425
  98.3 0.1 collective-permute-start.21
  98.4 4.1 %collective-permute-start.22 = (bf16[160,512]{1,0:T(8,128)(2,1)S(1)}, bf16[160,512]{1,0:T(8,128)(2,1)S(1)}, u32[]{:S(2)}, u32[]{:S(2)}) collective-permute-start(bf16[160,512]{1,0:T(8,128)(2,1)S(1)} %get-tuple-element.46), channel_id=1, source_target_pairs={{0,128},{64,192},{128,0},{192,64},{1,129},{65,193},{129,1},{193,65... | collective-permute-start | bytes 491528 | tf_op jit(solution)/shard_map/ppermute | solution.py:288
  102.5 2.9 %collective-permute-done.21 = bf16[160,512]{1,0:T(8,128)(2,1)S(1)} collective-permute-done((bf16[160,512]{1,0:T(8,128)(2,1)S(1)}, bf16[160,512]{1,0:T(8,128)(2,1)S(1)}, u32[]{:S(2)}, u32[]{:S(2)}) %collective-permute-start.21) | collective-permute-done | bytes 163872 | tf_op jit(solution)/shard_map/ppermute | solution.py:288
  105.4 2.1 %collective-permute-done.22 = bf16[160,512]{1,0:T(8,128)(2,1)S(1)} collective-permute-done((bf16[160,512]{1,0:T(8,128)(2,1)S(1)}, bf16[160,512]{1,0:T(8,128)(2,1)S(1)}, u32[]{:S(2)}, u32[]{:S(2)}) %collective-permute-start.22) | collective-permute-done | bytes 163872 | tf_op jit(solution)/shard_map/ppermute | solution.py:288
  107.5 2.7 %collective-permute-done.23 = bf16[160,512]{1,0:T(8,128)(2,1)S(1)} collective-permute-done((bf16[160,512]{1,0:T(8,128)(2,1)S(1)}, bf16[160,512]{1,0:T(8,128)(2,1)S(1)}, u32[]{:S(2)}, u32[]{:S(2)}) %collective-permute-start.23) | collective-permute-done | bytes 163872 | tf_op jit(solution)/shard_map/ppermute | solution.py:288
  110.2 0.1 add_convert_fusion
  110.4 16.3 %all_to_all.10 = bf16[8,20,512]{2,1,0:T(8,128)(2,1)S(1)} all-to-all(bf16[8,20,512]{2,1,0:T(8,128)(2,1)S(1)} %reshape.23), channel_id=1, replica_groups=mesh['y'=4,'x'=4,'core'=2,'leaf'=8] {'leaf'}, dimensions={0} | all-to-all | bytes 327680 | tf_op jit(solution)/shard_map/all_to_all | solution.py:439
  126.7 0.7 convert_reduce_fusion
  (32 shorter events, 0.2 us)
Async XLA Ops:
  7.2 50.7 %all-gather.3.cloned.1.call-start = ((), (), s32[]{:S(2)}) async-start(), calls=%async_computation.4 | async-start | bytes 1179648 | tf_op jit(solution)/shard_map/all_gather | solution.py:310
  7.9 9.6 %collective-permute-start = (bf16[128,512]{1,0:T(8,128)(2,1)}, bf16[128,512]{1,0:T(8,128)(2,1)S(1)}, u32[]{:S(2)}, u32[]{:S(2)}) collective-permute-start(bf16[128,512]{1,0:T(8,128)(2,1)} %bitcast.28), channel_id=1, source_target_pairs={{0,1},{1,2},{2,3},{3,4},{4,5},{5,6},{6,7},{7,0},{8,9},{9,10},{10,1... | collective-permute-start | bytes 393224 | tf_op jit(solution)/shard_map/ppermute | solution.py:288
  9.9 7.7 %collective-permute-start.4 = (bf16[128,512]{1,0:T(8,128)(2,1)}, bf16[128,512]{1,0:T(8,128)(2,1)S(1)}, u32[]{:S(2)}, u32[]{:S(2)}) collective-permute-start(bf16[128,512]{1,0:T(8,128)(2,1)} %bitcast.29), channel_id=1, source_target_pairs={{0,7},{1,0},{2,1},{3,2},{4,3},{5,4},{6,5},{7,6},{8,15},{9,8},{10,9... | collective-permute-start | bytes 393224 | tf_op jit(solution)/shard_map/ppermute | solution.py:288
  17.5 12.8 %copy-start.5 = (bf16[128,512]{1,0:T(8,128)(2,1)}, bf16[128,512]{1,0:T(8,128)(2,1)S(1)}, u32[]{:S(2)}) copy-start(bf16[128,512]{1,0:T(8,128)(2,1)S(1)} %collective-permute-done.refs_1_) | copy-start | bytes 393220
  17.5 6.2 %collective-permute-start.1 = (bf16[128,512]{1,0:T(8,128)(2,1)S(1)}, bf16[128,512]{1,0:T(8,128)(2,1)S(1)}, u32[]{:S(2)}, u32[]{:S(2)}) collective-permute-start(bf16[128,512]{1,0:T(8,128)(2,1)S(1)} %collective-permute-done.refs_1_), channel_id=1, source_target_pairs={{0,1},{1,2},{2,3},{3,4},{4,5},{5,6},{6,7},{7,0},{8,9},{9,10},{10,1... | collective-permute-start | bytes 393224 | tf_op jit(solution)/shard_map/ppermute | solution.py:288
  17.6 12.8 %copy-start.6 = (bf16[128,512]{1,0:T(8,128)(2,1)}, bf16[128,512]{1,0:T(8,128)(2,1)S(1)}, u32[]{:S(2)}) copy-start(bf16[128,512]{1,0:T(8,128)(2,1)S(1)} %collective-permute-done.4.refs_7_) | copy-start | bytes 393220
  17.6 6.2 %collective-permute-start.5 = (bf16[128,512]{1,0:T(8,128)(2,1)S(1)}, bf16[128,512]{1,0:T(8,128)(2,1)S(1)}, u32[]{:S(2)}, u32[]{:S(2)}) collective-permute-start(bf16[128,512]{1,0:T(8,128)(2,1)S(1)} %collective-permute-done.4.refs_7_), channel_id=1, source_target_pairs={{0,7},{1,0},{2,1},{3,2},{4,3},{5,4},{6,5},{7,6},{8,15},{9,8},{10,9... | collective-permute-start | bytes 393224 | tf_op jit(solution)/shard_map/ppermute | solution.py:288
  23.7 6.7 %copy-start.7 = (bf16[128,512]{1,0:T(8,128)(2,1)}, bf16[128,512]{1,0:T(8,128)(2,1)S(1)}, u32[]{:S(2)}) copy-start(bf16[128,512]{1,0:T(8,128)(2,1)S(1)} %collective-permute-done.1.refs_2_) | copy-start | bytes 393220
  23.7 6.6 %collective-permute-start.2 = (bf16[128,512]{1,0:T(8,128)(2,1)S(1)}, bf16[128,512]{1,0:T(8,128)(2,1)S(1)}, u32[]{:S(2)}, u32[]{:S(2)}) collective-permute-start(bf16[128,512]{1,0:T(8,128)(2,1)S(1)} %collective-permute-done.1.refs_2_), channel_id=1, source_target_pairs={{0,1},{1,2},{2,3},{3,4},{4,5},{5,6},{6,7},{7,0},{8,9},{9,10},{10,1... | collective-permute-start | bytes 393224 | tf_op jit(solution)/shard_map/ppermute | solution.py:288
  23.7 6.7 %copy-start.8 = (bf16[128,512]{1,0:T(8,128)(2,1)}, bf16[128,512]{1,0:T(8,128)(2,1)S(1)}, u32[]{:S(2)}) copy-start(bf16[128,512]{1,0:T(8,128)(2,1)S(1)} %collective-permute-done.5.refs_6_) | copy-start | bytes 393220
  23.7 11.6 %collective-permute-start.6 = (bf16[128,512]{1,0:T(8,128)(2,1)S(1)}, bf16[128,512]{1,0:T(8,128)(2,1)S(1)}, u32[]{:S(2)}, u32[]{:S(2)}) collective-permute-start(bf16[128,512]{1,0:T(8,128)(2,1)S(1)} %collective-permute-done.5.refs_6_), channel_id=1, source_target_pairs={{0,7},{1,0},{2,1},{3,2},{4,3},{5,4},{6,5},{7,6},{8,15},{9,8},{10,9... | collective-permute-start | bytes 393224 | tf_op jit(solution)/shard_map/ppermute | solution.py:288
  30.4 0.6 copy-start.9
  30.4 7.3 %collective-permute-start.3 = (bf16[128,512]{1,0:T(8,128)(2,1)S(1)}, bf16[128,512]{1,0:T(8,128)(2,1)S(1)}, u32[]{:S(2)}, u32[]{:S(2)}) collective-permute-start(bf16[128,512]{1,0:T(8,128)(2,1)S(1)} %collective-permute-done.2.refs_3_), channel_id=1, source_target_pairs={{0,1},{1,2},{2,3},{3,4},{4,5},{5,6},{6,7},{7,0},{8,9},{9,10},{10,1... | collective-permute-start | bytes 393224 | tf_op jit(solution)/shard_map/ppermute | solution.py:288
  31.0 36.3 %all-to-all-start = ((bf16[8,640,128]{2,1,0:T(8,128)(2,1)}), bf16[8,640,128]{2,1,0:T(8,128)(2,1)S(1)}, u32[]{:S(2)}, u32[]{:S(2)}) async-start(bf16[8,640,128]{2,1,0:T(8,128)(2,1)} %bitcast.10), calls=%async_computation | async-start | bytes 2621440 | tf_op jit(solution)/shard_map/all_to_all | solution.py:325
  35.3 92.1 %reduce-scatter.2.cloned.1.call-start = ((), (), s32[]{:S(2)}) async-start(), calls=%async_computation.3 | async-start | bytes 1179648 | tf_op jit(solution)/shard_map/reduce_scatter | solution.py:419
  35.3 2.3 %copy-start.10 = (bf16[128,512]{1,0:T(8,128)(2,1)}, bf16[128,512]{1,0:T(8,128)(2,1)S(1)}, u32[]{:S(2)}) copy-start(bf16[128,512]{1,0:T(8,128)(2,1)S(1)} %collective-permute-done.6.refs_5_) | copy-start | bytes 393220
  37.6 0.6 copy-start.11
  45.8 6.6 %collective-permute-start.7 = (bf16[128,512]{1,0:T(8,128)(2,1)}, bf16[128,512]{1,0:T(8,128)(2,1)S(1)}, u32[]{:S(2)}, u32[]{:S(2)}) collective-permute-start(bf16[128,512]{1,0:T(8,128)(2,1)} %get-tuple-element.27), channel_id=1, source_target_pairs={{0,1},{1,2},{2,3},{3,4},{4,5},{5,6},{6,7},{7,0},{8,9},{9,10},{10,1... | collective-permute-start | bytes 393224 | tf_op jit(solution)/shard_map/ppermute | solution.py:288
  45.9 7.6 %collective-permute-start.11 = (bf16[128,512]{1,0:T(8,128)(2,1)}, bf16[128,512]{1,0:T(8,128)(2,1)S(1)}, u32[]{:S(2)}, u32[]{:S(2)}) collective-permute-start(bf16[128,512]{1,0:T(8,128)(2,1)} %get-tuple-element.39), channel_id=1, source_target_pairs={{0,7},{1,0},{2,1},{3,2},{4,3},{5,4},{6,5},{7,6},{8,15},{9,8},{10,9... | collective-permute-start | bytes 393224 | tf_op jit(solution)/shard_map/ppermute | solution.py:288
  53.4 13.9 %collective-permute-start.8 = (bf16[128,512]{1,0:T(8,128)(2,1)S(1)}, bf16[128,512]{1,0:T(8,128)(2,1)S(1)}, u32[]{:S(2)}, u32[]{:S(2)}) collective-permute-start(bf16[128,512]{1,0:T(8,128)(2,1)S(1)} %add_convert_fusion.6), channel_id=1, source_target_pairs={{0,1},{1,2},{2,3},{3,4},{4,5},{5,6},{6,7},{7,0},{8,9},{9,10},{10,1... | collective-permute-start | bytes 393224 | tf_op jit(solution)/shard_map/ppermute | solution.py:288
  54.4 13.0 %collective-permute-start.12 = (bf16[128,512]{1,0:T(8,128)(2,1)S(1)}, bf16[128,512]{1,0:T(8,128)(2,1)S(1)}, u32[]{:S(2)}, u32[]{:S(2)}) collective-permute-start(bf16[128,512]{1,0:T(8,128)(2,1)S(1)} %add_convert_fusion.3), channel_id=1, source_target_pairs={{0,7},{1,0},{2,1},{3,2},{4,3},{5,4},{6,5},{7,6},{8,15},{9,8},{10,9... | collective-permute-start | bytes 393224 | tf_op jit(solution)/shard_map/ppermute | solution.py:288
  57.9 9.4 %copy-start.3 = (bf16[128,512]{1,0:T(8,128)(2,1)S(1)}, bf16[128,512]{1,0:T(8,128)(2,1)}, u32[]{:S(2)}) copy-start(bf16[128,512]{1,0:T(8,128)(2,1)} %get-tuple-element.37) | copy-start | bytes 393220
  67.2 0.9 copy-start.2
  67.2 6.7 %copy-start.1 = (bf16[128,512]{1,0:T(8,128)(2,1)S(1)}, bf16[128,512]{1,0:T(8,128)(2,1)}, u32[]{:S(2)}) copy-start(bf16[128,512]{1,0:T(8,128)(2,1)} %get-tuple-element.38) | copy-start | bytes 393220
  67.3 13.0 %copy-start.4 = (bf16[128,512]{1,0:T(8,128)(2,1)S(1)}, bf16[128,512]{1,0:T(8,128)(2,1)}, u32[]{:S(2)}) copy-start(bf16[128,512]{1,0:T(8,128)(2,1)} %get-tuple-element.42) | copy-start | bytes 393220
  67.4 6.6 %collective-permute-start.9 = (bf16[128,512]{1,0:T(8,128)(2,1)S(1)}, bf16[128,512]{1,0:T(8,128)(2,1)S(1)}, u32[]{:S(2)}, u32[]{:S(2)}) collective-permute-start(bf16[128,512]{1,0:T(8,128)(2,1)S(1)} %add_convert_fusion.5), channel_id=1, source_target_pairs={{0,1},{1,2},{2,3},{3,4},{4,5},{5,6},{6,7},{7,0},{8,9},{9,10},{10,1... | collective-permute-start | bytes 393224 | tf_op jit(solution)/shard_map/ppermute | solution.py:288
  68.2 7.0 %collective-permute-start.13 = (bf16[128,512]{1,0:T(8,128)(2,1)S(1)}, bf16[128,512]{1,0:T(8,128)(2,1)S(1)}, u32[]{:S(2)}, u32[]{:S(2)}) collective-permute-start(bf16[128,512]{1,0:T(8,128)(2,1)S(1)} %add_convert_fusion.2), channel_id=1, source_target_pairs={{0,7},{1,0},{2,1},{3,2},{4,3},{5,4},{6,5},{7,6},{8,15},{9,8},{10,9... | collective-permute-start | bytes 393224 | tf_op jit(solution)/shard_map/ppermute | solution.py:288
  74.0 6.3 %collective-permute-start.10 = (bf16[128,512]{1,0:T(8,128)(2,1)S(1)}, bf16[128,512]{1,0:T(8,128)(2,1)S(1)}, u32[]{:S(2)}, u32[]{:S(2)}) collective-permute-start(bf16[128,512]{1,0:T(8,128)(2,1)S(1)} %add_convert_fusion.4), channel_id=1, source_target_pairs={{0,1},{1,2},{2,3},{3,4},{4,5},{5,6},{6,7},{7,0},{8,9},{9,10},{10,1... | collective-permute-start | bytes 393224 | tf_op jit(solution)/shard_map/ppermute | solution.py:288
  80.3 30.0 %copy-start = (bf16[128,512]{1,0:T(8,128)(2,1)}, bf16[128,512]{1,0:T(8,128)(2,1)S(1)}, u32[]{:S(2)}) copy-start(bf16[128,512]{1,0:T(8,128)(2,1)S(1)} %add_convert_fusion.1.refs_0_) | copy-start | bytes 393220
  80.3 10.3 %collective-permute-start.19 = (bf16[128,512]{1,0:T(8,128)(2,1)S(1)}, bf16[128,512]{1,0:T(8,128)(2,1)S(1)}, u32[]{:S(2)}, u32[]{:S(2)}) collective-permute-start(bf16[128,512]{1,0:T(8,128)(2,1)S(1)} %add_convert_fusion.1.refs_0_), channel_id=1, source_target_pairs={{0,48},{16,0},{32,16},{48,32},{1,49},{17,1},{33,17},{49,33},{2,50}... | collective-permute-start | bytes 393224 | tf_op jit(solution)/shard_map/ppermute | solution.py:288
  82.9 9.4 %collective-permute-start.17 = (bf16[128,512]{1,0:T(8,128)(2,1)S(1)}, bf16[128,512]{1,0:T(8,128)(2,1)S(1)}, u32[]{:S(2)}, u32[]{:S(2)}) collective-permute-start(bf16[128,512]{1,0:T(8,128)(2,1)S(1)} %add_convert_fusion.1.refs_0_), channel_id=1, source_target_pairs={{0,32},{16,48},{32,0},{48,16},{1,33},{17,49},{33,1},{49,17},{2,34}... | collective-permute-start | bytes 393224 | tf_op jit(solution)/shard_map/ppermute | solution.py:288
  89.3 6.2 %collective-permute-start.15 = (bf16[128,512]{1,0:T(8,128)(2,1)S(1)}, bf16[128,512]{1,0:T(8,128)(2,1)S(1)}, u32[]{:S(2)}, u32[]{:S(2)}) collective-permute-start(bf16[128,512]{1,0:T(8,128)(2,1)S(1)} %add_convert_fusion.1.refs_0_), channel_id=1, source_target_pairs={{0,16},{16,32},{32,48},{48,0},{1,17},{17,33},{33,49},{49,1},{2,18}... | collective-permute-start | bytes 393224 | tf_op jit(solution)/shard_map/ppermute | solution.py:288
  90.7 4.9 %collective-permute-start.14 = (bf16[128,512]{1,0:T(8,128)(2,1)S(1)}, bf16[128,512]{1,0:T(8,128)(2,1)S(1)}, u32[]{:S(2)}, u32[]{:S(2)}) collective-permute-start(bf16[128,512]{1,0:T(8,128)(2,1)S(1)} %add_convert_fusion.1.refs_0_), channel_id=1, source_target_pairs={{0,8},{8,0},{1,9},{9,1},{2,10},{10,2},{3,11},{11,3},{4,12},{12,4},... | collective-permute-start | bytes 393224 | tf_op jit(solution)/shard_map/ppermute | solution.py:288
  90.7 4.9 %collective-permute-start.20 = (bf16[128,512]{1,0:T(8,128)(2,1)S(1)}, bf16[128,512]{1,0:T(8,128)(2,1)S(1)}, u32[]{:S(2)}, u32[]{:S(2)}) collective-permute-start(bf16[128,512]{1,0:T(8,128)(2,1)S(1)} %collective-permute-done.19.refs_6_), channel_id=1, source_target_pairs={{0,8},{8,0},{1,9},{9,1},{2,10},{10,2},{3,11},{11,3},{4,12},{12,4},... | collective-permute-start | bytes 393224 | tf_op jit(solution)/shard_map/ppermute | solution.py:288
  92.3 3.3 %collective-permute-start.18 = (bf16[128,512]{1,0:T(8,128)(2,1)S(1)}, bf16[128,512]{1,0:T(8,128)(2,1)S(1)}, u32[]{:S(2)}, u32[]{:S(2)}) collective-permute-start(bf16[128,512]{1,0:T(8,128)(2,1)S(1)} %collective-permute-done.17.refs_4_), channel_id=1, source_target_pairs={{0,8},{8,0},{1,9},{9,1},{2,10},{10,2},{3,11},{11,3},{4,12},{12,4},... | collective-permute-start | bytes 393224 | tf_op jit(solution)/shard_map/ppermute | solution.py:288
  95.5 1.3 %collective-permute-start.16 = (bf16[128,512]{1,0:T(8,128)(2,1)S(1)}, bf16[128,512]{1,0:T(8,128)(2,1)S(1)}, u32[]{:S(2)}, u32[]{:S(2)}) collective-permute-start(bf16[128,512]{1,0:T(8,128)(2,1)S(1)} %collective-permute-done.15.refs_2_), channel_id=1, source_target_pairs={{0,8},{8,0},{1,9},{9,1},{2,10},{10,2},{3,11},{11,3},{4,12},{12,4},... | collective-permute-start | bytes 393224 | tf_op jit(solution)/shard_map/ppermute | solution.py:288
  98.3 7.1 %collective-permute-start.21 = (bf16[160,512]{1,0:T(8,128)(2,1)S(1)}, bf16[160,512]{1,0:T(8,128)(2,1)S(1)}, u32[]{:S(2)}, u32[]{:S(2)}) collective-permute-start(bf16[160,512]{1,0:T(8,128)(2,1)S(1)} %get-tuple-element.45), channel_id=1, source_target_pairs={{0,64},{64,128},{128,192},{192,0},{1,65},{65,129},{129,193},{193,1... | collective-permute-start | bytes 491528 | tf_op jit(solution)/shard_map/ppermute | solution.py:288
  98.4 9.2 %collective-permute-start.22 = (bf16[160,512]{1,0:T(8,128)(2,1)S(1)}, bf16[160,512]{1,0:T(8,128)(2,1)S(1)}, u32[]{:S(2)}, u32[]{:S(2)}) collective-permute-start(bf16[160,512]{1,0:T(8,128)(2,1)S(1)} %get-tuple-element.46), channel_id=1, source_target_pairs={{0,128},{64,192},{128,0},{192,64},{1,129},{65,193},{129,1},{193,65... | collective-permute-start | bytes 491528 | tf_op jit(solution)/shard_map/ppermute | solution.py:288
  102.5 7.7 %collective-permute-start.23 = (bf16[160,512]{1,0:T(8,128)(2,1)S(1)}, bf16[160,512]{1,0:T(8,128)(2,1)S(1)}, u32[]{:S(2)}, u32[]{:S(2)}) collective-permute-start(bf16[160,512]{1,0:T(8,128)(2,1)S(1)} %get-tuple-element.47), channel_id=1, source_target_pairs={{0,192},{64,0},{128,64},{192,128},{1,193},{65,1},{129,65},{193,129... | collective-permute-start | bytes 491528 | tf_op jit(solution)/shard_map/ppermute | solution.py:288
Sparse Core Ops, SparseCore 0:
  9.8 42.2 all-gather.2
  67.4 45.4 reduce-scatter.1

commit v4 on v3

--- a/solution.py
+++ b/solution.py
@@ -23,25 +23,28 @@
 LIMIT = pltpu.CompilerParams(vmem_limit_bytes=60 * 1024 * 1024)
 
 
-def climb(own_ref, par_ref, len_ref, slot_ref, lim_ref, off_ref, nodes):
+def climb(own_ref, par_ref, len_ref, lim_ref, off_ref, nodes):
     own = own_ref[0]
-    slot_ref[0] = own
+    for back in range(nodes):
+        lim_ref[back] = 0
+        off_ref[back] = 0
     lim_ref[0] = len_ref[own]
-    off_ref[0] = 0
+    total = tiled(len_ref[own])
     cursor = own
-    count = jnp.int32(1)
-    total = tiled(len_ref[own])
-    for step in range(1, nodes):
+    for _ in range(1, nodes):
         more = cursor > 0
         up = jnp.where(more, par_ref[cursor], 0)
-        length = jnp.where(more, len_ref[up], 0)
-        slot_ref[step] = up
-        lim_ref[step] = length
-        off_ref[step] = total
-        total = total + tiled(length)
-        count = count + more.astype(jnp.int32)
+        length = len_ref[up]
+        back = own - up
+
+        @pl.when(more)
+        def _(back=back, length=length, total=total):
+            lim_ref[back] = length
+            off_ref[back] = total
+
+        total = total + jnp.where(more, tiled(length), 0)
         cursor = up
-    return count, total
+    return total
 
 
 def tiled(length):
@@ -52,9 +55,9 @@
     return pl.ds(pl.multiple_of(start, TILE), size)
 
 
-def each_slot(count, nodes, act):
-    for slot in range(nodes):
-        pl.when(slot < count)(functools.partial(act, slot))
+def each_member(lim_ref, nodes, act):
+    for back in range(nodes):
+        pl.when(lim_ref[back] > 0)(functools.partial(act, back))
 
 
 def stack_heads(q_ref, g_ref, qs, gs, length):
@@ -76,15 +79,15 @@
     return place
 
 
-def first_places(first_ref, lim_ref, off_ref, count, seg, nodes):
+def first_places(first_ref, lim_ref, off_ref, seg, nodes):
     first_ref[...] = jnp.full_like(first_ref, FAR)
     place = lax.broadcasted_iota(jnp.int32, (seg, HD), 0)
 
-    def act(slot):
-        seen = place if slot == 0 else jnp.zeros_like(place)
-        first_ref[at(off_ref[slot], seg), :] = jnp.where(place < lim_ref[slot], seen, FAR)
-
-    each_slot(count, nodes, act)
+    def act(back):
+        seen = place if back == 0 else jnp.zeros_like(place)
+        first_ref[at(off_ref[back], seg), :] = jnp.where(place < lim_ref[back], seen, FAR)
+
+    each_member(lim_ref, nodes, act)
 
 
 def masked_scores(keys, q, first, place):
@@ -94,34 +97,31 @@
 
 
 def value_kernel(own_ref, par_ref, len_ref, q_ref, g_ref, *refs):
-    nodes = (len(refs) - 15) // 2
+    nodes = (len(refs) - 12) // 2
     keys, values = refs[:nodes], refs[nodes : 2 * nodes]
-    t_ref, qs, gs, kc, dvc, kp, first_ref, e_scr, p_low, top_scr, m_scr, l_scr, slot_ref, lim_ref, off_ref = refs[2 * nodes :]
+    t_ref, qs, gs, kp, first_ref, e_scr, p_low, top_scr, m_scr, l_scr, lim_ref, off_ref = refs[2 * nodes :]
     seg = q_ref.shape[0]
     width = qs.shape[0]
     heads = width // seg
     chunk = 2 * seg
     own = own_ref[0]
     length = len_ref[own]
-    count, total = climb(own_ref, par_ref, len_ref, slot_ref, lim_ref, off_ref, nodes)
+    total = climb(own_ref, par_ref, len_ref, lim_ref, off_ref, nodes)
     pairs = (total + chunk - 1) // chunk
 
     @pl.when(pl.program_id(0) == 0)
     def _():
-        first_places(first_ref, lim_ref, off_ref, count, seg, nodes)
+        first_places(first_ref, lim_ref, off_ref, seg, nodes)
         qs[...] = jnp.zeros_like(qs)
         gs[...] = jnp.zeros_like(gs)
         kp[...] = jnp.zeros_like(kp)
 
     stack_heads(q_ref, g_ref, qs, gs, length)
-    for back in range(nodes):
-        kc[back] = keys[back][...]
-
-    def pack(slot):
-        kp[at(off_ref[slot], seg), :] = kc[own - slot_ref[slot]]
-
-    each_slot(count, nodes, pack)
-    dvc[...] = jnp.zeros_like(dvc)
+
+    def pack(back):
+        kp[at(off_ref[back], seg), :] = keys[back][...]
+
+    each_member(lim_ref, nodes, pack)
     m_scr[...] = jnp.full_like(m_scr, NEG)
     l_scr[...] = jnp.zeros_like(l_scr)
 
@@ -165,48 +165,43 @@
     t_ref[0] = m_scr[...] * RATE + jnp.log2(jnp.maximum(l_scr[...], TINY))
     row = lax.broadcasted_iota(jnp.int32, (seg, HD), 0)
 
-    def unpack(slot):
-        dv = kp[at(off_ref[slot], seg), :]
-        dvc[own - slot_ref[slot]] = jnp.where(row < lim_ref[slot], dv, jnp.zeros((), BF16))
-
-    each_slot(count, nodes, unpack)
     for back in range(nodes):
-        values[back][...] = dvc[back]
-
-
-def score_kernel(own_ref, par_ref, len_ref, q_ref, g_ref, t_ref, *refs):
-    nodes = len(refs) - 19
+        dv = kp[at(off_ref[back], seg), :]
+        values[back][...] = jnp.where(row < lim_ref[back], dv, jnp.zeros((), BF16))
+
+
+def score_kernel(kept, own_ref, par_ref, len_ref, q_ref, g_ref, t_ref, *refs):
+    nodes = len(refs) - 17 - kept
     keys = refs[:nodes]
-    v_ref, dq_ref, dk_ref, qs, gs, kc, kp, vp, dkp, first_ref, s_scr, dp_scr, ds_low, t_scr, dqt, turned, slot_ref, lim_ref, off_ref = refs[nodes:]
+    v_ref = refs[nodes]
+    dq_ref, dk_ref, qs, gs, kp, vp, dkp, first_ref, s_scr, dp_scr, ds_low, t_scr, dqt, turned, lim_ref, off_ref = refs[nodes + 1 + kept :]
     seg = q_ref.shape[0]
     width = qs.shape[0]
     heads = width // seg
     chunk = 2 * seg
     own = own_ref[0]
     length = len_ref[own]
-    count, total = climb(own_ref, par_ref, len_ref, slot_ref, lim_ref, off_ref, nodes)
+    total = climb(own_ref, par_ref, len_ref, lim_ref, off_ref, nodes)
     pairs = (total + chunk - 1) // chunk
 
     @pl.when(pl.program_id(0) == 0)
     def _():
-        first_places(first_ref, lim_ref, off_ref, count, seg, nodes)
+        first_places(first_ref, lim_ref, off_ref, seg, nodes)
         qs[...] = jnp.zeros_like(qs)
         gs[...] = jnp.zeros_like(gs)
         kp[...] = jnp.zeros_like(kp)
         vp[...] = jnp.zeros_like(vp)
 
     stack_heads(q_ref, g_ref, qs, gs, length)
-    for back in range(nodes):
-        kc[back] = keys[back][...]
-
-    def whole(slot):
-        return pl.ds(pl.multiple_of(slot_ref[slot] * seg, seg), seg)
-
-    def pack(slot):
-        kp[at(off_ref[slot], seg), :] = kc[own - slot_ref[slot]]
-        vp[at(off_ref[slot], seg), :] = v_ref[whole(slot), :]
-
-    each_slot(count, nodes, pack)
+
+    def whole(back):
+        return pl.ds(pl.multiple_of((own - back) * seg, seg), seg)
+
+    def pack(back):
+        kp[at(off_ref[back], seg), :] = keys[back][...]
+        vp[at(off_ref[back], seg), :] = v_ref[whole(back), :]
+
+    each_member(lim_ref, nodes, pack)
     dk_ref[...] = jnp.zeros_like(dk_ref)
     t_scr[...] = jnp.zeros_like(t_scr)
     dqt[...] = jnp.zeros_like(dqt)
@@ -252,11 +247,11 @@
         )
     row = lax.broadcasted_iota(jnp.int32, (seg, HD), 0)
 
-    def unpack(slot):
-        dk = dkp[at(off_ref[slot], seg), :]
-        dk_ref[whole(slot), :] = jnp.where(row < lim_ref[slot], dk, jnp.zeros((), BF16))
-
-    each_slot(count, nodes, unpack)
+    def unpack(back):
+        dk = dkp[at(off_ref[back], seg), :]
+        dk_ref[whole(back), :] = jnp.where(row < lim_ref[back], dk, jnp.zeros((), BF16))
+
+    each_member(lim_ref, nodes, unpack)
     for part in range(heads):
         turned[part * seg : (part + 1) * seg, :] = dqt[:, part * seg : (part + 1) * seg].T * SCALE
     for head in range(heads):
@@ -333,7 +328,7 @@
     stats = jax.ShapeDtypeStruct((heads_kv, 1, width), F32)
     stacked = [pltpu.VMEM((width, HD), BF16), pltpu.VMEM((width, HD), BF16)]
     tall = pltpu.VMEM((nz // 2, 2 * seg, width), F32)
-    tree = [pltpu.SMEM((nz,), jnp.int32)] * 3
+    tree = [pltpu.SMEM((nz,), jnp.int32)] * 2
     packed = pltpu.VMEM((rows, HD), BF16)
     places = pltpu.VMEM((rows, HD), jnp.int32)
     *value_back, row_log = pl.pallas_call(
@@ -346,8 +341,6 @@
             out_specs=[spec_b] * nz + [spec_s],
             scratch_shapes=[
                 *stacked,
-                pltpu.VMEM((nz, seg, HD), BF16),
-                pltpu.VMEM((nz, seg, HD), BF16),
                 packed,
                 places,
                 tall,
@@ -364,21 +357,25 @@
         ),
     )(*scalars, queries[0], out_grad[0], *key_back)
 
-    def score_grads(row_log):
+    def score_grads(first, heads, row_log, kept):
+        def moved(spec):
+            return pl.BlockSpec(spec.block_shape, lambda k, *_: spec.index_map(k + first))
+
+        given = [moved(spec) for spec in [spec_q, spec_q, spec_s] + [spec_b] * nz + [spec_k]]
+        count = len(scalars) + len(given)
         return pl.pallas_call(
-            score_kernel,
+            functools.partial(score_kernel, len(kept)),
             out_shape=(
                 jax.ShapeDtypeStruct((seg, q_width), BF16),
                 jax.ShapeDtypeStruct((rows, kv_width), BF16),
             ),
             grid_spec=pltpu.PrefetchScalarGridSpec(
                 num_scalar_prefetch=3,
-                grid=(heads_kv,),
-                in_specs=[spec_q, spec_q, spec_s] + [spec_b] * nz + [spec_k],
-                out_specs=[spec_q, spec_k],
+                grid=(heads,),
+                in_specs=given + [pl.BlockSpec(memory_space=pl.ANY)] * len(kept),
+                out_specs=[moved(spec_q), moved(spec_k)],
                 scratch_shapes=[
                     *stacked,
-                    pltpu.VMEM((nz, seg, HD), BF16),
                     packed,
                     packed,
                     packed,
@@ -392,27 +389,29 @@
                     *tree,
                 ],
             ),
+            input_output_aliases={count + i: i for i in range(len(kept))},
             compiler_params=LIMIT,
             cost_estimate=pl.CostEstimate(
                 flops=8 * seg * rows * q_width, bytes_accessed=6 * seg * q_width, transcendentals=0
             ),
-        )(*scalars, queries[0], out_grad[0], row_log, *key_back, value_all)
+        )(*scalars, queries[0], out_grad[0], row_log, *key_back, value_all, *kept)
 
     up, down = value_back[half], value_back[half - 1]
+    grads = ()
     for hop in range(1, half + 1):
         ready = up
         up = shift(up, "leaf", 1)
         if hop < half:
             down = shift(down, "leaf", -1)
-        if hop == 2:
-            query_grad, key_part = score_grads(after(row_log, ready))
-            up, query_grad, key_part, turned = lax.optimization_barrier(
-                (up, query_grad, key_part, turned)
-            )
+        if hop in (2, 3):
+            part = heads_kv // 2
+            grads = score_grads((hop - 2) * part, part, after(row_log, ready), grads)
+            up, turned, *grads = lax.optimization_barrier((up, turned, *grads))
         if hop < half:
             up = plus(up, value_back[half + hop])
             if hop < half - 1:
                 down = plus(down, value_back[half - 1 - hop])
+    query_grad, key_part = grads
     value_grad = (
         up.astype(F32) + down.astype(F32) + value_back[0].astype(F32)
     ).astype(BF16)

time: 136 us -> 134 us (0.985); the launches traced: 134 us -> 134 us
  starting transfers between devices: 42.4 us -> 38.8 us
  Pallas kernels: 18.2 us -> 21.2 us
    ppermute x24, starting transfers between devices: 38.1 us -> 34.5 us  [shift(): return lax.ppermute(block, axis, [(i, (i + step) % n) for i in range(n)])]
    pallas_call x1 -> x2, Pallas kernels: 9.32 us -> 12.3 us  [score_grads(): pl.pallas_call(functools.partial(score_kernel, len(kept)), out_shape=(jax...]
  transfers between devices with their start and end apart: 27 -> 27, of which waited for: 14 -> 16; matrix products, arithmetic and copies ran while one was open for 4% -> 4% of each run, Pallas kernels for 14% -> 16%
where the time goes in v4:
time: 134 us
  starting transfers between devices  38.8 us (29%)
  waiting for transfers between devices  35.1 us (26%)
  Pallas kernels  21.2 us (16%)
  blocking collectives  17.4 us (13%)
  between operations  14.3 us (11%)
  local copies, waits for them, and re-layouts  4.32 us (3%)
  other arithmetic  2.85 us (2%)
    ppermute x24, starting transfers between devices, shift(): return lax.ppermute(block, axis, [(i, (i + step) % n) for i in range(n)])  34.5 us
    ppermute x24, waiting for transfers between devices, shift(): return lax.ppermute(block, axis, [(i, (i + step) % n) for i in range(n)])  34.4 us
    all_to_all x1, blocking collectives, on_device(): term = lax.all_to_all(term, 'leaf', 0, 0, tiled=True)  17.4 us
    pallas_call x2, Pallas kernels, score_grads(): pl.pallas_call(functools.partial(score_kernel, len(kept)), out_shape=(jax...  12.3 us
    pallas_call x1, Pallas kernels, on_device(): pl.pallas_call(value_kernel, out_shape=[jax.ShapeDtypeStruct((seg, kv_wid...  7.56 us
    all_to_all x1, starting transfers between devices, on_device(): lax.all_to_all(after(facing, key_back[1]), ('x', 'core'), 0, 0, tiled=True)  4.25 us
    unnamed x25, local copies, waits for them, and re-layouts  3.06 us
  transfers between devices with their start and end apart: 27, of which 16 were waited for; matrix products, arithmetic and copies ran while one was open for 4% of the time, Pallas kernels for 16%

profile of v4, /device:TPU:8, one launch (start us, length us, event | category | flops | bytes accessed | tf_op | source)
XLA Modules:
  0.0 134.0 jit_solution(4467644077043838861)
XLA Ops:
  7.2 0.0 all-gather.3.cloned.1.call-start
  7.2 0.7 all-gather.3.cloned.1.call-update
  7.9 2.0 %collective-permute-start = (bf16[128,512]{1,0:T(8,128)(2,1)}, bf16[128,512]{1,0:T(8,128)(2,1)S(1)}, u32[]{:S(2)}, u32[]{:S(2)}) collective-permute-start(bf16[128,512]{1,0:T(8,128)(2,1)} %bitcast.31), channel_id=1, source_target_pairs={{0,1},{1,2},{2,3},{3,4},{4,5},{5,6},{6,7},{7,0},{8,9},{9,10},{10,1... | collective-permute-start | bytes 393224 | tf_op jit(solution)/shard_map/ppermute | solution.py:283
  9.9 4.0 %collective-permute-start.4 = (bf16[128,512]{1,0:T(8,128)(2,1)}, bf16[128,512]{1,0:T(8,128)(2,1)S(1)}, u32[]{:S(2)}, u32[]{:S(2)}) collective-permute-start(bf16[128,512]{1,0:T(8,128)(2,1)} %bitcast.32), channel_id=1, source_target_pairs={{0,7},{1,0},{2,1},{3,2},{4,3},{5,4},{6,5},{7,6},{8,15},{9,8},{10,9... | collective-permute-start | bytes 393224 | tf_op jit(solution)/shard_map/ppermute | solution.py:283
  13.9 1.8 %copy.14 = bf16[1,128,5120]{1,2,0:T(8,128)(2,1)S(1)} copy(bf16[1,128,5120]{2,1,0:T(8,128)(2,1)} %param.11) | data formatting | bytes 2621440 | tf_op args[4]
  15.7 1.2 copy.15
  16.9 0.6 collective-permute-done.refs_1_
  17.5 0.0 collective-permute-start.1
  17.5 0.0 collective-permute-done.4.refs_7_
  17.6 3.2 %collective-permute-start.5 = (bf16[128,512]{1,0:T(8,128)(2,1)S(1)}, bf16[128,512]{1,0:T(8,128)(2,1)S(1)}, u32[]{:S(2)}, u32[]{:S(2)}) collective-permute-start(bf16[128,512]{1,0:T(8,128)(2,1)S(1)} %collective-permute-done.4.refs_7_), channel_id=1, source_target_pairs={{0,7},{1,0},{2,1},{3,2},{4,3},{5,4},{6,5},{7,6},{8,15},{9,8},{10,9... | collective-permute-start | bytes 393224 | tf_op jit(solution)/shard_map/ppermute | solution.py:283
  20.8 2.9 %collective-permute-done.1.refs_2_ = bf16[128,512]{1,0:T(8,128)(2,1)S(1)} collective-permute-done((bf16[128,512]{1,0:T(8,128)(2,1)S(1)}, bf16[128,512]{1,0:T(8,128)(2,1)S(1)}, u32[]{:S(2)}, u32[]{:S(2)}) %collective-permute-start.1) | collective-permute-done | bytes 131104 | tf_op jit(solution)/shard_map/ppermute | solution.py:283
  23.7 0.0 collective-permute-start.2
  23.7 3.2 %collective-permute-start.6 = (bf16[128,512]{1,0:T(8,128)(2,1)S(1)}, bf16[128,512]{1,0:T(8,128)(2,1)S(1)}, u32[]{:S(2)}, u32[]{:S(2)}) collective-permute-start(bf16[128,512]{1,0:T(8,128)(2,1)S(1)} %collective-permute-done.5.refs_6_), channel_id=1, source_target_pairs={{0,7},{1,0},{2,1},{3,2},{4,3},{5,4},{6,5},{7,6},{8,15},{9,8},{10,9... | collective-permute-start | bytes 393224 | tf_op jit(solution)/shard_map/ppermute | solution.py:283
  27.0 3.4 %collective-permute-done.2.refs_3_ = bf16[128,512]{1,0:T(8,128)(2,1)S(1)} collective-permute-done((bf16[128,512]{1,0:T(8,128)(2,1)S(1)}, bf16[128,512]{1,0:T(8,128)(2,1)S(1)}, u32[]{:S(2)}, u32[]{:S(2)}) %collective-permute-start.2) | collective-permute-done | bytes 131104 | tf_op jit(solution)/shard_map/ppermute | solution.py:283
  30.4 0.6 copy-done.9
  31.0 4.3 %all-to-all-start = ((bf16[8,640,128]{2,1,0:T(8,128)(2,1)}), bf16[8,640,128]{2,1,0:T(8,128)(2,1)S(1)}, u32[]{:S(2)}, u32[]{:S(2)}) async-start(bf16[8,640,128]{2,1,0:T(8,128)(2,1)} %bitcast.10), calls=%async_computation | async-start | bytes 2621440 | tf_op jit(solution)/shard_map/all_to_all | solution.py:320
  35.3 0.0 reduce-scatter.2.cloned.1.call-start
  35.3 2.3 %collective-permute-done.3.refs_4_ = bf16[128,512]{1,0:T(8,128)(2,1)S(1)} collective-permute-done((bf16[128,512]{1,0:T(8,128)(2,1)S(1)}, bf16[128,512]{1,0:T(8,128)(2,1)S(1)}, u32[]{:S(2)}, u32[]{:S(2)}) %collective-permute-start.3) | collective-permute-done | bytes 131104 | tf_op jit(solution)/shard_map/ppermute | solution.py:283
  37.6 0.6 copy-done.11
  38.3 7.6 %shard_map.102 = (bf16[128,512]{1,0:T(8,128)(2,1)}, bf16[128,512]{1,0:T(8,128)(2,1)}, bf16[128,512]{1,0:T(8,128)(2,1)}, bf16[128,512]{1,0:T(8,128)(2,1)}, bf16[1...) custom-call(s32[1]{0:T(128)} %bitcast.own_ref, ...), custom_call_target="tpu_custom_call" | custom-call | flops 2147483648 | bytes 2097152 | tf_op jit(solution)/shard_map/pallas_call | solution.py:334
  45.8 0.1 collective-permute-start.7
  45.9 3.2 %collective-permute-start.11 = (bf16[128,512]{1,0:T(8,128)(2,1)}, bf16[128,512]{1,0:T(8,128)(2,1)S(1)}, u32[]{:S(2)}, u32[]{:S(2)}) collective-permute-start(bf16[128,512]{1,0:T(8,128)(2,1)} %get-tuple-element.53), channel_id=1, source_target_pairs={{0,7},{1,0},{2,1},{3,2},{4,3},{5,4},{6,5},{7,6},{8,15},{9,8},{10,9... | collective-permute-start | bytes 393224 | tf_op jit(solution)/shard_map/ppermute | solution.py:283
  49.2 4.0 %collective-permute-done.7 = bf16[128,512]{1,0:T(8,128)(2,1)S(1)} collective-permute-done((bf16[128,512]{1,0:T(8,128)(2,1)}, bf16[128,512]{1,0:T(8,128)(2,1)S(1)}, u32[]{:S(2)}, u32[]{:S(2)}) %collective-permute-start.7) | collective-permute-done | bytes 131104 | tf_op jit(solution)/shard_map/ppermute | solution.py:283
  53.2 0.9 add_convert_fusion.6
  54.1 0.1 collective-permute-start.8
  54.2 0.0 collective-permute-done.11
  54.2 0.9 add_convert_fusion.3
  55.2 3.5 %collective-permute-start.12 = (bf16[128,512]{1,0:T(8,128)(2,1)S(1)}, bf16[128,512]{1,0:T(8,128)(2,1)S(1)}, u32[]{:S(2)}, u32[]{:S(2)}) collective-permute-start(bf16[128,512]{1,0:T(8,128)(2,1)S(1)} %add_convert_fusion.3), channel_id=1, source_target_pairs={{0,7},{1,0},{2,1},{3,2},{4,3},{5,4},{6,5},{7,6},{8,15},{9,8},{10,9... | collective-permute-start | bytes 393224 | tf_op jit(solution)/shard_map/ppermute | solution.py:283
  58.6 6.2 %shard_map.103 = (bf16[128,4096]{1,0:T(8,128)(2,1)}, bf16[1024,512]{1,0:T(8,128)(2,1)}) custom-call(s32[1]{0:T(128)} %bitcast.own_ref, s32[8]{0:T(128)} %bitcast.38, s32[8]{0:T(128)} %bitcast.41, bf16[128,4096]{1,0:T(8,128)(2,1)} %bitcast.24, bf16[128,4096]{1,0:T(8,128)(2,1)} %bitcast.27, f32[4,1,1024]{2,1,0:T(1,128)} %get-tuple-element.44.t_ref, ...), custom_call_target="tpu_custom_call" | custom-call | flops 4294967296 | bytes 3145728 | tf_op jit(solution)/shard_map/pallas_call | solution.py:366
  64.9 0.1 collective-permute-start.9
  65.0 6.1 %shard_map.104 = (bf16[128,4096]{1,0:T(8,128)(2,1)}, bf16[1024,512]{1,0:T(8,128)(2,1)}) custom-call(s32[1]{0:T(128)} %bitcast.own_ref, s32[8]{0:T(128)} %bitcast.39, s32[8]{0:T(128)} %bitcast.42, bf16[128,4096]{1,0:T(8,128)(2,1)} %bitcast.25, bf16[128,4096]{1,0:T(8,128)(2,1)} %bitcast.28, ...), custom_call_target="tpu_custom_call", output_to_operand_aliasing={{0}: (15, {}), {1}: (16, {})} | custom-call | flops 4294967296 | bytes 3145728 | tf_op jit(solution)/shard_map/pallas_call | solution.py:366
  71.1 0.1 collective-permute-done.9
  71.2 0.0 reduce-scatter.2.cloned.1.call-update
  71.3 2.4 %collective-permute-start.13 = (bf16[128,512]{1,0:T(8,128)(2,1)S(1)}, bf16[128,512]{1,0:T(8,128)(2,1)S(1)}, u32[]{:S(2)}, u32[]{:S(2)}) collective-permute-start(bf16[128,512]{1,0:T(8,128)(2,1)S(1)} %add_convert_fusion.2), channel_id=1, source_target_pairs={{0,7},{1,0},{2,1},{3,2},{4,3},{5,4},{6,5},{7,6},{8,15},{9,8},{10,9... | collective-permute-start | bytes 393224 | tf_op jit(solution)/shard_map/ppermute | solution.py:283
  73.8 1.3 collective-permute-start.10
  75.1 2.3 %collective-permute-done.13 = bf16[128,512]{1,0:T(8,128)(2,1)S(1)} collective-permute-done((bf16[128,512]{1,0:T(8,128)(2,1)S(1)}, bf16[128,512]{1,0:T(8,128)(2,1)S(1)}, u32[]{:S(2)}, u32[]{:S(2)}) %collective-permute-start.13) | collective-permute-done | bytes 131104 | tf_op jit(solution)/shard_map/ppermute | solution.py:283
  77.3 3.5 %collective-permute-done.10 = bf16[128,512]{1,0:T(8,128)(2,1)S(1)} collective-permute-done((bf16[128,512]{1,0:T(8,128)(2,1)S(1)}, bf16[128,512]{1,0:T(8,128)(2,1)S(1)}, u32[]{:S(2)}, u32[]{:S(2)}) %collective-permute-start.10) | collective-permute-done | bytes 131104 | tf_op jit(solution)/shard_map/ppermute | solution.py:283
  80.9 0.1 add_convert_fusion.1.refs_0_
  80.9 0.0 copy-start
  81.0 4.6 %collective-permute-start.19 = (bf16[128,512]{1,0:T(8,128)(2,1)S(1)}, bf16[128,512]{1,0:T(8,128)(2,1)S(1)}, u32[]{:S(2)}, u32[]{:S(2)}) collective-permute-start(bf16[128,512]{1,0:T(8,128)(2,1)S(1)} %add_convert_fusion.1.refs_0_), channel_id=1, source_target_pairs={{0,48},{16,0},{32,16},{48,32},{1,49},{17,1},{33,17},{49,33},{2,50}... | collective-permute-start | bytes 393224 | tf_op jit(solution)/shard_map/ppermute | solution.py:283
  85.5 0.0 collective-permute-start.17
  85.5 1.0 collective-permute-start.15
  86.5 0.0 collective-permute-start.14
  86.5 3.0 %collective-permute-done.19.refs_6_ = bf16[128,512]{1,0:T(8,128)(2,1)S(1)} collective-permute-done((bf16[128,512]{1,0:T(8,128)(2,1)S(1)}, bf16[128,512]{1,0:T(8,128)(2,1)S(1)}, u32[]{:S(2)}, u32[]{:S(2)}) %collective-permute-start.19) | collective-permute-done | bytes 131104 | tf_op jit(solution)/shard_map/ppermute | solution.py:283
  89.4 0.0 collective-permute-start.20
  89.4 2.6 %collective-permute-done.17.refs_4_ = bf16[128,512]{1,0:T(8,128)(2,1)S(1)} collective-permute-done((bf16[128,512]{1,0:T(8,128)(2,1)S(1)}, bf16[128,512]{1,0:T(8,128)(2,1)S(1)}, u32[]{:S(2)}, u32[]{:S(2)}) %collective-permute-start.17) | collective-permute-done | bytes 131104 | tf_op jit(solution)/shard_map/ppermute | solution.py:283
  92.1 0.0 collective-permute-start.18
  92.1 1.0 collective-permute-done.15.refs_2_
  93.1 0.0 collective-permute-start.16
  93.1 0.1 pad_add_fusion.place_ref
  93.2 0.0 collective-permute-done.14.refs_1_
  93.2 0.0 collective-permute-done.20.refs_7_
  93.2 0.3 collective-permute-done.18.refs_5_
  93.4 1.0 collective-permute-done.16.refs_3_
  94.4 1.4 %shard_map.105 = (bf16[160,512]{1,0:T(8,128)(2,1)S(1)}, bf16[160,512]{1,0:T(8,128)(2,1)S(1)}, bf16[160,512]{1,0:T(8,128)(2,1)S(1)}, bf16[160,512]{1,0:T(8,128)(2,1)S(1)}) custom-call(s32[3]{0:T(128)S(1)} %pad_add_fusion.place_ref, bf16[8,640,128]{2,1,0:T(8,128)(2,1)S(1)} %all-to-all-done.x_ref, bf16[128,512]{1,0:T(8,128)(2,1)S(1)} %add_convert_fusion.1.refs_0_, ...), custom_call_target="tpu_custom_call" | custom-call | flops 671088640 | bytes 2621440 | tf_op jit(solution)/shard_map/pallas_call | solution.py:424
  95.8 3.6 %collective-permute-start.21 = (bf16[160,512]{1,0:T(8,128)(2,1)S(1)}, bf16[160,512]{1,0:T(8,128)(2,1)S(1)}, u32[]{:S(2)}, u32[]{:S(2)}) collective-permute-start(bf16[160,512]{1,0:T(8,128)(2,1)S(1)} %get-tuple-element.59), channel_id=1, source_target_pairs={{0,64},{64,128},{128,192},{192,0},{1,65},{65,129},{129,193},{193,1... | collective-permute-start | bytes 491528 | tf_op jit(solution)/shard_map/ppermute | solution.py:283
  99.5 0.0 collective-permute-start.22
  99.5 2.2 %collective-permute-start.23 = (bf16[160,512]{1,0:T(8,128)(2,1)S(1)}, bf16[160,512]{1,0:T(8,128)(2,1)S(1)}, u32[]{:S(2)}, u32[]{:S(2)}) collective-permute-start(bf16[160,512]{1,0:T(8,128)(2,1)S(1)} %get-tuple-element.61), channel_id=1, source_target_pairs={{0,192},{64,0},{128,64},{192,128},{1,193},{65,1},{129,65},{193,129... | collective-permute-start | bytes 491528 | tf_op jit(solution)/shard_map/ppermute | solution.py:283
  101.6 5.1 %collective-permute-done.21 = bf16[160,512]{1,0:T(8,128)(2,1)S(1)} collective-permute-done((bf16[160,512]{1,0:T(8,128)(2,1)S(1)}, bf16[160,512]{1,0:T(8,128)(2,1)S(1)}, u32[]{:S(2)}, u32[]{:S(2)}) %collective-permute-start.21) | collective-permute-done | bytes 163872 | tf_op jit(solution)/shard_map/ppermute | solution.py:283
  106.7 1.3 collective-permute-done.22
  108.0 0.9 collective-permute-done.23
  108.9 0.1 add_convert_fusion
  109.1 17.4 %all_to_all.10 = bf16[8,20,512]{2,1,0:T(8,128)(2,1)S(1)} all-to-all(bf16[8,20,512]{2,1,0:T(8,128)(2,1)S(1)} %reshape.23), channel_id=1, replica_groups=mesh['y'=4,'x'=4,'core'=2,'leaf'=8] {'leaf'}, dimensions={0} | all-to-all | bytes 327680 | tf_op jit(solution)/shard_map/all_to_all | solution.py:438
  126.5 0.7 convert_reduce_fusion
  (33 shorter events, 0.2 us)
Async XLA Ops:
  7.2 51.5 %all-gather.3.cloned.1.call-start = ((), (), s32[]{:S(2)}) async-start(), calls=%async_computation.4 | async-start | bytes 1179648 | tf_op jit(solution)/shard_map/all_gather | solution.py:305
  7.9 9.6 %collective-permute-start = (bf16[128,512]{1,0:T(8,128)(2,1)}, bf16[128,512]{1,0:T(8,128)(2,1)S(1)}, u32[]{:S(2)}, u32[]{:S(2)}) collective-permute-start(bf16[128,512]{1,0:T(8,128)(2,1)} %bitcast.31), channel_id=1, source_target_pairs={{0,1},{1,2},{2,3},{3,4},{4,5},{5,6},{6,7},{7,0},{8,9},{9,10},{10,1... | collective-permute-start | bytes 393224 | tf_op jit(solution)/shard_map/ppermute | solution.py:283
  9.9 7.7 %collective-permute-start.4 = (bf16[128,512]{1,0:T(8,128)(2,1)}, bf16[128,512]{1,0:T(8,128)(2,1)S(1)}, u32[]{:S(2)}, u32[]{:S(2)}) collective-permute-start(bf16[128,512]{1,0:T(8,128)(2,1)} %bitcast.32), channel_id=1, source_target_pairs={{0,7},{1,0},{2,1},{3,2},{4,3},{5,4},{6,5},{7,6},{8,15},{9,8},{10,9... | collective-permute-start | bytes 393224 | tf_op jit(solution)/shard_map/ppermute | solution.py:283
  17.5 12.8 %copy-start.5 = (bf16[128,512]{1,0:T(8,128)(2,1)}, bf16[128,512]{1,0:T(8,128)(2,1)S(1)}, u32[]{:S(2)}) copy-start(bf16[128,512]{1,0:T(8,128)(2,1)S(1)} %collective-permute-done.refs_1_) | copy-start | bytes 393220
  17.5 6.2 %collective-permute-start.1 = (bf16[128,512]{1,0:T(8,128)(2,1)S(1)}, bf16[128,512]{1,0:T(8,128)(2,1)S(1)}, u32[]{:S(2)}, u32[]{:S(2)}) collective-permute-start(bf16[128,512]{1,0:T(8,128)(2,1)S(1)} %collective-permute-done.refs_1_), channel_id=1, source_target_pairs={{0,1},{1,2},{2,3},{3,4},{4,5},{5,6},{6,7},{7,0},{8,9},{9,10},{10,1... | collective-permute-start | bytes 393224 | tf_op jit(solution)/shard_map/ppermute | solution.py:283
  17.6 12.8 %copy-start.6 = (bf16[128,512]{1,0:T(8,128)(2,1)}, bf16[128,512]{1,0:T(8,128)(2,1)S(1)}, u32[]{:S(2)}) copy-start(bf16[128,512]{1,0:T(8,128)(2,1)S(1)} %collective-permute-done.4.refs_7_) | copy-start | bytes 393220
  17.6 6.2 %collective-permute-start.5 = (bf16[128,512]{1,0:T(8,128)(2,1)S(1)}, bf16[128,512]{1,0:T(8,128)(2,1)S(1)}, u32[]{:S(2)}, u32[]{:S(2)}) collective-permute-start(bf16[128,512]{1,0:T(8,128)(2,1)S(1)} %collective-permute-done.4.refs_7_), channel_id=1, source_target_pairs={{0,7},{1,0},{2,1},{3,2},{4,3},{5,4},{6,5},{7,6},{8,15},{9,8},{10,9... | collective-permute-start | bytes 393224 | tf_op jit(solution)/shard_map/ppermute | solution.py:283
  23.7 6.7 %copy-start.7 = (bf16[128,512]{1,0:T(8,128)(2,1)}, bf16[128,512]{1,0:T(8,128)(2,1)S(1)}, u32[]{:S(2)}) copy-start(bf16[128,512]{1,0:T(8,128)(2,1)S(1)} %collective-permute-done.1.refs_2_) | copy-start | bytes 393220
  23.7 6.6 %collective-permute-start.2 = (bf16[128,512]{1,0:T(8,128)(2,1)S(1)}, bf16[128,512]{1,0:T(8,128)(2,1)S(1)}, u32[]{:S(2)}, u32[]{:S(2)}) collective-permute-start(bf16[128,512]{1,0:T(8,128)(2,1)S(1)} %collective-permute-done.1.refs_2_), channel_id=1, source_target_pairs={{0,1},{1,2},{2,3},{3,4},{4,5},{5,6},{6,7},{7,0},{8,9},{9,10},{10,1... | collective-permute-start | bytes 393224 | tf_op jit(solution)/shard_map/ppermute | solution.py:283
  23.7 6.7 %copy-start.8 = (bf16[128,512]{1,0:T(8,128)(2,1)}, bf16[128,512]{1,0:T(8,128)(2,1)S(1)}, u32[]{:S(2)}) copy-start(bf16[128,512]{1,0:T(8,128)(2,1)S(1)} %collective-permute-done.5.refs_6_) | copy-start | bytes 393220
  23.7 11.6 %collective-permute-start.6 = (bf16[128,512]{1,0:T(8,128)(2,1)S(1)}, bf16[128,512]{1,0:T(8,128)(2,1)S(1)}, u32[]{:S(2)}, u32[]{:S(2)}) collective-permute-start(bf16[128,512]{1,0:T(8,128)(2,1)S(1)} %collective-permute-done.5.refs_6_), channel_id=1, source_target_pairs={{0,7},{1,0},{2,1},{3,2},{4,3},{5,4},{6,5},{7,6},{8,15},{9,8},{10,9... | collective-permute-start | bytes 393224 | tf_op jit(solution)/shard_map/ppermute | solution.py:283
  30.4 0.7 copy-start.9
  30.4 7.3 %collective-permute-start.3 = (bf16[128,512]{1,0:T(8,128)(2,1)S(1)}, bf16[128,512]{1,0:T(8,128)(2,1)S(1)}, u32[]{:S(2)}, u32[]{:S(2)}) collective-permute-start(bf16[128,512]{1,0:T(8,128)(2,1)S(1)} %collective-permute-done.2.refs_3_), channel_id=1, source_target_pairs={{0,1},{1,2},{2,3},{3,4},{4,5},{5,6},{6,7},{7,0},{8,9},{9,10},{10,1... | collective-permute-start | bytes 393224 | tf_op jit(solution)/shard_map/ppermute | solution.py:283
  31.0 33.9 %all-to-all-start = ((bf16[8,640,128]{2,1,0:T(8,128)(2,1)}), bf16[8,640,128]{2,1,0:T(8,128)(2,1)S(1)}, u32[]{:S(2)}, u32[]{:S(2)}) async-start(bf16[8,640,128]{2,1,0:T(8,128)(2,1)} %bitcast.10), calls=%async_computation | async-start | bytes 2621440 | tf_op jit(solution)/shard_map/all_to_all | solution.py:320
  35.3 91.9 %reduce-scatter.2.cloned.1.call-start = ((), (), s32[]{:S(2)}) async-start(), calls=%async_computation.3 | async-start | bytes 1179648 | tf_op jit(solution)/shard_map/reduce_scatter | solution.py:418
  35.3 2.3 %copy-start.10 = (bf16[128,512]{1,0:T(8,128)(2,1)}, bf16[128,512]{1,0:T(8,128)(2,1)S(1)}, u32[]{:S(2)}) copy-start(bf16[128,512]{1,0:T(8,128)(2,1)S(1)} %collective-permute-done.6.refs_5_) | copy-start | bytes 393220
  37.6 0.6 copy-start.11
  45.8 7.3 %collective-permute-start.7 = (bf16[128,512]{1,0:T(8,128)(2,1)}, bf16[128,512]{1,0:T(8,128)(2,1)S(1)}, u32[]{:S(2)}, u32[]{:S(2)}) collective-permute-start(bf16[128,512]{1,0:T(8,128)(2,1)} %get-tuple-element.34), channel_id=1, source_target_pairs={{0,1},{1,2},{2,3},{3,4},{4,5},{5,6},{6,7},{7,0},{8,9},{9,10},{10,1... | collective-permute-start | bytes 393224 | tf_op jit(solution)/shard_map/ppermute | solution.py:283
  45.9 8.3 %collective-permute-start.11 = (bf16[128,512]{1,0:T(8,128)(2,1)}, bf16[128,512]{1,0:T(8,128)(2,1)S(1)}, u32[]{:S(2)}, u32[]{:S(2)}) collective-permute-start(bf16[128,512]{1,0:T(8,128)(2,1)} %get-tuple-element.53), channel_id=1, source_target_pairs={{0,7},{1,0},{2,1},{3,2},{4,3},{5,4},{6,5},{7,6},{8,15},{9,8},{10,9... | collective-permute-start | bytes 393224 | tf_op jit(solution)/shard_map/ppermute | solution.py:283
  54.1 10.7 %collective-permute-start.8 = (bf16[128,512]{1,0:T(8,128)(2,1)S(1)}, bf16[128,512]{1,0:T(8,128)(2,1)S(1)}, u32[]{:S(2)}, u32[]{:S(2)}) collective-permute-start(bf16[128,512]{1,0:T(8,128)(2,1)S(1)} %add_convert_fusion.6), channel_id=1, source_target_pairs={{0,1},{1,2},{2,3},{3,4},{4,5},{5,6},{6,7},{7,0},{8,9},{9,10},{10,1... | collective-permute-start | bytes 393224 | tf_op jit(solution)/shard_map/ppermute | solution.py:283
  55.2 16.1 %collective-permute-start.12 = (bf16[128,512]{1,0:T(8,128)(2,1)S(1)}, bf16[128,512]{1,0:T(8,128)(2,1)S(1)}, u32[]{:S(2)}, u32[]{:S(2)}) collective-permute-start(bf16[128,512]{1,0:T(8,128)(2,1)S(1)} %add_convert_fusion.3), channel_id=1, source_target_pairs={{0,7},{1,0},{2,1},{3,2},{4,3},{5,4},{6,5},{7,6},{8,15},{9,8},{10,9... | collective-permute-start | bytes 393224 | tf_op jit(solution)/shard_map/ppermute | solution.py:283
  58.6 6.2 %copy-start.3 = (bf16[128,512]{1,0:T(8,128)(2,1)S(1)}, bf16[128,512]{1,0:T(8,128)(2,1)}, u32[]{:S(2)}) copy-start(bf16[128,512]{1,0:T(8,128)(2,1)} %get-tuple-element.42) | copy-start | bytes 393220
  64.9 6.3 %copy-start.2 = (bf16[128,512]{1,0:T(8,128)(2,1)S(1)}, bf16[128,512]{1,0:T(8,128)(2,1)}, u32[]{:S(2)}) copy-start(bf16[128,512]{1,0:T(8,128)(2,1)} %get-tuple-element.55) | copy-start | bytes 393220
  64.9 6.3 %collective-permute-start.9 = (bf16[128,512]{1,0:T(8,128)(2,1)S(1)}, bf16[128,512]{1,0:T(8,128)(2,1)S(1)}, u32[]{:S(2)}, u32[]{:S(2)}) collective-permute-start(bf16[128,512]{1,0:T(8,128)(2,1)S(1)} %add_convert_fusion.5), channel_id=1, source_target_pairs={{0,1},{1,2},{2,3},{3,4},{4,5},{5,6},{6,7},{7,0},{8,9},{9,10},{10,1... | collective-permute-start | bytes 393224 | tf_op jit(solution)/shard_map/ppermute | solution.py:283
  71.1 2.6 %copy-start.1 = (bf16[128,512]{1,0:T(8,128)(2,1)S(1)}, bf16[128,512]{1,0:T(8,128)(2,1)}, u32[]{:S(2)}) copy-start(bf16[128,512]{1,0:T(8,128)(2,1)} %get-tuple-element.52) | copy-start | bytes 393220
  71.1 9.8 %copy-start.4 = (bf16[128,512]{1,0:T(8,128)(2,1)S(1)}, bf16[128,512]{1,0:T(8,128)(2,1)}, u32[]{:S(2)}) copy-start(bf16[128,512]{1,0:T(8,128)(2,1)} %get-tuple-element.56) | copy-start | bytes 393220
  71.3 6.1 %collective-permute-start.13 = (bf16[128,512]{1,0:T(8,128)(2,1)S(1)}, bf16[128,512]{1,0:T(8,128)(2,1)S(1)}, u32[]{:S(2)}, u32[]{:S(2)}) collective-permute-start(bf16[128,512]{1,0:T(8,128)(2,1)S(1)} %add_convert_fusion.2), channel_id=1, source_target_pairs={{0,7},{1,0},{2,1},{3,2},{4,3},{5,4},{6,5},{7,6},{8,15},{9,8},{10,9... | collective-permute-start | bytes 393224 | tf_op jit(solution)/shard_map/ppermute | solution.py:283
  73.8 7.1 %collective-permute-start.10 = (bf16[128,512]{1,0:T(8,128)(2,1)S(1)}, bf16[128,512]{1,0:T(8,128)(2,1)S(1)}, u32[]{:S(2)}, u32[]{:S(2)}) collective-permute-start(bf16[128,512]{1,0:T(8,128)(2,1)S(1)} %add_convert_fusion.4), channel_id=1, source_target_pairs={{0,1},{1,2},{2,3},{3,4},{4,5},{5,6},{6,7},{7,0},{8,9},{9,10},{10,1... | collective-permute-start | bytes 393224 | tf_op jit(solution)/shard_map/ppermute | solution.py:283
  80.9 28.1 %copy-start = (bf16[128,512]{1,0:T(8,128)(2,1)}, bf16[128,512]{1,0:T(8,128)(2,1)S(1)}, u32[]{:S(2)}) copy-start(bf16[128,512]{1,0:T(8,128)(2,1)S(1)} %add_convert_fusion.1.refs_0_) | copy-start | bytes 393220
  81.0 8.5 %collective-permute-start.19 = (bf16[128,512]{1,0:T(8,128)(2,1)S(1)}, bf16[128,512]{1,0:T(8,128)(2,1)S(1)}, u32[]{:S(2)}, u32[]{:S(2)}) collective-permute-start(bf16[128,512]{1,0:T(8,128)(2,1)S(1)} %add_convert_fusion.1.refs_0_), channel_id=1, source_target_pairs={{0,48},{16,0},{32,16},{48,32},{1,49},{17,1},{33,17},{49,33},{2,50}... | collective-permute-start | bytes 393224 | tf_op jit(solution)/shard_map/ppermute | solution.py:283
  85.5 6.6 %collective-permute-start.17 = (bf16[128,512]{1,0:T(8,128)(2,1)S(1)}, bf16[128,512]{1,0:T(8,128)(2,1)S(1)}, u32[]{:S(2)}, u32[]{:S(2)}) collective-permute-start(bf16[128,512]{1,0:T(8,128)(2,1)S(1)} %add_convert_fusion.1.refs_0_), channel_id=1, source_target_pairs={{0,32},{16,48},{32,0},{48,16},{1,33},{17,49},{33,1},{49,17},{2,34}... | collective-permute-start | bytes 393224 | tf_op jit(solution)/shard_map/ppermute | solution.py:283
  85.5 7.6 %collective-permute-start.15 = (bf16[128,512]{1,0:T(8,128)(2,1)S(1)}, bf16[128,512]{1,0:T(8,128)(2,1)S(1)}, u32[]{:S(2)}, u32[]{:S(2)}) collective-permute-start(bf16[128,512]{1,0:T(8,128)(2,1)S(1)} %add_convert_fusion.1.refs_0_), channel_id=1, source_target_pairs={{0,16},{16,32},{32,48},{48,0},{1,17},{17,33},{33,49},{49,1},{2,18}... | collective-permute-start | bytes 393224 | tf_op jit(solution)/shard_map/ppermute | solution.py:283
  86.5 6.7 %collective-permute-start.14 = (bf16[128,512]{1,0:T(8,128)(2,1)S(1)}, bf16[128,512]{1,0:T(8,128)(2,1)S(1)}, u32[]{:S(2)}, u32[]{:S(2)}) collective-permute-start(bf16[128,512]{1,0:T(8,128)(2,1)S(1)} %add_convert_fusion.1.refs_0_), channel_id=1, source_target_pairs={{0,8},{8,0},{1,9},{9,1},{2,10},{10,2},{3,11},{11,3},{4,12},{12,4},... | collective-permute-start | bytes 393224 | tf_op jit(solution)/shard_map/ppermute | solution.py:283
  89.4 3.7 %collective-permute-start.20 = (bf16[128,512]{1,0:T(8,128)(2,1)S(1)}, bf16[128,512]{1,0:T(8,128)(2,1)S(1)}, u32[]{:S(2)}, u32[]{:S(2)}) collective-permute-start(bf16[128,512]{1,0:T(8,128)(2,1)S(1)} %collective-permute-done.19.refs_6_), channel_id=1, source_target_pairs={{0,8},{8,0},{1,9},{9,1},{2,10},{10,2},{3,11},{11,3},{4,12},{12,4},... | collective-permute-start | bytes 393224 | tf_op jit(solution)/shard_map/ppermute | solution.py:283
  92.1 1.3 %collective-permute-start.18 = (bf16[128,512]{1,0:T(8,128)(2,1)S(1)}, bf16[128,512]{1,0:T(8,128)(2,1)S(1)}, u32[]{:S(2)}, u32[]{:S(2)}) collective-permute-start(bf16[128,512]{1,0:T(8,128)(2,1)S(1)} %collective-permute-done.17.refs_4_), channel_id=1, source_target_pairs={{0,8},{8,0},{1,9},{9,1},{2,10},{10,2},{3,11},{11,3},{4,12},{12,4},... | collective-permute-start | bytes 393224 | tf_op jit(solution)/shard_map/ppermute | solution.py:283
  93.1 1.3 %collective-permute-start.16 = (bf16[128,512]{1,0:T(8,128)(2,1)S(1)}, bf16[128,512]{1,0:T(8,128)(2,1)S(1)}, u32[]{:S(2)}, u32[]{:S(2)}) collective-permute-start(bf16[128,512]{1,0:T(8,128)(2,1)S(1)} %collective-permute-done.15.refs_2_), channel_id=1, source_target_pairs={{0,8},{8,0},{1,9},{9,1},{2,10},{10,2},{3,11},{11,3},{4,12},{12,4},... | collective-permute-start | bytes 393224 | tf_op jit(solution)/shard_map/ppermute | solution.py:283
  95.8 10.9 %collective-permute-start.21 = (bf16[160,512]{1,0:T(8,128)(2,1)S(1)}, bf16[160,512]{1,0:T(8,128)(2,1)S(1)}, u32[]{:S(2)}, u32[]{:S(2)}) collective-permute-start(bf16[160,512]{1,0:T(8,128)(2,1)S(1)} %get-tuple-element.59), channel_id=1, source_target_pairs={{0,64},{64,128},{128,192},{192,0},{1,65},{65,129},{129,193},{193,1... | collective-permute-start | bytes 491528 | tf_op jit(solution)/shard_map/ppermute | solution.py:283
  99.5 8.6 %collective-permute-start.22 = (bf16[160,512]{1,0:T(8,128)(2,1)S(1)}, bf16[160,512]{1,0:T(8,128)(2,1)S(1)}, u32[]{:S(2)}, u32[]{:S(2)}) collective-permute-start(bf16[160,512]{1,0:T(8,128)(2,1)S(1)} %get-tuple-element.60), channel_id=1, source_target_pairs={{0,128},{64,192},{128,0},{192,64},{1,129},{65,193},{129,1},{193,65... | collective-permute-start | bytes 491528 | tf_op jit(solution)/shard_map/ppermute | solution.py:283
  99.5 9.5 %collective-permute-start.23 = (bf16[160,512]{1,0:T(8,128)(2,1)S(1)}, bf16[160,512]{1,0:T(8,128)(2,1)S(1)}, u32[]{:S(2)}, u32[]{:S(2)}) collective-permute-start(bf16[160,512]{1,0:T(8,128)(2,1)S(1)} %get-tuple-element.61), channel_id=1, source_target_pairs={{0,192},{64,0},{128,64},{192,128},{1,193},{65,1},{129,65},{193,129... | collective-permute-start | bytes 491528 | tf_op jit(solution)/shard_map/ppermute | solution.py:283
Sparse Core Ops, SparseCore 0:
  9.8 42.4 all-gather.2
  71.3 42.8 reduce-scatter.1
